TPU v7x, 32 devices: a whole 2x2x4 slice. The times are simulated.
32 devices in a mesh: dp: 8 (over z, x), mp: 4 (over y, core).
Axes of the slice: x: 2, y: 2, z: 4, core: 2. Of those that a mesh axis runs over, the one named last changes fastest.
Arguments:
- teacher_in: bfloat16 [16384, 1024], P('dp'), may hold values from -6 to 6
- segment_ids: int32 [8, 2048], replicated, may hold values from 0 to 7, never falling along the last dimension, each value on 1 to 1568 neighbouring positions
- keep_mask: int32 [8, 2048], replicated, may hold values from 0 to 1, as said below
- block_owner: int32 [8, 12], replicated, may hold values from -1 to 7, as said below
- student_in: bfloat16 [96, 128, 768], P('dp'), may hold values from -6 to 6
- t_norm1_gain: bfloat16 [1024], replicated, may hold values from 0.25 to 1.75
- t_norm1_shift: bfloat16 [1024], replicated, may hold values from -1.75 to 1.75
- t_qkv: bfloat16 [3, 1024, 1024], P(None, None, 'mp'), may hold values from -0.1875 to 0.1875
- t_qv_bias: bfloat16 [2, 1024], P(None, 'mp'), may hold values from -0.3125 to 0.3125
- t_out: bfloat16 [1024, 1024], P('mp'), may hold values from -3 to 3
- t_out_bias: bfloat16 [1024], replicated, may hold values from -1.75 to 1.75
- t_norm2_gain: bfloat16 [1024], replicated, may hold values from 0.25 to 1.75
- t_norm2_shift: bfloat16 [1024], replicated, may hold values from -1.75 to 1.75
- t_fc1: bfloat16 [1024, 4096], P(None, 'mp'), may hold values from -0.1875 to 0.1875
- t_fc1_bias: bfloat16 [4096], P('mp'), may hold values from -1.75 to 1.75
- t_fc2: bfloat16 [4096, 1024], P('mp'), may hold values from -0.09375 to 0.09375
- t_fc2_bias: bfloat16 [1024], replicated, may hold values from -1.75 to 1.75
- s_norm1_gain: bfloat16 [768], replicated, may hold values from 0.25 to 1.75
- s_norm1_shift: bfloat16 [768], replicated, may hold values from -1.75 to 1.75
- s_qkv: bfloat16 [3, 768, 768], P(None, None, 'mp'), may hold values from -0.21875 to 0.21875
- s_qv_bias: bfloat16 [2, 768], P(None, 'mp'), may hold values from -0.3125 to 0.3125
- s_out: bfloat16 [768, 768], P('mp'), may hold values from -3.5 to 3.5
- s_out_bias: bfloat16 [768], replicated, may hold values from -1.75 to 1.75
- s_norm2_gain: bfloat16 [768], replicated, may hold values from 0.25 to 1.75
- s_norm2_shift: bfloat16 [768], replicated, may hold values from -1.75 to 1.75
- s_fc1: bfloat16 [768, 3072], P(None, 'mp'), may hold values from -0.21875 to 0.21875
- s_fc1_bias: bfloat16 [3072], P('mp'), may hold values from -1.75 to 1.75
- s_fc2: bfloat16 [3072, 768], P('mp'), may hold values from -0.109375 to 0.109375
- s_fc2_bias: bfloat16 [768], replicated, may hold values from -1.75 to 1.75
- head_weight: bfloat16 [768, 1024], replicated, may hold values from -0.21875 to 0.21875
- head_bias: bfloat16 [1024], replicated, may hold values from -1.75 to 1.75
Outputs:
- loss: float32 [], replicated
- student_out: bfloat16 [64, 128, 768], P('dp', 'mp')
- grad_student_in: float32 [96, 128, 768], P('dp', 'mp')
- grad_s_norm1_gain: float32 [768], replicated
- grad_s_norm1_shift: float32 [768], replicated
- grad_s_qkv: float32 [3, 768, 768], P(None, None, 'mp')
- grad_s_qv_bias: float32 [2, 768], P(None, 'mp')
- grad_s_out: float32 [768, 768], P('mp')
- grad_s_out_bias: float32 [768], replicated
- grad_s_norm2_gain: float32 [768], replicated
- grad_s_norm2_shift: float32 [768], replicated
- grad_s_fc1: float32 [768, 3072], P(None, 'mp')
- grad_s_fc1_bias: float32 [3072], P('mp')
- grad_s_fc2: float32 [3072, 768], P('mp')
- grad_s_fc2_bias: float32 [768], replicated
- grad_head: float32 [768, 1024], replicated
- grad_head_bias: float32 [1024], replicated
Inputs may be any that keep to these rules, and one draw needn't show every extreme that they name: `keep_mask`: the ones of each row fill at least 4 and at most 12 blocks of 128 (rounded up); some row fills exactly 12. `block_owner`: entry (i, b) names the index of dp that processes block b of home i's kept slots; it is -1 exactly for the blocks that hold no kept token of row i of keep_mask. Every index of dp is named exactly 8 times; no row names one index more than 2 times, and some row names some index exactly 2 times. `segment_ids`: row i numbers the clips of home i, never falling; each clip has 1 to 1568 tokens and one has exactly 1568.
All inputs are finite; a program needn't handle non-finite values.
Results may differ from a plain program's by a relative error of at most 0.015.
The roundings to bfloat16 on the way count: a program that leaves them out, or rounds other values in their place, can miss the bound.
Values may be sent and summed in bfloat16 or wider, within the bound.
No kernel may reach another device: no remote copies, remote signals or barrier semaphores. Data moves between devices by JAX's collectives and lax.ppermute only.
A program may use at most 128 MiB of HBM per device.

v0:
```python
import jax
import jax.numpy as jnp
from jax import lax
from jax.sharding import PartitionSpec as P

HD = 64
OWN = 8
CLIPS = 8


eps = 1e-05
minus_big = -1e30


def layer_norm(values, gain, shift):
    mean = jnp.mean(values, axis=-1, keepdims=True)
    centred = values - mean
    spread = jnp.mean(centred * centred, axis=-1, keepdims=True)
    return centred * lax.rsqrt(spread + eps) * gain + shift


def row_block():
    return 512


def kept_layout(mask_row, seg_row, slots, clips):
    total = mask_row.shape[0]
    places = jnp.arange(total, dtype=jnp.int32)
    rank = jnp.cumsum(mask_row) - 1
    target = jnp.where(mask_row == 1, rank, slots)
    source = jnp.zeros((slots,), jnp.int32).at[target].set(places, mode="drop")
    kept_total = jnp.sum(mask_row)
    live = jnp.arange(slots, dtype=jnp.int32) < kept_total
    seg_kept = jnp.where(live, seg_row[source], clips)
    labels = jnp.arange(clips, dtype=jnp.int32)
    member = (seg_row[None, :] == labels[:, None]).astype(jnp.int32)
    counts = jnp.sum(member * mask_row[None, :], axis=1)
    inverse = 1.0 / jnp.maximum(counts, 1).astype(jnp.float32)
    pick = (seg_kept[:, None] == labels[None, :]).astype(jnp.float32)
    weight = jnp.sum(pick * inverse[None, :], axis=1)
    return (source, live, seg_kept, weight)


def split_heads(proj, bias, count):
    width = proj.shape[2]
    query = (proj[0] + bias[0]).astype(jnp.bfloat16).reshape(count, width // HD, HD)
    key_rows = proj[1].astype(jnp.bfloat16).reshape(count, width // HD, HD)
    value = (proj[2] + bias[1]).astype(jnp.bfloat16).reshape(count, width // HD, HD)
    return (query, key_rows, value)


def attend(queries, keys, values, seg_rows, scale):
    count, heads, size = queries.shape
    step = row_block()

    def one_block(start):
        q_part = lax.dynamic_slice_in_dim(queries, start, step, 0)
        s_part = lax.dynamic_slice_in_dim(seg_rows, start, step, 0)
        scores = (
            jnp.einsum("qhd,khd->hqk", q_part, keys, preferred_element_type=jnp.float32) * scale
        )
        same = s_part[:, None] == seg_rows[None, :]
        scores = jnp.where(same[None], scores, minus_big)
        top = jnp.max(scores, axis=-1, keepdims=True)
        expd = jnp.exp(scores - top)
        total = jnp.sum(expd, axis=-1, keepdims=True)
        probs = (expd / total).astype(jnp.bfloat16)
        mixed = jnp.einsum("hqk,khd->qhd", probs, values, preferred_element_type=jnp.float32)
        return (mixed, (top + jnp.log(total))[..., 0])

    starts = jnp.arange(count // step, dtype=jnp.int32) * step
    mixed, lse = lax.map(one_block, starts)
    return (mixed.reshape(count, heads * size), lse)


def attend_back(queries, keys, values, seg_rows, lse, grad_mixed, scale):
    count, heads, size = queries.shape
    step = row_block()

    def one_block(carry, index):
        grad_keys, grad_values = carry
        start = index * step
        q_part = lax.dynamic_slice_in_dim(queries, start, step, 0)
        s_part = lax.dynamic_slice_in_dim(seg_rows, start, step, 0)
        g_part = lax.dynamic_slice_in_dim(grad_mixed, start, step, 0)
        scores = (
            jnp.einsum("qhd,khd->hqk", q_part, keys, preferred_element_type=jnp.float32) * scale
        )
        same = s_part[:, None] == seg_rows[None, :]
        scores = jnp.where(same[None], scores, minus_big)
        probs = jnp.exp(scores - lse[index][..., None])
        low_probs = probs.astype(jnp.bfloat16)
        grad_probs = jnp.einsum("qhd,khd->hqk", g_part, values, preferred_element_type=jnp.float32)
        delta = jnp.sum(probs * grad_probs, axis=-1, keepdims=True)
        grad_scores = (probs * (grad_probs - delta)).astype(jnp.bfloat16)
        grad_q = (
            jnp.einsum("hqk,khd->qhd", grad_scores, keys, preferred_element_type=jnp.float32)
            * scale
        )
        grad_keys = (
            grad_keys
            + jnp.einsum("hqk,qhd->khd", grad_scores, q_part, preferred_element_type=jnp.float32)
            * scale
        )
        grad_values = grad_values + jnp.einsum(
            "hqk,qhd->khd", low_probs, g_part, preferred_element_type=jnp.float32
        )
        return ((grad_keys, grad_values), grad_q)

    zeros = jnp.zeros((count, heads, size), jnp.float32)
    (grad_keys, grad_values), grad_q = lax.scan(
        one_block, (zeros, zeros), jnp.arange(count // step, dtype=jnp.int32)
    )
    return (
        grad_q.reshape(count, heads * size).astype(jnp.bfloat16),
        grad_keys.reshape(count, heads * size).astype(jnp.bfloat16),
        grad_values.reshape(count, heads * size).astype(jnp.bfloat16),
    )


def body(
    teacher_in,
    segment_ids,
    keep_mask,
    block_owner,
    student_in,
    t_norm1_gain,
    t_norm1_shift,
    t_qkv,
    t_qv_bias,
    t_out,
    t_out_bias,
    t_norm2_gain,
    t_norm2_shift,
    t_fc1,
    t_fc1_bias,
    t_fc2,
    t_fc2_bias,
    s_norm1_gain,
    s_norm1_shift,
    s_qkv,
    s_qv_bias,
    s_out,
    s_out_bias,
    s_norm2_gain,
    s_norm2_shift,
    s_fc1,
    s_fc1_bias,
    s_fc2,
    s_fc2_bias,
    head_weight,
    head_bias,
):
    parts_mp = lax.axis_size("mp")
    my_mp = lax.axis_index("mp")
    homes = lax.axis_size("dp")
    my_home = lax.axis_index("dp")
    slots, block, width = student_in.shape
    piece = block // parts_mp
    rows = slots * block
    capacity = (slots + homes - 1) // homes
    scale = HD ** (-0.5)
    first = (my_mp == 0).astype(jnp.float32)
    sources, lives, segs, weights = jax.vmap(lambda m, s: kept_layout(m, s, rows, CLIPS))(
        keep_mask, segment_ids
    )
    source = sources[my_home]
    live = lives[my_home]
    seg_kept = segs[my_home]
    seg_row = segment_ids[my_home]
    t_rows, t_width = teacher_in.shape
    x_teach = teacher_in.astype(jnp.float32)
    a_teach = layer_norm(x_teach, t_norm1_gain, t_norm1_shift).astype(jnp.bfloat16)
    proj_teach = jnp.einsum("td,pdc->ptc", a_teach, t_qkv, preferred_element_type=jnp.float32)
    t_query, t_key, t_value = split_heads(proj_teach, t_qv_bias, t_rows)
    mixed_teach, _ = attend(t_query, t_key, t_value, seg_row, scale)
    ctx_teach = mixed_teach.astype(jnp.bfloat16)
    part_teach = jnp.dot(ctx_teach, t_out, preferred_element_type=jnp.float32)
    summed = lax.psum(part_teach.astype(jnp.bfloat16), "mp").astype(jnp.float32)
    resid_teach = x_teach + summed + t_out_bias
    a2_teach = layer_norm(resid_teach, t_norm2_gain, t_norm2_shift).astype(jnp.bfloat16)
    carry_teach = resid_teach * first
    hidden_teach = jnp.dot(a2_teach, t_fc1, preferred_element_type=jnp.float32) + t_fc1_bias
    act_teach = jax.nn.gelu(hidden_teach, approximate=False).astype(jnp.bfloat16)
    term_teach = (
        jnp.dot(act_teach, t_fc2, preferred_element_type=jnp.float32)
        + carry_teach
        + first * t_fc2_bias
    )
    kept_term = jnp.where(live[:, None], term_teach[source], 0.0).reshape(slots, block, t_width)
    x_stud = student_in.reshape(rows, width)
    x_stud32 = x_stud.astype(jnp.float32)
    a_stud = layer_norm(x_stud32, s_norm1_gain, s_norm1_shift).astype(jnp.bfloat16)
    proj_stud = jnp.einsum("td,pdc->ptc", a_stud, s_qkv, preferred_element_type=jnp.float32)
    s_query, s_key, s_value = split_heads(proj_stud, s_qv_bias, rows)
    mixed_stud, lse_stud = attend(s_query, s_key, s_value, seg_kept, scale)
    ctx_stud = mixed_stud.astype(jnp.bfloat16)
    term_stud = jnp.dot(ctx_stud, s_out, preferred_element_type=jnp.float32) + first * (
        x_stud32 + s_out_bias
    )
    target_f, resid_stud = (
        lax.psum_scatter(
            kept_term.astype(jnp.bfloat16), "mp", scatter_dimension=1, tiled=True
        ).astype(jnp.float32),
        lax.psum_scatter(
            term_stud.reshape(slots, block, width).astype(jnp.bfloat16),
            "mp",
            scatter_dimension=1,
            tiled=True,
        ).astype(jnp.float32),
    )
    target = target_f.astype(jnp.bfloat16)
    sent = resid_stud.astype(jnp.bfloat16)
    owners = block_owner[my_home]
    labels = jnp.arange(homes, dtype=jnp.int32)
    hits = (owners[:, None] == labels[None, :]).astype(jnp.int32)
    order_in = jnp.sum((jnp.cumsum(hits, axis=0) - hits) * hits, axis=1)
    place = jnp.where(owners >= 0, owners * capacity + order_in, homes * capacity)
    safe = jnp.minimum(place, homes * capacity - 1)
    outbound_h = (
        jnp.zeros((homes * capacity, piece, width), jnp.bfloat16).at[place].set(sent, mode="drop")
    )
    outbound_t = (
        jnp.zeros((homes * capacity, piece, t_width), jnp.bfloat16)
        .at[place]
        .set(target, mode="drop")
    )
    inbound_h, inbound_t = (
        lax.all_to_all(outbound_h, "dp", split_axis=0, concat_axis=0, tiled=True),
        lax.all_to_all(outbound_t, "dp", split_axis=0, concat_axis=0, tiled=True),
    )
    flat_owner = block_owner.reshape(-1)
    mine = (flat_owner == my_home).astype(jnp.int32)
    per_source = jnp.sum(mine.reshape(homes, slots), axis=1)
    slot_live = (jnp.arange(capacity, dtype=jnp.int32)[None, :] < per_source[:, None]).reshape(-1)
    slot_rank = jnp.cumsum(slot_live.astype(jnp.int32)) - 1
    chosen = (
        jnp.zeros((OWN,), jnp.int32)
        .at[jnp.where(slot_live, slot_rank, OWN)]
        .set(jnp.arange(homes * capacity, dtype=jnp.int32), mode="drop")
    )
    own_h = inbound_h[chosen]
    full_h = lax.all_gather(own_h, "mp", axis=1, tiled=True)
    a2_own = layer_norm(full_h.astype(jnp.float32), s_norm2_gain, s_norm2_shift).astype(
        jnp.bfloat16
    )
    pre_own = (
        jnp.einsum("obd,df->obf", a2_own, s_fc1, preferred_element_type=jnp.float32) + s_fc1_bias
    )
    act_own = jax.nn.gelu(pre_own, approximate=False).astype(jnp.bfloat16)
    term_own = jnp.einsum(
        "obf,fd->obd", act_own, s_fc2, preferred_element_type=jnp.float32
    ) + first * (full_h.astype(jnp.float32) + s_fc2_bias)
    out_piece = lax.psum_scatter(
        term_own.astype(jnp.bfloat16), "mp", scatter_dimension=1, tiled=True
    )
    own_t = inbound_t[chosen]
    global_rank = jnp.cumsum(mine) - 1
    anchor = (
        jnp.zeros((OWN,), jnp.int32)
        .at[jnp.where(mine == 1, global_rank, OWN)]
        .set(jnp.arange(homes * slots, dtype=jnp.int32), mode="drop")
    )
    row_weight = weights.reshape(homes * slots, block)[anchor]
    my_weight = lax.dynamic_slice_in_dim(row_weight, my_mp * piece, piece, 1)
    guess = (
        jnp.einsum("obd,de->obe", out_piece, head_weight, preferred_element_type=jnp.float32)
        + head_bias
    )
    miss = guess - own_t.astype(jnp.float32)
    loss_part = 0.5 * jnp.sum(my_weight[..., None] * miss * miss)
    grad_guess = (my_weight[..., None] * miss).astype(jnp.bfloat16)
    grad_head = jnp.einsum("obd,obe->de", out_piece, grad_guess, preferred_element_type=jnp.float32)
    grad_head_bias = jnp.sum(grad_guess.astype(jnp.float32), axis=(0, 1))
    grad_out = jnp.einsum(
        "obe,de->obd", grad_guess, head_weight, preferred_element_type=jnp.float32
    ).astype(jnp.bfloat16)
    full_grad_out = lax.all_gather(grad_out, "mp", axis=1, tiled=True)
    grad_act = jnp.einsum("obd,fd->obf", full_grad_out, s_fc2, preferred_element_type=jnp.float32)
    _, gelu_back = jax.vjp(lambda v: jax.nn.gelu(v, approximate=False), pre_own)
    grad_pre = gelu_back(grad_act)[0].astype(jnp.bfloat16)
    grad_fc2 = jnp.einsum("obf,obd->fd", act_own, full_grad_out, preferred_element_type=jnp.float32)
    grad_fc2_bias = jnp.sum(grad_out.astype(jnp.float32), axis=(0, 1))
    grad_fc1 = jnp.einsum("obd,obf->df", a2_own, grad_pre, preferred_element_type=jnp.float32)
    grad_fc1_bias = jnp.sum(grad_pre.astype(jnp.float32), axis=(0, 1))
    grad_a2 = jnp.einsum("obf,df->obd", grad_pre, s_fc1, preferred_element_type=jnp.float32)
    grad_a2_piece = lax.psum_scatter(
        grad_a2.astype(jnp.bfloat16), "mp", scatter_dimension=1, tiled=True
    ).astype(jnp.float32)
    _, norm2_back = jax.vjp(
        layer_norm,
        own_h.astype(jnp.float32),
        s_norm2_gain.astype(jnp.float32),
        s_norm2_shift.astype(jnp.float32),
    )
    grad_h_norm, grad_norm2_gain, grad_norm2_shift = norm2_back(grad_a2_piece)
    grad_sent = (grad_out.astype(jnp.float32) + grad_h_norm).astype(jnp.bfloat16)
    returning = jnp.zeros((homes * capacity, piece, width), jnp.bfloat16).at[chosen].set(grad_sent)
    inbound_back = lax.all_to_all(returning, "dp", split_axis=0, concat_axis=0, tiled=True)
    grad_home = jnp.where(
        (owners >= 0)[:, None, None], inbound_back[safe], jnp.zeros((), jnp.bfloat16)
    )
    full_grad_home = lax.all_gather(grad_home, "mp", axis=1, tiled=True).reshape(rows, width)
    grad_out_w = jnp.einsum(
        "tc,td->cd", ctx_stud, full_grad_home, preferred_element_type=jnp.float32
    )
    grad_out_bias = jnp.sum(grad_home.astype(jnp.float32), axis=(0, 1))
    heads_here = s_qkv.shape[2] // HD
    grad_ctx = jnp.einsum(
        "td,cd->tc", full_grad_home, s_out, preferred_element_type=jnp.float32
    ).astype(jnp.bfloat16)
    grad_q, grad_k, grad_v = attend_back(
        s_query, s_key, s_value, seg_kept, lse_stud, grad_ctx.reshape(rows, heads_here, HD), scale
    )
    grad_proj = jnp.stack([grad_q, grad_k, grad_v])
    grad_qkv = jnp.einsum("td,ptc->pdc", a_stud, grad_proj, preferred_element_type=jnp.float32)
    grad_qv_bias = jnp.stack(
        [jnp.sum(grad_q.astype(jnp.float32), axis=0), jnp.sum(grad_v.astype(jnp.float32), axis=0)]
    )
    grad_a1 = jnp.einsum("ptc,pdc->td", grad_proj, s_qkv, preferred_element_type=jnp.float32)
    grad_a1_piece = lax.psum_scatter(
        grad_a1.reshape(slots, block, width).astype(jnp.bfloat16),
        "mp",
        scatter_dimension=1,
        tiled=True,
    ).astype(jnp.float32)
    x_piece = lax.dynamic_slice_in_dim(student_in, my_mp * piece, piece, 1).astype(jnp.float32)
    _, norm1_back = jax.vjp(
        layer_norm, x_piece, s_norm1_gain.astype(jnp.float32), s_norm1_shift.astype(jnp.float32)
    )
    grad_x_norm, grad_norm1_gain, grad_norm1_shift = norm1_back(grad_a1_piece)
    grad_in = grad_home.astype(jnp.float32) + grad_x_norm
    sum_qkv, sum_qv_bias, sum_out_w, sum_fc1, sum_fc1_bias, sum_fc2 = lax.psum(
        (grad_qkv, grad_qv_bias, grad_out_w, grad_fc1, grad_fc1_bias, grad_fc2), "dp"
    )
    (
        sum_norm1_gain,
        sum_norm1_shift,
        sum_out_bias,
        sum_norm2_gain,
        sum_norm2_shift,
        sum_fc2_bias,
        sum_head,
        sum_head_bias,
        loss,
    ) = lax.psum(
        (
            grad_norm1_gain,
            grad_norm1_shift,
            grad_out_bias,
            grad_norm2_gain,
            grad_norm2_shift,
            grad_fc2_bias,
            grad_head,
            grad_head_bias,
            loss_part,
        ),
        ("dp", "mp"),
    )
    return (
        loss,
        out_piece,
        grad_in,
        sum_norm1_gain,
        sum_norm1_shift,
        sum_qkv,
        sum_qv_bias,
        sum_out_w,
        sum_out_bias,
        sum_norm2_gain,
        sum_norm2_shift,
        sum_fc1,
        sum_fc1_bias,
        sum_fc2,
        sum_fc2_bias,
        sum_head,
        sum_head_bias,
    )


def solution(mesh):
    in_specs = (
        P("dp", None),
        P(),
        P(),
        P(),
        P("dp", None, None),
        P(),
        P(),
        P(None, None, "mp"),
        P(None, "mp"),
        P("mp", None),
        P(),
        P(),
        P(),
        P(None, "mp"),
        P("mp"),
        P("mp", None),
        P(),
        P(),
        P(),
        P(None, None, "mp"),
        P(None, "mp"),
        P("mp", None),
        P(),
        P(),
        P(),
        P(None, "mp"),
        P("mp"),
        P("mp", None),
        P(),
        P(),
        P(),
    )
    out_specs = (
        P(),
        P("dp", "mp", None),
        P("dp", "mp", None),
        P(),
        P(),
        P(None, None, "mp"),
        P(None, "mp"),
        P("mp", None),
        P(),
        P(),
        P(),
        P(None, "mp"),
        P("mp"),
        P("mp", None),
        P(),
        P(),
        P(),
    )
    return jax.shard_map(body, mesh=mesh, in_specs=in_specs, out_specs=out_specs, check_vma=False)
```

profile of v0, /device:TPU:0, one launch (start us, length us, event | category | flops | bytes accessed | tf_op | source)
XLA Modules:
  0.0 1209.8 jit_solution(15706625997255900835)
XLA Ops:
  19.9 60.5 %scatter_custom_fusion.5 = s32[12288]{0:T(1024)S(1)} fusion(s32[16384]{0:T(1024)S(1)} %bitcast.284, s32[16384]{0:T(1024)S(1)} %bitcast.285, s32[]{:T(128)} %constant.102.clone.1), kind=kCustom, calls=%fused_computation.262 | custom fusion | bytes 49156
  81.1 75.4 %gather_fusion.5 = s32[12288]{0:T(1024)S(1)} fusion(s32[8,2048]{1,0:T(8,128)S(1)} %copy-done.2, s32[12288]{0:T(1024)S(1)} %reshape.693), kind=kCustom, calls=%fused_computation.5 | custom fusion | bytes 196608 | tf_op jit(solution)/shard_map/vmap()/gather | solution.py:34
  159.5 41.1 %while.37 = (s32[]{:T(128)}, bf16[3,512,3,64]{1,3,2,0:T(8,128)(2,1)S(1)}, f32[3,3,512]{2,1,0:T(4,128)}, s32[3]{0:T(128)S(1)}, s32[1536]{0:T(1024)S(1)}, /*index=...) while((s32[]{:T(128)}, ...), condition=%wide.region_15.16_spmd, body=%wide.region_12.15_spmd.sunk | while | flops 633076224 | bytes 33306816 | solution.py:72
  168.6 4.0 fusion.291
  182.3 4.0 fusion.291
  195.9 4.0 fusion.291
  201.3 4.3 fusion.80
  211.0 4.3 fusion.96
  222.9 93.9 %while.38 = (s32[]{:T(128)}, bf16[4,512,4,64]{1,3,2,0:T(8,128)(2,1)}, s32[4]{0:T(128)S(1)}, s32[2048]{0:T(1024)S(1)}, s32[1,2048]{1,0:T(1,128)S(1)}, /*index=5*/...) while((s32[]{:T(128)}, ...), condition=%wide.region_29.30_spmd, body=%wide.region_26.29_spmd.sunk | while | flops 1099958272 | bytes 38566064 | solution.py:72
  226.2 10.7 fusion.295
  236.9 9.5 fusion.296
  249.7 10.7 fusion.295
  260.5 9.4 fusion.296
  273.1 10.7 fusion.295
  283.9 9.4 fusion.296
  296.6 10.7 fusion.295
  307.3 9.4 fusion.296
  331.4 7.2 all-to-all-start
  338.7 72.2 %all-reduce.7.cloned.1.call-done = bf16[2048,1024]{1,0:T(8,128)(2,1)} async-done(((bf16[2048,1024]{1,0:T(8,128)(2,1)}), bf16[2048,1024]{1,0:T(8,128)(2,1)}) %all-reduce.7.cloned.1.call-update) | async-done | bytes 4194320 | tf_op jit(solution)/shard_map/psum | solution.py:179
  410.9 5.0 fusion.71
  420.4 31.5 %add_add_fusion = bf16[2048,1024]{1,0:T(8,128)(2,1)} fusion(bf16[2048,1024]{1,0:T(8,128)(2,1)} %all-reduce.7.cloned.1.call-done, bf16[2048,1024]{1,0:T(8,128)(2,1)} %param.37, f32[1024]{0:T(1024)S(1)} %convert_multiply_fusion.4, f32[]{:T(128)S(6)} %convert_element_type.325, f32[1024]{0:T(1024)S(1)} %convert_element_type.351, ...), kind=kOutput, calls=%fused_computation.85 | convolution fusion | flops 8763998208 | bytes 16814084 | tf_op jit(solution)/shard_map/dot_general | solution.py:186
  451.9 10.5 gather_fusion.2
  472.9 8.5 multiply_convert_fusion.1
  485.3 18.8 %reduce-scatter.10.cloned.1.call-done = bf16[12,32,1024]{2,1,0:T(8,128)(2,1)} async-done(((bf16[12,128,1024]{2,1,0:T(8,128)(2,1)}), bf16[12,32,1024]{2,1,0:T(8,128)(2,1)}) %reduce-scatter.10.cloned.1.call-update) | async-done | bytes 786448 | tf_op jit(solution)/shard_map/reduce_scatter | solution.py:202
  508.3 5.5 all-to-all-start.1
  516.3 23.3 %all-to-all-done.1 = bf16[16,32,1024]{2,1,0:T(8,128)(2,1)S(1)} async-done(((bf16[16,32,1024]{2,1,0:T(8,128)(2,1)}), bf16[16,32,1024]{2,1,0:T(8,128)(2,1)S(1)}, u32[]{:S(2)}, u32[]{:S(2)}) %all-to-all-start.1) | async-done | bytes 1048608 | tf_op jit(solution)/shard_map/all_to_all | solution.py:230
  546.3 17.9 %all-gather.5.cloned.1.call-done = bf16[8,128,768]{2,1,0:T(8,128)(2,1)} async-done(((bf16[8,32,768]{2,1,0:T(8,128)(2,1)}), bf16[8,128,768]{2,1,0:T(8,128)(2,1)}) %all-gather.5.cloned.1.call-update) | async-done | bytes 1572880 | tf_op jit(solution)/shard_map/all_gather | solution.py:278
  564.1 5.6 convert_reduce_fusion.3
  573.6 28.2 %reduce-scatter.12.cloned.1.call-done = bf16[8,32,768]{2,1,0:T(8,128)(2,1)} async-done(((bf16[8,128,768]{2,1,0:T(8,128)(2,1)}), bf16[8,32,768]{2,1,0:T(8,128)(2,1)}) %reduce-scatter.12.cloned.1.call-update) | async-done | bytes 393232 | tf_op jit(solution)/shard_map/reduce_scatter | solution.py:287
  609.4 5.5 all-to-all-start.2
  615.0 20.1 %all-to-all-done.2 = bf16[16,32,768]{2,1,0:T(8,128)(2,1)S(1)} async-done(((bf16[16,32,768]{2,1,0:T(8,128)(2,1)}), bf16[16,32,768]{2,1,0:T(8,128)(2,1)S(1)}, u32[]{:S(2)}, u32[]{:S(2)}) %all-to-all-start.2) | async-done | bytes 786464 | tf_op jit(solution)/shard_map/all_to_all | solution.py:299
  636.9 22.2 %all-gather.7.cloned.1.call-done = bf16[12,128,768]{2,1,0:T(8,128)(2,1)} async-done(((bf16[12,32,768]{2,1,0:T(8,128)(2,1)}), bf16[12,128,768]{2,1,0:T(8,128)(2,1)}) %all-gather.7.cloned.1.call-update) | async-done | bytes 2359312 | tf_op jit(solution)/shard_map/all_gather | solution.py:303
  663.5 103.4 %while.39 = (s32[]{:T(128)}, f32[1536,3,64]{0,2,1:T(8,128)}, f32[1536,3,64]{0,2,1:T(8,128)S(1)}, bf16[3,512,3,64]{1,3,2,0:T(8,128)(2,1)}, s32[3]{0:T(128)S(1)}, ...) while((s32[]{:T(128)}, f32[1536,3,64]{0,2,1:T(8,128)}, ...), condition=%wide.region_45.46_spmd.clone, body=%wide.region_43.45_spmd.clone.sunk | while | flops 1533540864 | bytes 150854096 | solution.py:111
  671.4 7.2 multiply_reduce_fusion.4
  678.6 9.4 multiply_convert_fusion.5
  688.0 5.0 fusion.308
  705.8 7.2 multiply_reduce_fusion.4
  713.1 9.4 multiply_convert_fusion.5
  722.5 5.0 fusion.308
  740.3 7.2 multiply_reduce_fusion.4
  747.5 9.4 multiply_convert_fusion.5
  756.9 5.0 fusion.308
  771.1 4.9 bitcast_convert_fusion
  778.7 5.0 convolution_bitcast_fusion.1
  794.2 22.2 %all-reduce.1 = (f32[2,192]{1,0:T(2,128)}, f32[768]{0:T(1024)}) all-reduce(f32[2,192]{1,0:T(2,128)S(1)} %pad_maximum_fusion.3, f32[768]{0:T(1024)S(1)} %get-tuple-element.342), channel_id=1, replica_groups=mesh['dp'=8,'mp'=4] {'dp'}, use_global_device_ids=true, to_apply=%region_58.59 | all-reduce | flops 1152 | bytes 9216 | tf_op jit(solution)/shard_map/psum | solution.py:333
  820.4 38.2 %all-reduce = (f32[]{:T(128)}, f32[768]{0:T(1024)}, f32[768]{0:T(1024)}, f32[768]{0:T(1024)}, f32[768]{0:T(1024)}, /*index=5*/f32[768]{0:T(1024)}, f32[768]{0:T(1024)}, f32[1024]{0:T(1024)}) all-reduce(f32[]{:T(128)S(6)} %mul.391, f32[768]{0:T(1024)S(1)} %get-tuple-element.218, ...), channel_id=1, replica_groups=mesh['dp'=8,'mp'=4] {'dp','mp'}, use_global_device_ids=true, to_apply=%region_36.37 | all-reduce | flops 5633 | bytes 45064 | tf_op jit(solution)/shard_map/psum | solution.py:346
  861.3 91.8 %all-reduce.9.cloned.1.call-done = f32[768,1024]{1,0:T(8,128)} async-done(((f32[768,1024]{1,0:T(8,128)}), f32[768,1024]{1,0:T(8,128)}) %all-reduce.9.cloned.1.call-update) | async-done | bytes 3145744 | tf_op jit(solution)/shard_map/psum | solution.py:346
  953.1 240.3 %all-reduce.11.cloned.1.call-done = (f32[3,768,192]{1,2,0:T(8,128)}, f32[192,768]{1,0:T(8,128)}, f32[768,768]{1,0:T(8,128)}, f32[768,768]{1,0:T(8,128)}) async-done(((f32[3,768,192]{1,2,0:T(8,128)}, f32[192,768]{1,0:T(8,128)}, f32[768,768]{1,0:T(8,128)}, f32[768,768]{1,0:T(8,128)}), (f32[3,768,192]{1,2,0:T(8,128)}, f32[192,768]{1,0:T(8,128)}, f32[768,768]{1,0:T(8,128)}, ...) | async-done | bytes 7077904 | tf_op jit(solution)/shard_map/psum | solution.py:333
  (462 shorter events, 185.0 us)
Async XLA Ops:
  7.2 413.2 %copy-start = (bf16[1024,1024]{1,0:T(8,128)(2,1)S(1)}, bf16[1024,1024]{1,0:T(8,128)(2,1)}, u32[]{:S(2)}) copy-start(bf16[1024,1024]{1,0:T(8,128)(2,1)} %param.52) | copy-start | bytes 6291460
  7.2 320.2 %reduce-scatter.6.cloned.1.call-start = ((), (), s32[]{:S(2)}) async-start(), calls=%async_computation.8 | async-start | bytes 2949120 | tf_op jit(solution)/shard_map/reduce_scatter | solution.py:205
  14.9 66.3 %copy-start.2 = (s32[8,2048]{1,0:T(8,128)S(1)}, s32[8,2048]{1,0:T(8,128)}, u32[]{:S(2)}) copy-start(s32[8,2048]{1,0:T(8,128)} %param.38) | copy-start | bytes 196612
  19.6 136.9 %copy-start.54 = (s32[8]{0:T(128)}, s32[8]{0:T(128)S(1)}, u32[]{:S(2)}) copy-start(s32[8]{0:T(128)S(1)} %get-tuple-element.333) | copy-start | bytes 100
  205.6 205.3 %all-reduce.7.cloned.1.call-start = ((), (), s32[]{:S(2)}) async-start(), calls=%async_computation.10 | async-start | bytes 8388608 | tf_op jit(solution)/shard_map/psum | solution.py:179
  326.7 89.2 %copy-start.63 = (s32[8]{0:T(128)}, s32[8]{0:T(128)S(1)}, u32[]{:S(2)}) copy-start(s32[8]{0:T(128)S(1)} %compare_select_fusion.6) | copy-start | bytes 100
  326.8 92.2 %copy-start.53 = (s32[1024]{0:T(1024)}, s32[1024]{0:T(1024)S(1)}, u32[]{:S(2)}) copy-start(s32[1024]{0:T(1024)S(1)} %pad_clamp_fusion.2) | copy-start | bytes 12292
  327.3 88.6 %copy-start.80 = (s32[12]{0:T(128)}, s32[12]{0:T(128)S(1)}, u32[]{:S(2)}) copy-start(s32[12]{0:T(128)S(1)} %fusion.176) | copy-start | bytes 148
  331.4 87.5 %all-to-all-start = ((bf16[16,32,768]{2,1,0:T(8,128)(2,1)}), bf16[16,32,768]{2,1,0:T(8,128)(2,1)S(1)}, u32[]{:S(2)}, u32[]{:S(2)}) async-start(bf16[16,32,768]{2,1,0:T(8,128)(2,1)} %scatter_fusion), calls=%async_computation.1 | async-start | bytes 1572864 | tf_op jit(solution)/shard_map/all_to_all | solution.py:229
  338.7 127.9 %all-gather.9.cloned.1.call-start = ((), (), s32[]{:S(2)}) async-start(), calls=%async_computation.17 | async-start | bytes 1966080 | tf_op jit(solution)/shard_map/all_gather | solution.py:243
  410.9 5.9 copy-start.13
  420.3 83.8 %reduce-scatter.10.cloned.1.call-start = ((), (), s32[]{:S(2)}) async-start(), calls=%async_computation.11 | async-start | bytes 3932160 | tf_op jit(solution)/shard_map/reduce_scatter | solution.py:202
  465.9 74.5 %reduce-scatter.8.cloned.1.call-start = ((), (), s32[]{:S(2)}) async-start(), calls=%async_computation.9 | async-start | bytes 1966080 | tf_op jit(solution)/shard_map/reduce_scatter | solution.py:254
  466.5 6.3 copy-start.57
  472.9 8.6 copy-start.21
  472.9 9.7 copy-start.86
  482.6 22.6 %copy-start.81 = (s32[12]{0:T(128)S(1)}, s32[12]{0:T(128)}, u32[]{:S(2)}) copy-start(s32[12]{0:T(128)} %copy-done.80) | copy-start | bytes 148
  485.2 28.7 %copy-start.77 = (bf16[1024]{0:T(1024)(128)(2,1)S(1)}, bf16[1024]{0:T(1024)(128)(2,1)}, u32[]{:S(2)}) copy-start(bf16[1024]{0:T(1024)(128)(2,1)} %param.67) | copy-start | bytes 6148
  485.2 28.7 %copy-start.51 = (s32[8,12]{1,0:T(8,128)S(1)}, s32[8,12]{1,0:T(8,128)}, u32[]{:S(2)}) copy-start(s32[8,12]{1,0:T(8,128)} %get-tuple-element.317) | copy-start | bytes 1156
  485.2 28.9 %copy-start.3 = (s32[8,2048]{1,0:T(8,128)S(1)}, s32[8,2048]{1,0:T(8,128)}, u32[]{:S(2)}) copy-start(s32[8,2048]{1,0:T(8,128)} %param.38) | copy-start | bytes 196612
  485.2 28.9 %copy-start.34 = (s32[8,2048]{1,0:T(8,128)S(1)}, s32[8,2048]{1,0:T(8,128)}, u32[]{:S(2)}) copy-start(s32[8,2048]{1,0:T(8,128)} %param.39) | copy-start | bytes 196612
  485.2 29.2 %copy-start.44 = (s32[8,1536]{1,0:T(8,128)S(1)}, s32[8,1536]{1,0:T(8,128)}, u32[]{:S(2)}) copy-start(s32[8,1536]{1,0:T(8,128)} %copy-done.43) | copy-start | bytes 147460
  508.3 31.3 %all-to-all-start.1 = ((bf16[16,32,1024]{2,1,0:T(8,128)(2,1)}), bf16[16,32,1024]{2,1,0:T(8,128)(2,1)S(1)}, u32[]{:S(2)}, u32[]{:S(2)}) async-start(bf16[16,32,1024]{2,1,0:T(8,128)(2,1)} %scatter_fusion.1), calls=%async_computation.4 | async-start | bytes 2097152 | tf_op jit(solution)/shard_map/all_to_all | solution.py:230
  513.9 50.3 %all-gather.5.cloned.1.call-start = ((), (), s32[]{:S(2)}) async-start(), calls=%async_computation.12 | async-start | bytes 1966080 | tf_op jit(solution)/shard_map/all_gather | solution.py:278
  543.2 20.9 %copy-start.92 = (bf16[8,32,1024]{2,1,0:T(8,128)(2,1)}, bf16[8,32,1024]{2,1,0:T(8,128)(2,1)S(1)}, u32[]{:S(2)}) copy-start(bf16[8,32,1024]{2,1,0:T(8,128)(2,1)S(1)} %get-tuple-element.307) | copy-start | bytes 1572868
  546.2 55.6 %reduce-scatter.12.cloned.1.call-start = ((), (), s32[]{:S(2)}) async-start(), calls=%async_computation.13 | async-start | bytes 1966080 | tf_op jit(solution)/shard_map/reduce_scatter | solution.py:287
  564.1 6.7 copy-start.88
  573.4 31.3 %copy-start.28 = (bf16[8,32,768]{2,1,0:T(8,128)(2,1)S(1)}, bf16[8,32,768]{2,1,0:T(8,128)(2,1)}, u32[]{:S(2)}) copy-start(bf16[8,32,768]{2,1,0:T(8,128)(2,1)} %fusion.136) | copy-start | bytes 1179652
  573.4 33.7 %copy-start.64 = (s32[8]{0:T(128)S(1)}, s32[8]{0:T(128)}, u32[]{:S(2)}) copy-start(s32[8]{0:T(128)} %copy-done.63) | copy-start | bytes 100
  603.2 11.8 copy-start.78
  604.8 31.0 %copy-start.65 = (pred[12]{0:T(512)(128)(4,1)S(1)}, pred[12]{0:T(512)(128)(4,1)}, u32[]{:S(2)}) copy-start(pred[12]{0:T(512)(128)(4,1)} %get-tuple-element.310) | copy-start | bytes 40
  606.2 53.0 %copy-start.91 = (bf16[192,768]{1,0:T(8,128)(2,1)S(1)}, bf16[192,768]{1,0:T(8,128)(2,1)}, u32[]{:S(2)}) copy-start(bf16[192,768]{1,0:T(8,128)(2,1)} %param.58) | copy-start | bytes 884740
  609.4 25.7 %all-to-all-start.2 = ((bf16[16,32,768]{2,1,0:T(8,128)(2,1)}), bf16[16,32,768]{2,1,0:T(8,128)(2,1)S(1)}, u32[]{:S(2)}, u32[]{:S(2)}) async-start(bf16[16,32,768]{2,1,0:T(8,128)(2,1)} %scatter_fusion.2), calls=%async_computation.6 | async-start | bytes 1572864 | tf_op jit(solution)/shard_map/all_to_all | solution.py:299
  615.0 44.2 %all-gather.7.cloned.1.call-start = ((), (), s32[]{:S(2)}) async-start(), calls=%async_computation.14 | async-start | bytes 2949120 | tf_op jit(solution)/shard_map/all_gather | solution.py:303
  636.8 179.6 %reduce-scatter.14.cloned.1.call-start = ((), (), s32[]{:S(2)}) async-start(), calls=%async_computation.15 | async-start | bytes 2949120 | tf_op jit(solution)/shard_map/reduce_scatter | solution.py:321
  671.4 7.2 copy-start.4
  688.0 5.3 copy-start.18
  705.8 7.2 copy-start.4
  740.2 7.2 copy-start.4
  768.2 7.7 copy-start.31
  776.0 177.1 %all-reduce.9.cloned.1.call-start = ((), (), s32[]{:S(2)}) async-start(), calls=%async_computation.16 | async-start | bytes 6291456 | tf_op jit(solution)/shard_map/psum | solution.py:346
  778.4 5.3 copy-start.16
  778.4 5.3 copy-start.50
  778.4 5.3 copy-start.58
  778.4 415.0 %all-reduce.11.cloned.1.call-start = ((), (), s32[]{:S(2)}) async-start(), calls=%async_computation.18 | async-start | bytes 14155776 | tf_op jit(solution)/shard_map/psum | solution.py:333
  791.9 24.6 %copy-start.47 = (f32[768]{0:T(1024)S(1)}, f32[768]{0:T(1024)}, u32[]{:S(2)}) copy-start(f32[768]{0:T(1024)} %copy-done.46) | copy-start | bytes 9220
  791.9 28.5 %copy-start.56 = (f32[1024]{0:T(1024)S(1)}, f32[1024]{0:T(1024)}, u32[]{:S(2)}) copy-start(f32[1024]{0:T(1024)} %get-tuple-element.306) | copy-start | bytes 12292
  791.9 66.7 %copy-start.17 = (bf16[12,32,768]{2,1,0:T(8,128)(2,1)S(1)}, bf16[12,32,768]{2,1,0:T(8,128)(2,1)}, u32[]{:S(2)}) copy-start(bf16[12,32,768]{2,1,0:T(8,128)(2,1)} %get-tuple-element.309) | copy-start | bytes 1769476
  (74 other events, 230.2 us)
Sparse Core Ops, SparseCore 0:
  205.7 35.7 reduce-scatter.5
  322.7 88.1 all-reduce.6
  420.4 19.7 all-gather.8
  466.0 38.0 reduce-scatter.9
  507.2 28.1 reduce-scatter.7
  546.3 17.7 all-gather.4
  573.6 28.1 reduce-scatter.11
  636.9 22.1 all-gather.6
  776.1 33.0 reduce-scatter.13
  815.1 137.9 all-reduce.8
  958.8 234.6 all-reduce.10
where the time goes:
time: 1220 us; the launch traced here: 1210 us
  waiting for transfers between devices  535 us (44%)
  matrix products  244 us (20%)
  local copies, waits for them, and re-layouts  206 us (17%)
  other arithmetic  106 us (9%)
  blocking collectives  60.4 us (5%)
  loops' own time  22.1 us (2%)
  starting transfers between devices  19.3 us (2%)
  between operations  16.2 us (1%)
    psum x1, waiting for transfers between devices, body(): lax.psum((grad_qkv, grad_qv_bias, grad_out_w, grad_fc1, grad_fc1_bias, gr...  240 us
    psum x1, waiting for transfers between devices, body(): lax.psum((grad_norm1_gain, grad_norm1_shift, grad_out_bias, grad_norm2_ga...  91.8 us
    unnamed x192, local copies, waits for them, and re-layouts  77.1 us
    gather x3, local copies, waits for them, and re-layouts, kept_layout(): seg_kept = jnp.where(live, seg_row[source], clips)  75.4 us
    psum x1, waiting for transfers between devices, body(): summed = lax.psum(part_teach.astype(jnp.bfloat16), 'mp').astype(jnp.float32)  72.2 us
    dot_general x7, matrix products, one_block(): jnp.einsum('hqk,khd->qhd', probs, values, preferred_element_type=jnp.floa...  49.9 us
    sub x4, matrix products, one_block(): expd = jnp.exp(scores - top)  42.8 us
    psum x1, blocking collectives, body(): lax.psum((grad_norm1_gain, grad_norm1_shift, grad_out_bias, grad_norm2_ga...  38.2 us
  transfers between devices with their start and end apart: 14, of which 9 were waited for; matrix products, arithmetic and copies ran while one was open for 18% of the time, Pallas kernels for 0%

commit v1 on v0

v1 whole, which is shorter than its diff:
```python
import functools

import jax
import jax.numpy as jnp
from jax import lax
from jax.experimental import pallas as pl
from jax.experimental.pallas import tpu as pltpu
from jax.sharding import PartitionSpec as P

HD = 64
OWN = 8
CLIPS = 8
EPS = 1e-05
BIG = -1e30
F32 = jnp.float32
BF = jnp.bfloat16
LIMIT = 52 * 2**20

ORD, CUM, END, LOW = 0, 4, 12, 20


def dot_nn(a, b):
    return lax.dot_general(a, b, (((1,), (0,)), ((), ())), preferred_element_type=F32)


def dot_nt(a, b):
    return lax.dot_general(a, b, (((1,), (1,)), ((), ())), preferred_element_type=F32)


def dot_tn(a, b):
    return lax.dot_general(a, b, (((0,), (0,)), ((), ())), preferred_element_type=F32)


def unit(values):
    mean = jnp.mean(values, axis=-1, keepdims=True)
    centred = values - mean
    spread = jnp.mean(centred * centred, axis=-1, keepdims=True)
    inverse = lax.rsqrt(spread + EPS)
    return centred * inverse, inverse


def norm_low(values, gain_ref, shift_ref):
    u, _ = unit(values)
    return (u * gain_ref[...].astype(F32) + shift_ref[...].astype(F32)).astype(BF)


def whole(shape):
    return pl.BlockSpec(shape, lambda *_: (0,) * len(shape))


def call(kernel, name, grid, in_specs, out_specs, out_shape, args, scratch=(), flops=0, scalars=None):
    moved = sum(a.size * a.dtype.itemsize for a in args)
    moved += sum(s.size * jnp.dtype(s.dtype).itemsize for s in jax.tree.leaves(out_shape))
    params = pltpu.CompilerParams(
        dimension_semantics=("arbitrary",) * len(grid), vmem_limit_bytes=LIMIT
    )
    cost = pl.CostEstimate(flops=int(flops), bytes_accessed=int(moved), transcendentals=0)
    lead = 0 if scalars is None else 1
    spec = pltpu.PrefetchScalarGridSpec(
        num_scalar_prefetch=lead,
        grid=grid,
        in_specs=in_specs,
        out_specs=out_specs,
        scratch_shapes=list(scratch),
    )
    run = pl.pallas_call(
        kernel,
        grid_spec=spec,
        out_shape=out_shape,
        compiler_params=params,
        cost_estimate=cost,
        name=name,
    )
    return run(*([scalars] if lead else []), *args)


def sds(shape, dtype):
    return jax.ShapeDtypeStruct(shape, dtype)


def group_of(index, sc, base):
    group = jnp.zeros(index.shape, jnp.int32)
    for c in range(CLIPS):
        group = group + (index >= sc[base + c]).astype(jnp.int32)
    return group


def teacher_kv_kernel(x_ref, g_ref, s_ref, w_ref, b_ref, k_ref, v_ref):
    a = norm_low(x_ref[...].astype(F32), g_ref, s_ref)
    k_ref[...] = dot_nn(a, w_ref[1]).astype(BF)
    v_ref[...] = (dot_nn(a, w_ref[2]) + b_ref[1:2, :].astype(F32)).astype(BF)


def teacher_q_kernel(slots, block, step, sc, x_ref, rank_ref, g_ref, s_ref, w_ref, b_ref, xk_ref, q_ref, acc):
    j = pl.program_id(0)
    pieces, nb, piece, width = xk_ref.shape
    rows = pieces * nb * piece

    def slot_of(lanes):
        row = lax.broadcasted_iota(jnp.int32, (rows, lanes), 0)
        part = row // (nb * piece)
        inner = row % (nb * piece)
        order = jnp.zeros((rows, lanes), jnp.int32)
        for p in range(pieces):
            order = jnp.where(part == p, sc[ORD + p], order)
        return (j * nb + inner // piece) * block + order * piece + inner % piece

    slot = slot_of(step)
    acc[...] = jnp.zeros_like(acc)

    def one(t, _):
        hit = jnp.where(slot == rank_ref[pl.ds(t, 1), :], 1.0, 0.0).astype(BF)
        acc[...] += dot_nn(hit, x_ref[pl.ds(pl.multiple_of(t * step, step), step), :])
        return 0

    steps = slots // nb
    lax.fori_loop(sc[LOW + j], sc[LOW + steps + j], one, 0)
    kept = acc[...]
    xk_ref[...] = kept.astype(BF).reshape(xk_ref.shape)
    a = norm_low(kept, g_ref, s_ref)
    q = (dot_nn(a, w_ref[0]) + b_ref[0:1, :].astype(F32)).astype(BF)
    slot128 = slot_of(128)
    lane = lax.broadcasted_iota(jnp.int32, (rows, 128), 1)
    other = (lane != group_of(slot128, sc, CUM)) & (lane <= CLIPS)
    mask = jnp.where(other, BIG, 0.0).astype(BF)
    pairs = q.shape[1] // 128
    out = []
    for p in range(pairs):
        out += [q[:, 128 * p : 128 * (p + 1)], mask]
    q_ref[...] = jnp.concatenate(out, axis=1).reshape(q_ref.shape)


def teacher_attend_kernel(sc, q_ref, k_ref, v_ref, ctx_ref, kaug, vaug):
    keys, width = k_ref.shape
    heads = width // HD

    @pl.when(pl.program_id(0) == 0)
    def _():
        token = lax.broadcasted_iota(jnp.int32, (keys, 128), 0)
        lane = lax.broadcasted_iota(jnp.int32, (keys, 128), 1)
        hot = jnp.where(lane == group_of(token, sc, END), 1.0, 0.0).astype(BF)
        for h in range(heads):
            pair = h // 2
            mine = (lane // HD) == (h % 2)
            k = k_ref[:, 128 * pair : 128 * (pair + 1)].astype(F32)
            v = v_ref[:, 128 * pair : 128 * (pair + 1)].astype(F32)
            kaug[h, :, :128] = jnp.where(mine, k * (HD**-0.5), 0.0).astype(BF)
            kaug[h, :, 128:] = hot
            vaug[h] = jnp.where(mine, v, 0.0).astype(BF)

    pieces, nb, piece, both = q_ref.shape
    rows = pieces * nb * piece
    q = q_ref[...].reshape(rows, both)
    for pair in range(heads // 2):
        part = q[:, 256 * pair : 256 * (pair + 1)]
        total = jnp.zeros((rows, 128), F32)
        for h in (2 * pair, 2 * pair + 1):
            s = dot_nt(part, kaug[h])
            top = jnp.max(s, axis=1, keepdims=True)
            e = jnp.exp(s - top)
            under = 1.0 / jnp.sum(e, axis=1, keepdims=True)
            total += dot_nn(e.astype(BF), vaug[h]) * under
        ctx_ref[:, :, :, 128 * pair : 128 * (pair + 1)] = total.astype(BF).reshape(pieces, nb, piece, 128)


def student_qkv_kernel(block, used, sc, x_ref, g_ref, s_ref, w_ref, b_ref, xo_ref, a_ref, q_ref, k_ref, v_ref):
    slots, _, piece, width = x_ref.shape
    rows = slots * piece
    x = x_ref[...].reshape(rows, width)
    xo_ref[...] = x
    a = norm_low(x.astype(F32), g_ref, s_ref)
    a_ref[...] = a
    wide = q_ref.shape[1]
    row = lax.broadcasted_iota(jnp.int32, (rows, wide), 0)
    lane = lax.broadcasted_iota(jnp.int32, (rows, wide), 1)
    slot = (row // piece) * block + sc[ORD + pl.program_id(0)] * piece + row % piece
    same = (lane - used) == group_of(slot, sc, CUM)
    other = jnp.logical_not(same) & (lane >= used) & (lane <= used + CLIPS)
    q = (dot_nn(a, w_ref[0]) + b_ref[0:1, :].astype(F32)).astype(BF)
    q_ref[...] = jnp.where(other, BIG, q.astype(F32)).astype(BF)
    k = dot_nn(a, w_ref[1]).astype(BF).astype(F32) * (HD**-0.5)
    k_ref[...] = jnp.where(same, 1.0, k).astype(BF)
    v_ref[...] = (dot_nn(a, w_ref[2]) + b_ref[1:2, :].astype(F32)).astype(BF)


def three(value):
    high = value.astype(BF).astype(F32)
    middle = (value - high).astype(BF).astype(F32)
    return high, middle, value - high - middle


def put_three(base, lane, used, values):
    for h, value in enumerate(values):
        for i, part in enumerate(three(value)):
            base = jnp.where(lane == used + 16 + 8 * i + h, -part, base)
    return base


def one_lanes(lane, used, h):
    hit = lane == used + 16 + h
    return hit | (lane == used + 24 + h) | (lane == used + 32 + h)


def student_attend_kernel(used, q_ref, k_ref, v_ref, ctx_ref, mixed_ref, qb_ref, kaug, vaug):
    keys, wide = k_ref.shape
    heads = used // HD

    @pl.when(pl.program_id(0) == 0)
    def _():
        lane = lax.broadcasted_iota(jnp.int32, (keys, wide), 1)
        k = k_ref[...].astype(F32)
        v = v_ref[...].astype(F32)
        for h in range(heads):
            mine = (lane // HD) == h
            kaug[h] = jnp.where(mine | (lane >= used), k, 0.0).astype(BF)
            vaug[h] = jnp.where(mine, v, 0.0).astype(BF)

    q = q_ref[...]
    rows = q.shape[0]
    total = jnp.zeros((rows, wide), F32)
    logs = []
    for h in range(heads):
        s = dot_nt(q, kaug[h])
        top = jnp.max(s, axis=1, keepdims=True)
        e = jnp.exp(s - top)
        mass = jnp.sum(e, axis=1, keepdims=True)
        total += dot_nn(e.astype(BF), vaug[h]) * (1.0 / mass)
        logs.append(top + jnp.log(mass))
    mixed_ref[...] = total
    ctx_ref[...] = total[:, :used].astype(BF)
    lane = lax.broadcasted_iota(jnp.int32, (rows, wide), 1)
    qb_ref[...] = put_three(q.astype(F32), lane, used, logs).astype(BF)


def student_back_kernel(used, ds_ref, w_ref, mixed_ref, qb_ref, k_ref, v_ref, kt_ref, out_ref, sums_ref, kaug, vaug, dk, dv, dqs):
    keys, wide = k_ref.shape
    heads = used // HD
    j = pl.program_id(0)
    steps = pl.num_programs(0)

    @pl.when(j == 0)
    def _():
        lane = lax.broadcasted_iota(jnp.int32, (keys, wide), 1)
        k = k_ref[...].astype(F32)
        v = v_ref[...].astype(F32)
        for h in range(heads):
            mine = (lane // HD) == h
            ones = one_lanes(lane, used, h)
            keep = mine | ((lane >= used) & (lane <= used + CLIPS))
            kaug[h] = jnp.where(ones, 1.0, jnp.where(keep, k, 0.0)).astype(BF)
            vaug[h] = jnp.where(ones, 1.0, jnp.where(mine, v, 0.0)).astype(BF)
        dk[...] = jnp.zeros_like(dk)
        dv[...] = jnp.zeros_like(dv)
        dqs[...] = jnp.zeros_like(dqs)

    qb = qb_ref[...]
    rows = qb.shape[0]
    lane = lax.broadcasted_iota(jnp.int32, (rows, wide), 1)
    da = dot_nt(ds_ref[...], w_ref[...]).astype(BF).astype(F32)
    product = da * mixed_ref[...]
    deltas = [
        jnp.sum(jnp.where((lane // HD) == h, product, 0.0), axis=1, keepdims=True)
        for h in range(heads)
    ]
    daug = put_three(da, lane, used, deltas).astype(BF)
    qf = qb.astype(F32)
    grads_q = []
    for h in range(heads):
        mine = (lane // HD) == h
        pt = jnp.exp(dot_nt(kaug[h], qb))
        dpt = dot_nt(vaug[h], daug)
        dst = (pt * dpt).astype(BF)
        dv[...] += dot_nn(pt.astype(BF), jnp.where(mine, da, 0.0).astype(BF))
        dk[...] += dot_nn(dst, jnp.where(mine, qf, 0.0).astype(BF))
        grads_q.append(dot_nn(kt_ref[HD * h : HD * (h + 1), :], dst))
    grads_q.append(jnp.zeros((wide - used, rows), F32))
    dq = jnp.concatenate(grads_q, axis=0).T.astype(BF)
    out_ref[pl.ds(pl.multiple_of(j * rows, rows), rows), 0:wide] = dq
    dqs[...] += jnp.sum(dq.astype(F32), axis=0, keepdims=True)

    @pl.when(j == steps - 1)
    def _():
        out_ref[:, wide : 2 * wide] = (dk[...] * (HD**-0.5)).astype(BF)
        low = dv[...].astype(BF)
        out_ref[:, 2 * wide : 3 * wide] = low
        sums_ref[...] = jnp.concatenate(
            [dqs[...], jnp.sum(low.astype(F32), axis=0, keepdims=True)], axis=0
        )


def gelu_both(pre):
    phi = 0.5 * (1.0 + lax.erf(pre * 0.7071067811865476))
    return pre * phi, phi + pre * (0.3989422804014327 * jnp.exp(-0.5 * pre * pre))


def flipped(ref, lo, hi):
    half = ref.shape[0] // 2
    return jnp.concatenate([ref[half:, lo:hi], ref[:half, lo:hi]], axis=0)


def forward_kernel(
    student, half_steps,
    near_ref, far_ref, w0, w1, w2, w3, x_ref, ob_ref, g_ref, s_ref,
    f1a, f1b, b1a, b1b, f2a, f2b, b2_ref, *rest,
):
    if student:
        send_ref, own_ref, sent_ref, a2_ref, act_ref, slope_ref, a2, acc, base = rest
    else:
        send_ref, own_ref, a2, acc, base = rest
    j = pl.program_id(0)
    rows = x_ref.shape[0]

    @pl.when(j == 0)
    def _():
        c = w0.shape[0]
        parts = [
            dot_nn(near_ref[:, :c], w0[...]),
            dot_nn(near_ref[:, c : 2 * c], w1[...]),
            dot_nn(flipped(far_ref, 0, c), w2[...]),
            dot_nn(flipped(far_ref, c, 2 * c), w3[...]),
        ]
        if not student:
            parts = [p.astype(BF).astype(F32) for p in parts]
        resid = x_ref[...].astype(F32) + (parts[0] + parts[1] + parts[2] + parts[3])
        resid = resid + ob_ref[...].astype(F32)
        if student:
            low = resid.astype(BF)
            sent_ref[...] = low
            resid = low.astype(F32)
        a2[...] = norm_low(resid, g_ref, s_ref)
        if student:
            a2_ref[...] = a2[...]
        base[...] = resid[: rows // 2] + b2_ref[...].astype(F32)
        acc[...] = jnp.zeros_like(acc)

    def half(f1, b1, f2):
        pre = dot_nn(a2[...], f1[...]) + b1[...].astype(F32)
        if student:
            act, slope = gelu_both(pre)
            slope_ref[...] = slope
        else:
            act = pre * (0.5 * (1.0 + lax.erf(pre * 0.7071067811865476)))
        act = act.astype(BF)
        if student:
            act_ref[...] = act
        acc[...] += dot_nn(act, f2[...])

    @pl.when(j < half_steps)
    def _():
        half(f1a, b1a, f2a)

    @pl.when(j >= half_steps)
    def _():
        half(f1b, b1b, f2b)

    @pl.when(j == 2 * half_steps - 1)
    def _():
        own_ref[...] = acc[: rows // 2] + base[...]
        send_ref[...] = acc[rows // 2 :].astype(BF)


def forward(student, near, far, w_out, x, out_b, gain, shift, f1, b1, f2, b2, chunk):
    rows, width = near.shape[0], x.shape[1]
    hidden = f1[0].shape[1]
    n = hidden // chunk
    first = lambda j: jnp.minimum(j, n - 1)
    second = lambda j: jnp.maximum(j - n, 0)
    specs = [whole(near.shape), whole(far.shape)] + [whole(w.shape) for w in w_out]
    specs += [pl.BlockSpec((rows, width), lambda j: (0, 0))] + [whole((1, width))] * 3
    specs += [pl.BlockSpec((width, chunk), lambda j, f=f: (0, f(j))) for f in (first, second)]
    specs += [pl.BlockSpec((1, chunk), lambda j, f=f: (0, f(j))) for f in (first, second)]
    specs += [pl.BlockSpec((chunk, width), lambda j, f=f: (f(j), 0)) for f in (first, second)]
    specs += [whole((1, width))]
    half = rows // 2
    outs = [sds((half, width), BF), sds((half, width), F32)]
    out_specs = [whole((half, width))] * 2
    if student:
        outs += [sds((rows, width), BF)] * 2 + [sds((rows, 2 * hidden), BF), sds((rows, 2 * hidden), F32)]
        out_specs += [whole((rows, width))] * 2 + [pl.BlockSpec((rows, chunk), lambda j: (0, j))] * 2
    return call(
        functools.partial(forward_kernel, student, n),
        "student_forward" if student else "teacher_forward",
        (2 * n,),
        specs,
        out_specs,
        outs,
        (near, far, *w_out, x, out_b, gain, shift, *f1, *b1, *f2, b2),
        scratch=[pltpu.VMEM((rows, width), BF), pltpu.VMEM((rows, width), F32), pltpu.VMEM((half, width), F32)],
        flops=2 * rows * width * (4 * w_out[0].shape[0] + 4 * hidden),
    )


def head_kernel(block, sc, own_ref, recv_ref, out_ref, w_ref, b_ref, inv_ref, dg_ref, do_ref, loss_ref, hb_ref, ob_ref):
    rows, width = own_ref.shape
    target = (own_ref[...] + recv_ref[...].astype(F32)).astype(BF).astype(F32)
    row = lax.broadcasted_iota(jnp.int32, (rows, 1), 0)
    piece = block // 4
    slot = (row // piece) * block + sc[ORD] * piece + row % piece
    live = slot < sc[CUM + CLIPS - 1]
    group = group_of(slot, sc, CUM)
    weight = jnp.zeros((rows, 1), F32)
    for c in range(CLIPS):
        weight = jnp.where(group == c, inv_ref[0, c], weight)
    weight = jnp.where(live, weight, 0.0)
    target = jnp.where(live, target, 0.0)
    miss = dot_nn(out_ref[...], w_ref[...]) + b_ref[...].astype(F32) - target
    dg = (weight * miss).astype(BF)
    dg_ref[...] = dg
    loss_ref[...] = 0.5 * jnp.sum(weight * miss * miss, axis=0, keepdims=True)
    hb_ref[...] = jnp.sum(dg.astype(F32), axis=0, keepdims=True)
    do = dot_nt(dg, w_ref[...]).astype(BF)
    do_ref[...] = do
    ob_ref[...] = jnp.sum(do.astype(F32), axis=0, keepdims=True)


def feed_back_kernel(d0, d1, act_ref, slope_ref, a2_ref, f1a, f1b, f2a, f2b,
                     g1_ref, g1s_ref, g2_ref, g2s_ref, own_ref, send_ref, gb_ref, d, acc):
    j = pl.program_id(0)
    half = d0.shape[0]

    @pl.when(j == 0)
    def _():
        d[:half] = d0[...]
        d[half:] = d1[...]
        acc[...] = jnp.zeros_like(acc)

    def part(f1, f2, g1, g2):
        grad = d[...]
        dpre = (dot_nt(grad, f2[...]) * slope_ref[...]).astype(BF)
        gb_ref[...] = jnp.sum(dpre.astype(F32), axis=0, keepdims=True)
        acc[...] += dot_nt(dpre, f1[...])
        g2[...] = dot_tn(act_ref[...], grad).astype(g2.dtype)
        g1[...] = dot_tn(a2_ref[...], dpre).astype(g1.dtype)

    @pl.when(j == 0)
    def _():
        part(f1a, f2a, g1_ref, g2_ref)

    @pl.when(j == 1)
    def _():
        part(f1b, f2b, g1s_ref, g2s_ref)
        own_ref[...] = acc[:half]
        send_ref[...] = acc[half:].astype(BF)


def norm_back_kernel(own_ref, recv_ref, base_ref, x_ref, g_ref, dx_ref, sums_ref):
    d = own_ref[...].astype(F32) + recv_ref[...].astype(F32)
    u, inverse = unit(x_ref[...].astype(F32))
    e = g_ref[...].astype(F32) * d
    mean_e = jnp.mean(e, axis=-1, keepdims=True)
    mean_eu = jnp.mean(e * u, axis=-1, keepdims=True)
    dx = base_ref[...].astype(F32) + (e - mean_e - u * mean_eu) * inverse
    dx = dx.astype(dx_ref.dtype)
    dx_ref[...] = dx
    sums_ref[...] = jnp.concatenate(
        [
            jnp.sum(d * u, axis=0, keepdims=True),
            jnp.sum(d, axis=0, keepdims=True),
            jnp.sum(dx.astype(F32), axis=0, keepdims=True),
        ],
        axis=0,
    )


def norm_back(name, own, recv, base, x, gain, dtype):
    rows, width = own.shape
    half = pl.BlockSpec((rows, width), lambda *_: (0, 0))
    return call(
        norm_back_kernel, name, (1,),
        [half] * 4 + [whole((1, width))],
        [half, whole((3, width))],
        [sds((rows, width), dtype), sds((3, width), F32)],
        (own, recv, base, x, gain),
    )


def swap(x, bit, count):
    return lax.ppermute(x, "mp", [(i, i ^ bit) for i in range(count)])


def row(vector):
    return vector.reshape(1, -1)


def layout(mask_row, seg_row, order, steps, span):
    tokens = mask_row.shape[0]
    grid = mask_row.reshape(tokens // 128, 128).astype(BF)
    upper = (jnp.arange(128)[:, None] <= jnp.arange(128)[None, :]).astype(BF)
    within = jnp.dot(grid, upper, preferred_element_type=F32)
    lines = tokens // 128
    lower = (jnp.arange(lines)[:, None] > jnp.arange(lines)[None, :]).astype(BF)
    ahead = jnp.dot(lower, within[:, 127:].astype(BF), preferred_element_type=F32)
    count = (within + ahead).astype(jnp.int32).reshape(tokens)
    rank = jnp.where(mask_row == 1, count - 1, -1)
    labels = jnp.arange(CLIPS, dtype=jnp.int32)
    upto = (seg_row[None, :] <= labels[:, None]).astype(jnp.int32)
    ends = jnp.sum(upto, axis=1)
    cum = jnp.sum(upto * mask_row[None, :], axis=1)
    edge = jnp.arange(steps, dtype=jnp.int32) * span
    low = jnp.sum((count[None, :] <= edge[:, None]).astype(jnp.int32), axis=1)
    high = jnp.sum((count[None, :] < edge[:, None] + span).astype(jnp.int32), axis=1)
    low = low // span
    high = jnp.minimum(high, tokens - 1) // span + 1
    each = cum - jnp.concatenate([jnp.zeros((1,), jnp.int32), cum[:-1]])
    inverse = 1.0 / jnp.maximum(each, 1).astype(F32)
    scalars = jnp.concatenate([order, cum, ends, low, high])
    return rank.reshape(tokens // span, span), scalars, inverse.reshape(1, CLIPS)


def body(
    teacher_in, segment_ids, keep_mask, block_owner, student_in,
    t_norm1_gain, t_norm1_shift, t_qkv, t_qv_bias, t_out, t_out_bias,
    t_norm2_gain, t_norm2_shift, t_fc1, t_fc1_bias, t_fc2, t_fc2_bias,
    s_norm1_gain, s_norm1_shift, s_qkv, s_qv_bias, s_out, s_out_bias,
    s_norm2_gain, s_norm2_shift, s_fc1, s_fc1_bias, s_fc2, s_fc2_bias,
    head_weight, head_bias,
):
    mp = lax.axis_size("mp")
    me = lax.axis_index("mp")
    homes = lax.axis_size("dp")
    home = lax.axis_index("dp")
    slots, block, width = student_in.shape
    piece = block // mp
    rows = slots * block
    mine = rows // mp
    near = 2 * mine
    tokens, t_width = teacher_in.shape
    used = s_qkv.shape[2]
    wide = 256
    nb = 2
    span = nb * block
    steps = slots // nb
    core = lambda x: swap(x, 1, mp)
    across = lambda x: swap(x, 2, mp)

    order = jnp.stack([me, me ^ 2, me ^ 1, me ^ 3]).astype(jnp.int32)
    mask_row = lax.dynamic_index_in_dim(keep_mask, home, 0, keepdims=False)
    seg_row = lax.dynamic_index_in_dim(segment_ids, home, 0, keepdims=False)
    rank, scalars, inverse = layout(mask_row, seg_row, order, steps, span)

    t_w2 = across(t_out)
    s_w2 = across(s_out)
    t_f1 = (t_fc1, core(t_fc1))
    t_f2 = (t_fc2, core(t_fc2))
    s_f1 = (s_fc1, core(s_fc1))
    s_f2 = (s_fc2, core(s_fc2))
    biases = core(jnp.concatenate([t_fc1_bias, s_fc1_bias]))
    t_b1 = (row(t_fc1_bias), row(biases[: t_fc1_bias.shape[0]]))
    s_b1 = (row(s_fc1_bias), row(biases[t_fc1_bias.shape[0] :]))
    t_w = (t_out, core(t_out), t_w2, core(t_w2))
    s_w = (s_out, core(s_out), s_w2, core(s_w2))

    w_pad = jnp.pad(s_qkv, ((0, 0), (0, 0), (0, wide - used)))
    b_pad = jnp.pad(s_qv_bias, ((0, 0), (0, wide - used)))
    x4 = student_in.reshape(slots, mp, piece, width)
    by_piece = lambda w: pl.BlockSpec((mine, w), lambda k, sc: (k, 0))
    x_stud, a_stud, sq, sk, sv = call(
        functools.partial(student_qkv_kernel, block, used), "student_qkv", (mp,),
        [
            pl.BlockSpec((slots, 1, piece, width), lambda k, sc: (0, sc[ORD + k], 0, 0)),
            whole((1, width)), whole((1, width)), whole(w_pad.shape), whole(b_pad.shape),
        ],
        [by_piece(width)] * 2 + [by_piece(wide)] * 3,
        [sds((rows, width), BF)] * 2 + [sds((rows, wide), BF)] * 3,
        (x4, row(s_norm1_gain), row(s_norm1_shift), w_pad, b_pad),
        flops=2 * rows * width * 3 * wide, scalars=scalars,
    )
    heads = used // HD
    qrows = 256
    by_rows = lambda w: pl.BlockSpec((qrows, w), lambda j: (j, 0))
    ctx, mixed, qb = call(
        functools.partial(student_attend_kernel, used), "student_attend", (rows // qrows,),
        [by_rows(wide), whole((rows, wide)), whole((rows, wide))],
        [by_rows(used), by_rows(wide), by_rows(wide)],
        [sds((rows, used), BF), sds((rows, wide), F32), sds((rows, wide), BF)],
        (sq, sk, sv),
        scratch=[pltpu.VMEM((heads, rows, wide), BF)] * 2,
        flops=heads * rows * rows * wide * 4,
    )
    s_near = jnp.concatenate([ctx[:near], core(ctx[near:])], axis=1)
    s_far = across(s_near)

    by_512 = lambda w: pl.BlockSpec((512, w), lambda j: (j, 0))
    cols = t_qkv.shape[2]
    tk, tv = call(
        teacher_kv_kernel, "teacher_kv", (tokens // 512,),
        [by_512(t_width), whole((1, t_width)), whole((1, t_width)), whole(t_qkv.shape), whole(t_qv_bias.shape)],
        [by_512(cols)] * 2,
        [sds((tokens, cols), BF)] * 2,
        (teacher_in, row(t_norm1_gain), row(t_norm1_shift), t_qkv, t_qv_bias),
        flops=2 * tokens * t_width * 2 * cols,
    )
    by_slot = lambda w: pl.BlockSpec((mp, nb, piece, w), lambda j, sc: (0, j, 0, 0))
    x_kept, tq = call(
        functools.partial(teacher_q_kernel, slots, block, span), "teacher_q", (steps,),
        [
            whole(teacher_in.shape), whole(rank.shape), whole((1, t_width)), whole((1, t_width)),
            whole(t_qkv.shape), whole(t_qv_bias.shape),
        ],
        [by_slot(t_width), by_slot(2 * cols)],
        [sds((mp, slots, piece, t_width), BF), sds((mp, slots, piece, 2 * cols), BF)],
        (teacher_in, rank, row(t_norm1_gain), row(t_norm1_shift), t_qkv, t_qv_bias),
        scratch=[pltpu.VMEM((span, t_width), F32)],
        flops=2 * rows * t_width * (cols + 512), scalars=scalars,
    )
    t_ctx = call(
        teacher_attend_kernel, "teacher_attend", (steps,),
        [by_slot(2 * cols), whole((tokens, cols)), whole((tokens, cols))],
        by_slot(cols),
        sds((mp, slots, piece, cols), BF),
        (tq, tk, tv),
        scratch=[pltpu.VMEM((cols // HD, tokens, 256), BF), pltpu.VMEM((cols // HD, tokens, 128), BF)],
        flops=(cols // HD) * rows * tokens * (512 + 256), scalars=scalars,
    ).reshape(rows, cols)
    t_near = jnp.concatenate([t_ctx[:near], core(t_ctx[near:])], axis=1)
    t_far = across(t_near)

    s_send, s_own, sent, a2, act, slope = forward(
        True, s_near, s_far, s_w, x_stud, row(s_out_bias), row(s_norm2_gain), row(s_norm2_shift),
        s_f1, s_b1, s_f2, row(s_fc2_bias), s_fc1.shape[1],
    )
    out_rows = (s_own + across(s_send).astype(F32)).astype(BF)

    t_send, t_own = forward(
        False, t_near, t_far, t_w, x_kept.reshape(rows, t_width), row(t_out_bias), row(t_norm2_gain),
        row(t_norm2_shift), t_f1, t_b1, t_f2, row(t_fc2_bias), 512,
    )
    t_recv = across(t_send)

    owners = lax.dynamic_index_in_dim(block_owner, home, 0, keepdims=False)
    capacity = (slots + homes - 1) // homes
    labels = jnp.arange(homes, dtype=jnp.int32)
    hits = (owners[:, None] == labels[None, :]).astype(jnp.int32)
    order_in = jnp.sum((jnp.cumsum(hits, axis=0) - hits) * hits, axis=1)
    place = jnp.where(owners >= 0, owners * capacity + order_in, homes * capacity)
    pick = (jnp.arange(homes * capacity, dtype=jnp.int32)[:, None] == place[None, :]).astype(BF)
    outbound = jnp.dot(pick, out_rows.reshape(slots, piece * width), preferred_element_type=BF)
    inbound = lax.all_to_all(
        outbound.reshape(homes * capacity, piece, width), "dp", split_axis=0, concat_axis=0, tiled=True
    )
    per_source = jnp.sum((block_owner == home).astype(jnp.int32), axis=1)
    before = jnp.cumsum(per_source) - per_source
    lane = jnp.arange(capacity, dtype=jnp.int32)
    target_slot = jnp.where(lane[None, :] < per_source[:, None], before[:, None] + lane[None, :], OWN).reshape(-1)
    choose = (jnp.arange(OWN, dtype=jnp.int32)[:, None] == target_slot[None, :]).astype(BF)
    student_out = jnp.dot(
        choose, inbound.reshape(homes * capacity, piece * width), preferred_element_type=BF
    ).reshape(OWN, piece, width)

    d_guess, d_out, loss_row, head_b_row, fc2_b_row = call(
        functools.partial(head_kernel, block), "head", (1,),
        [
            whole((mine, t_width)), whole((mine, t_width)), whole((mine, width)), whole((width, t_width)),
            whole((1, t_width)), pl.BlockSpec(memory_space=pltpu.SMEM),
        ],
        [whole((mine, t_width)), whole((mine, width)), whole((1, t_width)), whole((1, t_width)), whole((1, width))],
        [sds((mine, t_width), BF), sds((mine, width), BF), sds((1, t_width), F32), sds((1, t_width), F32), sds((1, width), F32)],
        (t_own, t_recv, out_rows, head_weight, row(head_bias), inverse),
        flops=4 * mine * width * t_width, scalars=scalars,
    )
    d_out_far = across(d_out)
    g_head = dot_tn(out_rows, d_guess)

    hidden = s_fc1.shape[1]
    cut = pl.BlockSpec((near, hidden), lambda j: (0, j))
    g1, g1_send, g2, g2_send, da2_own, da2_send, b1_row = call(
        feed_back_kernel, "feed_back", (2,),
        [whole((mine, width))] * 2 + [cut, cut, whole((near, width))]
        + [whole((width, hidden))] * 2 + [whole((hidden, width))] * 2,
        [whole((width, hidden))] * 2 + [whole((hidden, width))] * 2 + [whole((mine, width))] * 2
        + [pl.BlockSpec((1, hidden), lambda j: (0, j))],
        [
            sds((width, hidden), F32), sds((width, hidden), BF), sds((hidden, width), F32), sds((hidden, width), BF),
            sds((mine, width), F32), sds((mine, width), BF), sds((1, 2 * hidden), F32),
        ],
        (d_out, d_out_far, act, slope, a2, *s_f1, *s_f2),
        scratch=[pltpu.VMEM((near, width), BF), pltpu.VMEM((near, width), F32)],
        flops=2 * near * width * hidden * 8,
    )
    da2_far = across(da2_send)
    d_sent, sums2 = norm_back("norm2_back", da2_own, da2_far, d_out, sent[:mine], row(s_norm2_gain), BF)

    side = me % 2
    level = me // 2
    half_rows = width // 2
    quarter = width // 4
    low_head = g_head.astype(BF)
    head_send = lax.dynamic_slice_in_dim(low_head, (1 - side) * half_rows, half_rows, 0)
    head_half = lax.dynamic_slice_in_dim(g_head, side * half_rows, half_rows, 0) + core(head_send).astype(F32)
    low_half = head_half.astype(BF)
    head_send2 = lax.dynamic_slice_in_dim(low_half, (1 - level) * quarter, quarter, 0)
    head_quarter = lax.dynamic_slice_in_dim(head_half, level * quarter, quarter, 0) + across(head_send2).astype(F32)

    g2_sum = (g2 + core(g2_send).astype(F32)).astype(BF)
    g1_sum = (g1 + core(g1_send).astype(F32)).astype(BF)
    head_all = lax.psum(head_quarter.astype(BF), "dp")
    g2_all = lax.psum(g2_sum, "dp")
    g1_all = lax.psum(g1_sum, "dp")

    ds_near = jnp.concatenate([d_sent, across(d_sent)], axis=0)
    ds = jnp.concatenate([ds_near, core(ds_near)], axis=0)
    so_pad = jnp.pad(s_out, ((0, wide - used), (0, 0)))
    k_turned = sk[:, :used].T
    d_qkv, qv_sums = call(
        functools.partial(student_back_kernel, used), "student_back", (rows // qrows,),
        [
            by_rows(width), whole((wide, width)), by_rows(wide), by_rows(wide), whole((rows, wide)),
            whole((rows, wide)), whole((used, rows)),
        ],
        [whole((rows, 3 * wide)), whole((2, wide))],
        [sds((rows, 3 * wide), BF), sds((2, wide), F32)],
        (ds, so_pad, mixed, qb, sk, sv, k_turned),
        scratch=[pltpu.VMEM((heads, rows, wide), BF)] * 2 + [pltpu.VMEM((rows, wide), F32)] * 2
        + [pltpu.VMEM((1, wide), F32)],
        flops=heads * rows * rows * wide * 9,
    )
    g_out = dot_tn(ctx, ds)
    w_line = jnp.transpose(w_pad, (0, 2, 1)).reshape(3 * wide, width)
    da1 = dot_nn(d_qkv, w_line)
    da1_near = da1[:near] + core(da1[near:].astype(BF)).astype(F32)
    da1_far = across(da1_near[mine:].astype(BF))
    g_qkv = dot_tn(a_stud, d_qkv).reshape(width, 3, wide)[:, :, :used]
    grad_in, sums1 = norm_back("norm1_back", da1_near[:mine], da1_far, d_sent, x_stud[:mine], row(s_norm1_gain), F32)

    fit = lambda v: jnp.pad(v, ((0, 0), (0, t_width - v.shape[1])))
    short = jnp.concatenate(
        [fit(sums1[:2]), fit(sums2), fit(fc2_b_row), head_b_row, loss_row, fit(b1_row[:, hidden:])], axis=0
    )
    short_in = core(short)
    short_own = jnp.concatenate([short[:8], fit(b1_row[:, :hidden])], axis=0) + short_in
    short_sum = short_own[:8] + across(short_own[:8])
    short_dp = jnp.concatenate([short_sum, short_own[8:], fit(qv_sums)], axis=0)
    qkv_all, out_all, short_all = lax.psum((g_qkv.astype(BF), g_out.astype(BF), short_dp.astype(BF)), "dp")

    head_other = across(head_all)
    head_pair = jnp.where(
        level == 0,
        jnp.concatenate([head_all, head_other], axis=0),
        jnp.concatenate([head_other, head_all], axis=0),
    )
    head_peer = core(head_pair)
    grad_head = jnp.where(
        side == 0,
        jnp.concatenate([head_pair, head_peer], axis=0),
        jnp.concatenate([head_peer, head_pair], axis=0),
    ).astype(F32)
    vec = short_all.astype(F32)
    return (
        jnp.sum(vec[7]),
        student_out,
        grad_in.reshape(slots, piece, width),
        vec[0, :width],
        vec[1, :width],
        jnp.transpose(qkv_all.astype(F32), (1, 0, 2)),
        vec[9:11, :used],
        out_all.astype(F32),
        vec[4, :width],
        vec[2, :width],
        vec[3, :width],
        g1_all.astype(F32),
        vec[8, :hidden],
        g2_all.astype(F32),
        vec[5, :width],
        grad_head,
        vec[6, :t_width],
    )


def solution(mesh):
    rep = P()
    in_specs = (
        P("dp", None), rep, rep, rep, P("dp", None, None), rep, rep, P(None, None, "mp"), P(None, "mp"),
        P("mp", None), rep, rep, rep, P(None, "mp"), P("mp"), P("mp", None), rep, rep, rep,
        P(None, None, "mp"), P(None, "mp"), P("mp", None), rep, rep, rep, P(None, "mp"), P("mp"),
        P("mp", None), rep, rep, rep,
    )
    out_specs = (
        rep, P("dp", "mp", None), P("dp", "mp", None), rep, rep, P(None, None, "mp"), P(None, "mp"),
        P("mp", None), rep, rep, rep, P(None, "mp"), P("mp"), P("mp", None), rep, rep, rep,
    )
    return jax.shard_map(body, mesh=mesh, in_specs=in_specs, out_specs=out_specs, check_vma=False)
```

time: 1220 us -> 528 us (0.43)
  waiting for transfers between devices: 535 us -> 215 us
  matrix products: 244 us -> 12.6 us
  local copies, waits for them, and re-layouts: 206 us -> 38.6 us
  Pallas kernels: 0 us -> 149 us
  other arithmetic: 106 us -> 24.4 us
  blocking collectives: 60.4 us -> 35.3 us
  loops' own time: 22.1 us -> 0 us
    psum x3 -> x1, waiting for transfers between devices: 404 us -> 144 us  [body(): lax.psum((g_qkv.astype(BF), g_out.astype(BF), short_dp.astype(BF)), 'dp')]
    dot_general x42 -> x8, matrix products: 200 us -> 12.6 us  [the longest x3 6.15 us: dot_tn(): lax.dot_general(a, b, (((0,), (0,)), ((), ())), preferred_element_type=F32)]
    pallas_call x0 -> x12, Pallas kernels: none -> 149 us  [call(): return run(*([scalars] if lead else []), *args)]
    gather x8 -> x0, local copies, waits for them, and re-layouts: 89 us -> none  [the longest x3 75.4 us: kept_layout(): seg_kept = jnp.where(live, seg_row[source], clips)]
    ppermute x0 -> x31, waiting for transfers between devices: none -> 71.6 us  [swap(): return lax.ppermute(x, 'mp', [(i, i ^ bit) for i in range(count)])]
    unnamed x192 -> x121, local copies, waits for them, and re-layouts: 77.1 us -> 18.8 us
    reduce_scatter x5 -> x0, waiting for transfers between devices: 47.1 us -> none  [the longest x1 28.2 us: body(): lax.psum_scatter(grad_a2.astype(jnp.bfloat16), 'mp', scatter_dimension=1,...]
    all_to_all x3 -> x1, waiting for transfers between devices: 43.4 us -> 0.01 us  [body(): lax.all_to_all(outbound.reshape(homes * capacity, piece, width), 'dp', sp...]
  transfers between devices with their start and end apart: 14 -> 33, of which waited for: 9 -> 12; matrix products, arithmetic and copies ran while one was open for 18% -> 10% of each run, Pallas kernels for 0% -> 23%
where the time goes in v1:
time: 528 us; the launch traced here: 518 us
  waiting for transfers between devices  215 us (41%)
  Pallas kernels  149 us (28%)
  local copies, waits for them, and re-layouts  38.6 us (7%)
  blocking collectives  35.3 us (7%)
  starting transfers between devices  27 us (5%)
  other arithmetic  24.4 us (5%)
  between operations  15.5 us (3%)
  matrix products  12.6 us (2%)
    pallas_call x12, Pallas kernels, call(): return run(*([scalars] if lead else []), *args)  149 us
    psum x1, waiting for transfers between devices, body(): lax.psum((g_qkv.astype(BF), g_out.astype(BF), short_dp.astype(BF)), 'dp')  144 us
    ppermute x31, waiting for transfers between devices, swap(): return lax.ppermute(x, 'mp', [(i, i ^ bit) for i in range(count)])  71.6 us
    psum x1, blocking collectives, body(): lax.psum((g_qkv.astype(BF), g_out.astype(BF), short_dp.astype(BF)), 'dp')  35.3 us
    ppermute x31, starting transfers between devices, swap(): return lax.ppermute(x, 'mp', [(i, i ^ bit) for i in range(count)])  21.2 us
    unnamed x121, local copies, waits for them, and re-layouts  18.8 us
  transfers between devices with their start and end apart: 33, of which 12 were waited for; matrix products, arithmetic and copies ran while one was open for 10% of the time, Pallas kernels for 23%

profile of v1, /device:TPU:0, one launch (start us, length us, event | category | flops | bytes accessed | tf_op | source)
XLA Modules:
  0.0 517.7 jit_solution(6743721291737502276)
XLA Ops:
  7.2 3.0 collective-permute-start.12
  16.0 1.5 copy.65
  17.5 1.6 pad_bitcast_fusion
  19.6 7.4 %teacher_kv.1 = (bf16[2048,256]{1,0:T(8,128)(2,1)S(1)}, bf16[2048,256]{1,0:T(8,128)(2,1)}) custom-call(bf16[2048,1024]{1,0:T(8,128)(2,1)} %x_ref.3, bf16[1,1024]{1,0:T(2,128)(2,1)S(1)} %reshape.246.g_ref, bf16[1,1024]{1,0:T(2,128)(2,1)S(1)} %reshape.247.s_ref, bf16[3,1024,256]{2,1,0:T(8,128)(2,1)} %w_ref.4, bf16[2,256]{1,0:T(2,128)(2,1)S(1)} %copy-done.11), custom_call_target="tpu_custom_call" | custom-call | flops 2147483648 | bytes 7869440 | tf_op jit(solution)/shard_map/teacher_kv/pallas_call | solution.py:74
  27.0 11.9 %teacher_q.1 = (bf16[4,12,32,1024]{3,2,1,0:T(8,128)(2,1)}, bf16[4,12,32,512]{3,2,1,0:T(8,128)(2,1)S(1)}) custom-call(s32[32]{0:T(128)S(1)} %concatenate.55.sc, bf16[2048,1024]{1,0:T(8,128)(2,1)} %x_ref.3, s32[8,256]{1,0:T(8,128)S(1)} %broadcast_select_fusion.rank_ref, bf16[1,1024]{1,0:T(2,128)(2,1)S(1)} %reshape.246.g_ref, ...), custom_call_target="tpu_custom_call" | custom-call | flops 2415919104 | bytes 10499072 | tf_op jit(solution)/shard_map/teacher_q/pallas_call | solution.py:74
  40.1 23.9 %teacher_attend.1 = bf16[4,12,32,256]{3,2,1,0:T(8,128)(2,1)S(1)} custom-call(s32[32]{0:T(128)S(1)} %concatenate.55.sc, bf16[4,12,32,512]{3,2,1,0:T(8,128)(2,1)} %copy-done.12, bf16[2048,256]{1,0:T(8,128)(2,1)S(1)} %get-tuple-element.56.k_ref, bf16[2048,256]{1,0:T(8,128)(2,1)} %get-tuple-element.57.v_ref), custom_call_target="tpu_custom_call" | custom-call | flops 9663676416 | bytes 4456448 | tf_op jit(solution)/shard_map/teacher_attend/pallas_call | solution.py:74
  64.0 6.7 %student_qkv.1 = (bf16[1536,768]{1,0:T(8,128)(2,1)}, bf16[1536,768]{1,0:T(8,128)(2,1)}, bf16[1536,256]{1,0:T(8,128)(2,1)S(1)}, bf16[1536,256]{1,0:T(8,128)(2,1)S(1)}, bf16[1536,256]{1,0:T(8,128)(2,1)}) custom-call(s32[32]{0:T(128)S(1)} %concatenate.55.sc, bf16[12,4,32,768]{3,2,1,0:T(8,128)(2,1)} %bitcast.89, bf16[1,768]{1,0:T(2,128)(2,1)S(1)} %reshape.256.g_ref, ...), custom_call_target="tpu_custom_call" | custom-call | flops 1811939328 | bytes 10620928 | tf_op jit(solution)/shard_map/student_qkv/pallas_call | solution.py:74
  72.4 16.9 %student_attend.1 = (bf16[1536,192]{1,0:T(8,128)(2,1)S(1)}, f32[1536,256]{1,0:T(8,128)}, bf16[1536,256]{1,0:T(8,128)(2,1)S(1)}) custom-call(bf16[1536,256]{1,0:T(8,128)(2,1)} %copy-done.13, bf16[1536,256]{1,0:T(8,128)(2,1)} %copy-done.2, bf16[1536,256]{1,0:T(8,128)(2,1)} %get-tuple-element.63.v_ref), custom_call_target="tpu_custom_call" | custom-call | flops 7247757312 | bytes 5308416 | tf_op jit(solution)/shard_map/student_attend/pallas_call | solution.py:74
  91.0 3.8 collective-permute-done.9
  95.7 4.1 collective-permute-done.13.w3
  99.8 1.9 collective-permute-start.10
  101.7 13.6 %collective-permute-done.10.far_ref = bf16[768,384]{1,0:T(8,128)(2,1)S(1)} collective-permute-done((bf16[768,384]{1,0:T(8,128)(2,1)S(1)}, bf16[768,384]{1,0:T(8,128)(2,1)S(1)}, u32[]{:S(2)}, u32[]{:S(2)}) %collective-permute-start.10) | collective-permute-done | bytes 589856 | tf_op jit(solution)/shard_map/ppermute | solution.py:478
  115.3 1.7 collective-permute-start.1
  118.4 13.8 %student_forward.1 = (bf16[384,768]{1,0:T(8,128)(2,1)S(1)}, f32[384,768]{1,0:T(8,128)}, bf16[768,768]{1,0:T(8,128)(2,1)}, bf16[768,768]{1,0:T(8,128)(2,1)}, bf16...) custom-call(bf16[768,384]{1,0:T(8,128)(2,1)} %copy-done.31, bf16[768,384]{1,0:T(8,128)(2,1)} %copy-done.55, ...), custom_call_target="tpu_custom_call" | custom-call | flops 4529848320 | bytes 20653056 | tf_op jit(solution)/shard_map/student_forward/pallas_call | solution.py:74
  132.6 1.6 collective-permute-done.1.far_ref
  135.2 16.8 %teacher_forward.1 = (bf16[384,1024]{1,0:T(8,128)(2,1)}, f32[384,1024]{1,0:T(8,128)}) custom-call(bf16[768,512]{1,0:T(8,128)(2,1)} %copy-done.29, bf16[768,512]{1,0:T(8,128)(2,1)} %copy-done.54, bf16[256,1024]{1,0:T(8,128)(2,1)S(1)} %copy-done.10, bf16[256,1024]{1,0:T(8,128)(2,1)S(1)} %collective-permute-done.2.w1, ...), custom_call_target="tpu_custom_call" | custom-call | flops 8053063680 | bytes 17575936 | tf_op jit(solution)/shard_map/teacher_forward/pallas_call | solution.py:74
  152.0 1.9 collective-permute-start.8
  154.1 16.1 %collective-permute-done.8.recv_ref = bf16[384,1024]{1,0:T(8,128)(2,1)S(1)} collective-permute-done((bf16[384,1024]{1,0:T(8,128)(2,1)}, bf16[384,1024]{1,0:T(8,128)(2,1)S(1)}, u32[]{:S(2)}, u32[]{:S(2)}) %collective-permute-start.8) | collective-permute-done | bytes 786464 | tf_op jit(solution)/shard_map/ppermute | solution.py:478
  171.1 4.6 head.1
  175.7 1.7 collective-permute-start.17
  179.6 9.0 %collective-permute-done.17.d1 = bf16[384,768]{1,0:T(8,128)(2,1)S(1)} collective-permute-done((bf16[384,768]{1,0:T(8,128)(2,1)S(1)}, bf16[384,768]{1,0:T(8,128)(2,1)S(1)}, u32[]{:S(2)}, u32[]{:S(2)}) %collective-permute-start.17) | collective-permute-done | bytes 589856 | tf_op jit(solution)/shard_map/ppermute | solution.py:478
  190.5 15.4 %feed_back.1 = (f32[768,768]{1,0:T(8,128)}, bf16[768,768]{1,0:T(8,128)(2,1)}, f32[768,768]{1,0:T(8,128)}, bf16[768,768]{1,0:T(8,128)(2,1)}, f32[384,768]{1,0:T(8...) custom-call(bf16[384,768]{1,0:T(8,128)(2,1)S(1)} %get-tuple-element.68.d0.base_ref, ...), custom_call_target="tpu_custom_call" | custom-call | flops 7247757312 | bytes 23009280 | tf_op jit(solution)/shard_map/feed_back/pallas_call | solution.py:74
  208.4 1.9 slice.118.x_ref
  210.9 2.0 convert_add_fusion
  212.9 5.2 %collective-permute-done.18.recv_ref = bf16[384,768]{1,0:T(8,128)(2,1)S(1)} collective-permute-done((bf16[384,768]{1,0:T(8,128)(2,1)}, bf16[384,768]{1,0:T(8,128)(2,1)S(1)}, u32[]{:S(2)}, u32[]{:S(2)}) %collective-permute-start.18) | collective-permute-done | bytes 589856 | tf_op jit(solution)/shard_map/ppermute | solution.py:478
  220.0 2.6 norm2_back.1
  225.6 12.4 %collective-permute-done.19 = bf16[384,768]{1,0:T(8,128)(2,1)} collective-permute-done((bf16[384,768]{1,0:T(8,128)(2,1)S(1)}, bf16[384,768]{1,0:T(8,128)(2,1)}, u32[]{:S(2)}, u32[]{:S(2)}) %collective-permute-start.19) | collective-permute-done | bytes 589856 | tf_op jit(solution)/shard_map/ppermute | solution.py:478
  239.3 2.9 collective-permute-done.28
  242.2 1.8 add_convert_fusion.3
  245.2 2.8 add_convert_fusion.1
  248.0 2.6 add_convert_fusion
  252.4 25.6 %student_back.1 = (bf16[1536,768]{1,0:T(8,128)(2,1)}, f32[2,256]{1,0:T(2,128)S(1)}) custom-call(bf16[1536,768]{1,0:T(8,128)(2,1)} %copy-done.34, bf16[256,768]{1,0:T(8,128)(2,1)S(1)} %pad.37.w_ref, f32[1536,256]{1,0:T(8,128)} %get-tuple-element.76.mixed_ref, bf16[1536,256]{1,0:T(8,128)(2,1)S(1)} %copy-done.15, bf16[1536,256]{1,0:T(8,128)(2,1)} %copy-done.2, ...), custom_call_target="tpu_custom_call" | custom-call | flops 16307453952 | bytes 9635840 | tf_op jit(solution)/shard_map/student_back/pallas_call | solution.py:74
  278.0 3.8 convolution_convert_fusion
  284.0 1.5 copy.67
  285.6 4.0 fusion.25
  289.6 2.2 copy-done.21
  294.9 5.8 %all-to-all-start = ((bf16[16,32,768]{2,1,0:T(8,128)(2,1)}), bf16[16,32,768]{2,1,0:T(8,128)(2,1)}, u32[]{:S(2)}, u32[]{:S(2)}) async-start(bf16[16,32,768]{2,1,0:T(8,128)(2,1)} %copy.69), calls=%async_computation | async-start | bytes 1572864 | tf_op jit(solution)/shard_map/all_to_all | solution.py:638
  300.7 2.2 slice_add_fusion
  307.1 143.8 %all-reduce.11.cloned.1.call-done = (bf16[3,768,192]{1,2,0:T(8,128)(2,1)}, bf16[192,768]{1,0:T(8,128)(2,1)}, bf16[768,768]{1,0:T(8,128)(2,1)}, bf16[768,768]{1,0:T(8,128)(2,1)}, bf16[192,1024]{1,0:T(8,128)(2,1)}) async-done(((bf16[3,768,192]{1,2,0:T(8,128)(2,1)}, bf16[192,768]{1,0:T(8,128)(2,1)}, bf16[768,768]{1,0:T(8,128)(2,1)}, bf16[768,768]{1,0:T(8,128)(2,1)}, bf16[192,1024]{1,0:T(8,128)(2,1)}), ...) | async-done | bytes 3932176 | tf_op jit(solution)/shard_map/psum | solution.py:733
  450.9 1.5 collective-permute-start.29
  452.6 2.4 slice.149.own_ref
  454.9 3.4 norm1_back.1
  460.3 1.6 collective-permute-done.29
  462.3 1.7 fusion.1
  464.9 35.3 %psum.42 = bf16[11,1024]{1,0:T(8,128)(2,1)S(1)} all-reduce(bf16[11,1024]{1,0:T(8,128)(2,1)S(1)} %fusion.8), channel_id=1, replica_groups=mesh['dp'=8,'mp'=4] {'dp'}, use_global_device_ids=true, to_apply=%region_4.5 | all-reduce | flops 11264 | bytes 45056 | tf_op jit(solution)/shard_map/psum | solution.py:733
  504.9 1.6 convert_element_type.131
  506.6 1.6 convert_element_type.134
  508.1 2.3 fusion
  (263 shorter events, 48.9 us)
Async XLA Ops:
  7.2 443.7 %all-reduce.11.cloned.1.call-start = ((), (), s32[]{:S(2)}) async-start(), calls=%async_computation.1 | async-start | bytes 7864320 | tf_op jit(solution)/shard_map/psum | solution.py:733
  7.2 82.7 %collective-permute-start.12 = (bf16[192,768]{1,0:T(8,128)(2,1)}, bf16[192,768]{1,0:T(8,128)(2,1)S(1)}, u32[]{:S(2)}, u32[]{:S(2)}) collective-permute-start(bf16[192,768]{1,0:T(8,128)(2,1)} %w0.3), channel_id=1, source_target_pairs={{0,2},{1,3},{2,0},{3,1},{4,6},{5,7},{6,4},{7,5},{8,10},{9,11},{10,... | collective-permute-start | bytes 884744 | tf_op jit(solution)/shard_map/ppermute | solution.py:478
  10.3 80.1 %collective-permute-start.11 = (bf16[192,768]{1,0:T(8,128)(2,1)}, bf16[192,768]{1,0:T(8,128)(2,1)S(1)}, u32[]{:S(2)}, u32[]{:S(2)}) collective-permute-start(bf16[192,768]{1,0:T(8,128)(2,1)} %w0.3), channel_id=1, source_target_pairs={{0,1},{1,0},{2,3},{3,2},{4,5},{5,4},{6,7},{7,6},{8,9},{9,8},{10,11... | collective-permute-start | bytes 884744 | tf_op jit(solution)/shard_map/ppermute | solution.py:478
  11.0 78.4 %collective-permute-start.6 = (bf16[1792]{0:T(1024)(128)(2,1)S(1)}, bf16[1792]{0:T(1024)(128)(2,1)S(1)}, u32[]{:S(2)}, u32[]{:S(2)}) collective-permute-start(bf16[1792]{0:T(1024)(128)(2,1)S(1)} %pad_maximum_fusion.3), channel_id=1, source_target_pairs={{0,1},{1,0},{2,3},{3,2},{4,5},{5,4},{6,7},{7,6},{8,9},{9,8},{10,11... | collective-permute-start | bytes 10760 | tf_op jit(solution)/shard_map/ppermute | solution.py:478
  11.5 83.8 %collective-permute-start.3 = (bf16[256,1024]{1,0:T(8,128)(2,1)}, bf16[256,1024]{1,0:T(8,128)(2,1)S(1)}, u32[]{:S(2)}, u32[]{:S(2)}) collective-permute-start(bf16[256,1024]{1,0:T(8,128)(2,1)} %w0.2), channel_id=1, source_target_pairs={{0,2},{1,3},{2,0},{3,1},{4,6},{5,7},{6,4},{7,5},{8,10},{9,11},{10,... | collective-permute-start | bytes 1572872 | tf_op jit(solution)/shard_map/ppermute | solution.py:478
  11.6 122.7 %collective-permute-start.5 = (bf16[1024,1024]{1,0:T(8,128)(2,1)}, bf16[1024,1024]{1,0:T(8,128)(2,1)}, u32[]{:S(2)}, u32[]{:S(2)}) collective-permute-start(bf16[1024,1024]{1,0:T(8,128)(2,1)} %f1a.3), channel_id=1, source_target_pairs={{0,1},{1,0},{2,3},{3,2},{4,5},{5,4},{6,7},{7,6},{8,9},{9,8},{10,11... | collective-permute-start | bytes 6291464 | tf_op jit(solution)/shard_map/ppermute | solution.py:478
  89.4 44.8 %collective-permute-start.7 = (bf16[1024,1024]{1,0:T(8,128)(2,1)S(1)}, bf16[1024,1024]{1,0:T(8,128)(2,1)}, u32[]{:S(2)}, u32[]{:S(2)}) collective-permute-start(bf16[1024,1024]{1,0:T(8,128)(2,1)S(1)} %copy-done.49), channel_id=1, source_target_pairs={{0,1},{1,0},{2,3},{3,2},{4,5},{5,4},{6,7},{7,6},{8,9},{9,8},{10,11... | collective-permute-start | bytes 6291464 | tf_op jit(solution)/shard_map/ppermute | solution.py:478
  90.0 5.0 collective-permute-start
  90.3 26.8 %copy-start.10 = (bf16[256,1024]{1,0:T(8,128)(2,1)S(1)}, bf16[256,1024]{1,0:T(8,128)(2,1)}, u32[]{:S(2)}) copy-start(bf16[256,1024]{1,0:T(8,128)(2,1)} %w0.2) | copy-start | bytes 1572868
  90.3 27.3 %copy-start.36 = (bf16[768]{0:T(1024)(128)(2,1)S(1)}, bf16[768]{0:T(1024)(128)(2,1)}, u32[]{:S(2)}) copy-start(bf16[768]{0:T(1024)(128)(2,1)} %param.57) | copy-start | bytes 4612
  90.3 27.3 %copy-start.35 = (bf16[1024]{0:T(1024)(128)(2,1)S(1)}, bf16[1024]{0:T(1024)(128)(2,1)}, u32[]{:S(2)}) copy-start(bf16[1024]{0:T(1024)(128)(2,1)} %param.45) | copy-start | bytes 6148
  90.3 27.3 %copy-start.44 = (bf16[768]{0:T(1024)(128)(2,1)S(1)}, bf16[768]{0:T(1024)(128)(2,1)}, u32[]{:S(2)}) copy-start(bf16[768]{0:T(1024)(128)(2,1)} %param.54) | copy-start | bytes 4612
  90.3 27.4 %copy-start.45 = (bf16[768]{0:T(1024)(128)(2,1)S(1)}, bf16[768]{0:T(1024)(128)(2,1)}, u32[]{:S(2)}) copy-start(bf16[768]{0:T(1024)(128)(2,1)} %param.53) | copy-start | bytes 4612
  90.3 27.4 %copy-start.46 = (bf16[768]{0:T(1024)(128)(2,1)S(1)}, bf16[768]{0:T(1024)(128)(2,1)}, u32[]{:S(2)}) copy-start(bf16[768]{0:T(1024)(128)(2,1)} %param.55) | copy-start | bytes 4612
  90.3 27.4 %copy-start.47 = (bf16[768]{0:T(1024)(128)(2,1)S(1)}, bf16[768]{0:T(1024)(128)(2,1)}, u32[]{:S(2)}) copy-start(bf16[768]{0:T(1024)(128)(2,1)} %param.59) | copy-start | bytes 4612
  90.4 27.4 %copy-start.39 = (bf16[1024]{0:T(1024)(128)(2,1)S(1)}, bf16[1024]{0:T(1024)(128)(2,1)}, u32[]{:S(2)}) copy-start(bf16[1024]{0:T(1024)(128)(2,1)} %param.41) | copy-start | bytes 6148
  90.4 27.4 %copy-start.40 = (bf16[1024]{0:T(1024)(128)(2,1)S(1)}, bf16[1024]{0:T(1024)(128)(2,1)}, u32[]{:S(2)}) copy-start(bf16[1024]{0:T(1024)(128)(2,1)} %param.42) | copy-start | bytes 6148
  90.4 27.4 %copy-start.41 = (bf16[1024]{0:T(1024)(128)(2,1)S(1)}, bf16[1024]{0:T(1024)(128)(2,1)}, u32[]{:S(2)}) copy-start(bf16[1024]{0:T(1024)(128)(2,1)} %param.43) | copy-start | bytes 6148
  90.4 27.4 %copy-start.42 = (bf16[1024]{0:T(1024)(128)(2,1)S(1)}, bf16[1024]{0:T(1024)(128)(2,1)}, u32[]{:S(2)}) copy-start(bf16[1024]{0:T(1024)(128)(2,1)} %param.47) | copy-start | bytes 6148
  90.4 28.0 %copy-start.6 = (bf16[192,768]{1,0:T(8,128)(2,1)S(1)}, bf16[192,768]{1,0:T(8,128)(2,1)}, u32[]{:S(2)}) copy-start(bf16[192,768]{1,0:T(8,128)(2,1)} %w0.3) | copy-start | bytes 884740
  90.4 4.4 collective-permute-start.9
  94.8 22.2 %collective-permute-start.14 = (bf16[768,768]{1,0:T(8,128)(2,1)S(1)}, bf16[768,768]{1,0:T(8,128)(2,1)S(1)}, u32[]{:S(2)}, u32[]{:S(2)}) collective-permute-start(bf16[768,768]{1,0:T(8,128)(2,1)S(1)} %copy-done.50), channel_id=1, source_target_pairs={{0,1},{1,0},{2,3},{3,2},{4,5},{5,4},{6,7},{7,6},{8,9},{9,8},{10,11... | collective-permute-start | bytes 3538952 | tf_op jit(solution)/shard_map/ppermute | solution.py:478
  94.9 22.2 %collective-permute-start.15 = (bf16[768,768]{1,0:T(8,128)(2,1)S(1)}, bf16[768,768]{1,0:T(8,128)(2,1)S(1)}, u32[]{:S(2)}, u32[]{:S(2)}) collective-permute-start(bf16[768,768]{1,0:T(8,128)(2,1)S(1)} %copy-done.51), channel_id=1, source_target_pairs={{0,1},{1,0},{2,3},{3,2},{4,5},{5,4},{6,7},{7,6},{8,9},{9,8},{10,11... | collective-permute-start | bytes 3538952 | tf_op jit(solution)/shard_map/ppermute | solution.py:478
  95.3 4.4 collective-permute-start.13
  99.8 15.5 %collective-permute-start.10 = (bf16[768,384]{1,0:T(8,128)(2,1)S(1)}, bf16[768,384]{1,0:T(8,128)(2,1)S(1)}, u32[]{:S(2)}, u32[]{:S(2)}) collective-permute-start(bf16[768,384]{1,0:T(8,128)(2,1)S(1)} %pad_maximum_fusion.2.near_ref), channel_id=1, source_target_pairs={{0,2},{1,3},{2,0},{3,1},{4,6},{5,7},{6,4},{7,5},{8,10},{9,11},{10,... | collective-permute-start | bytes 1769480 | tf_op jit(solution)/shard_map/ppermute | solution.py:478
  101.7 30.5 %copy-start.29 = (bf16[768,512]{1,0:T(8,128)(2,1)}, bf16[768,512]{1,0:T(8,128)(2,1)S(1)}, u32[]{:S(2)}) copy-start(bf16[768,512]{1,0:T(8,128)(2,1)S(1)} %pad_maximum_fusion.1.near_ref) | copy-start | bytes 2359300
  115.3 18.9 %collective-permute-start.1 = (bf16[768,512]{1,0:T(8,128)(2,1)S(1)}, bf16[768,512]{1,0:T(8,128)(2,1)S(1)}, u32[]{:S(2)}, u32[]{:S(2)}) collective-permute-start(bf16[768,512]{1,0:T(8,128)(2,1)S(1)} %pad_maximum_fusion.1.near_ref), channel_id=1, source_target_pairs={{0,2},{1,3},{2,0},{3,1},{4,6},{5,7},{6,4},{7,5},{8,10},{9,11},{10,... | collective-permute-start | bytes 2359304 | tf_op jit(solution)/shard_map/ppermute | solution.py:478
  117.0 15.2 %collective-permute-start.2 = (bf16[256,1024]{1,0:T(8,128)(2,1)S(1)}, bf16[256,1024]{1,0:T(8,128)(2,1)S(1)}, u32[]{:S(2)}, u32[]{:S(2)}) collective-permute-start(bf16[256,1024]{1,0:T(8,128)(2,1)S(1)} %copy-done.10), channel_id=1, source_target_pairs={{0,1},{1,0},{2,3},{3,2},{4,5},{5,4},{6,7},{7,6},{8,9},{9,8},{10,11... | collective-permute-start | bytes 1572872 | tf_op jit(solution)/shard_map/ppermute | solution.py:478
  117.1 15.5 %collective-permute-start.4 = (bf16[256,1024]{1,0:T(8,128)(2,1)S(1)}, bf16[256,1024]{1,0:T(8,128)(2,1)S(1)}, u32[]{:S(2)}, u32[]{:S(2)}) collective-permute-start(bf16[256,1024]{1,0:T(8,128)(2,1)S(1)} %collective-permute-done.3.w2), channel_id=1, source_target_pairs={{0,1},{1,0},{2,3},{3,2},{4,5},{5,4},{6,7},{7,6},{8,9},{9,8},{10,11... | collective-permute-start | bytes 1572872 | tf_op jit(solution)/shard_map/ppermute | solution.py:478
  132.2 21.8 %collective-permute-start.16 = (bf16[384,768]{1,0:T(8,128)(2,1)S(1)}, bf16[384,768]{1,0:T(8,128)(2,1)S(1)}, u32[]{:S(2)}, u32[]{:S(2)}) collective-permute-start(bf16[384,768]{1,0:T(8,128)(2,1)S(1)} %get-tuple-element.67), channel_id=1, source_target_pairs={{0,2},{1,3},{2,0},{3,1},{4,6},{5,7},{6,4},{7,5},{8,10},{9,11},{10,... | collective-permute-start | bytes 1769480 | tf_op jit(solution)/shard_map/ppermute | solution.py:478
  152.0 18.2 %collective-permute-start.8 = (bf16[384,1024]{1,0:T(8,128)(2,1)}, bf16[384,1024]{1,0:T(8,128)(2,1)S(1)}, u32[]{:S(2)}, u32[]{:S(2)}) collective-permute-start(bf16[384,1024]{1,0:T(8,128)(2,1)} %get-tuple-element.60), channel_id=1, source_target_pairs={{0,2},{1,3},{2,0},{3,1},{4,6},{5,7},{6,4},{7,5},{8,10},{9,11},{10,... | collective-permute-start | bytes 2359304 | tf_op jit(solution)/shard_map/ppermute | solution.py:478
  175.7 12.9 %collective-permute-start.17 = (bf16[384,768]{1,0:T(8,128)(2,1)S(1)}, bf16[384,768]{1,0:T(8,128)(2,1)S(1)}, u32[]{:S(2)}, u32[]{:S(2)}) collective-permute-start(bf16[384,768]{1,0:T(8,128)(2,1)S(1)} %get-tuple-element.68.d0.base_ref), channel_id=1, source_target_pairs={{0,2},{1,3},{2,0},{3,1},{4,6},{5,7},{6,4},{7,5},{8,10},{9,11},{10,... | collective-permute-start | bytes 1769480 | tf_op jit(solution)/shard_map/ppermute | solution.py:478
  179.6 31.3 %collective-permute-start.27 = (bf16[384,1024]{1,0:T(8,128)(2,1)}, bf16[384,1024]{1,0:T(8,128)(2,1)}, u32[]{:S(2)}, u32[]{:S(2)}) collective-permute-start(bf16[384,1024]{1,0:T(8,128)(2,1)} %dynamic-slice_convert_fusion), channel_id=1, source_target_pairs={{0,1},{1,0},{2,3},{3,2},{4,5},{5,4},{6,7},{7,6},{8,9},{9,8},{10,11... | collective-permute-start | bytes 2359304 | tf_op jit(solution)/shard_map/ppermute | solution.py:478
  205.9 12.2 %collective-permute-start.18 = (bf16[384,768]{1,0:T(8,128)(2,1)}, bf16[384,768]{1,0:T(8,128)(2,1)S(1)}, u32[]{:S(2)}, u32[]{:S(2)}) collective-permute-start(bf16[384,768]{1,0:T(8,128)(2,1)} %get-tuple-element.73), channel_id=1, source_target_pairs={{0,2},{1,3},{2,0},{3,1},{4,6},{5,7},{6,4},{7,5},{8,10},{9,11},{10,... | collective-permute-start | bytes 1769480 | tf_op jit(solution)/shard_map/ppermute | solution.py:478
  210.4 34.8 %collective-permute-start.25 = (bf16[768,768]{1,0:T(8,128)(2,1)}, bf16[768,768]{1,0:T(8,128)(2,1)}, u32[]{:S(2)}, u32[]{:S(2)}) collective-permute-start(bf16[768,768]{1,0:T(8,128)(2,1)} %get-tuple-element.89), channel_id=1, source_target_pairs={{0,1},{1,0},{2,3},{3,2},{4,5},{5,4},{6,7},{7,6},{8,9},{9,8},{10,11... | collective-permute-start | bytes 3538952 | tf_op jit(solution)/shard_map/ppermute | solution.py:478
  210.4 37.6 %collective-permute-start.26 = (bf16[768,768]{1,0:T(8,128)(2,1)}, bf16[768,768]{1,0:T(8,128)(2,1)}, u32[]{:S(2)}, u32[]{:S(2)}) collective-permute-start(bf16[768,768]{1,0:T(8,128)(2,1)} %get-tuple-element.91), channel_id=1, source_target_pairs={{0,1},{1,0},{2,3},{3,2},{4,5},{5,4},{6,7},{7,6},{8,9},{9,8},{10,11... | collective-permute-start | bytes 3538952 | tf_op jit(solution)/shard_map/ppermute | solution.py:478
  222.6 15.4 %collective-permute-start.19 = (bf16[384,768]{1,0:T(8,128)(2,1)S(1)}, bf16[384,768]{1,0:T(8,128)(2,1)}, u32[]{:S(2)}, u32[]{:S(2)}) collective-permute-start(bf16[384,768]{1,0:T(8,128)(2,1)S(1)} %get-tuple-element.75.base_ref), channel_id=1, source_target_pairs={{0,2},{1,3},{2,0},{3,1},{4,6},{5,7},{6,4},{7,5},{8,10},{9,11},{10,... | collective-permute-start | bytes 1769480 | tf_op jit(solution)/shard_map/ppermute | solution.py:478
  224.5 17.7 %collective-permute-start.28 = (bf16[192,1024]{1,0:T(8,128)(2,1)}, bf16[192,1024]{1,0:T(8,128)(2,1)}, u32[]{:S(2)}, u32[]{:S(2)}) collective-permute-start(bf16[192,1024]{1,0:T(8,128)(2,1)} %dynamic-slice_convert_fusion.1), channel_id=1, source_target_pairs={{0,2},{1,3},{2,0},{3,1},{4,6},{5,7},{6,4},{7,5},{8,10},{9,11},{10,... | collective-permute-start | bytes 1179656 | tf_op jit(solution)/shard_map/ppermute | solution.py:478
  239.1 11.5 %collective-permute-start.20 = (bf16[768,768]{1,0:T(8,128)(2,1)S(1)}, bf16[768,768]{1,0:T(8,128)(2,1)S(1)}, u32[]{:S(2)}, u32[]{:S(2)}) collective-permute-start(bf16[768,768]{1,0:T(8,128)(2,1)S(1)} %pad_maximum_fusion), channel_id=1, source_target_pairs={{0,1},{1,0},{2,3},{3,2},{4,5},{5,4},{6,7},{7,6},{8,9},{9,8},{10,11... | collective-permute-start | bytes 3538952 | tf_op jit(solution)/shard_map/ppermute | solution.py:478
  291.9 8.8 %collective-permute-start.21 = (bf16[768,768]{1,0:T(8,128)(2,1)S(1)}, bf16[768,768]{1,0:T(8,128)(2,1)}, u32[]{:S(2)}, u32[]{:S(2)}) collective-permute-start(bf16[768,768]{1,0:T(8,128)(2,1)S(1)} %slice.186), channel_id=1, source_target_pairs={{0,1},{1,0},{2,3},{3,2},{4,5},{5,4},{6,7},{7,6},{8,9},{9,8},{10,11... | collective-permute-start | bytes 3538952 | tf_op jit(solution)/shard_map/ppermute | solution.py:478
  294.9 167.5 %all-to-all-start = ((bf16[16,32,768]{2,1,0:T(8,128)(2,1)}), bf16[16,32,768]{2,1,0:T(8,128)(2,1)}, u32[]{:S(2)}, u32[]{:S(2)}) async-start(bf16[16,32,768]{2,1,0:T(8,128)(2,1)} %copy.69), calls=%async_computation | async-start | bytes 1572864 | tf_op jit(solution)/shard_map/all_to_all | solution.py:638
  304.4 150.5 %collective-permute-start.22 = (bf16[384,768]{1,0:T(8,128)(2,1)S(1)}, bf16[384,768]{1,0:T(8,128)(2,1)S(1)}, u32[]{:S(2)}, u32[]{:S(2)}) collective-permute-start(bf16[384,768]{1,0:T(8,128)(2,1)S(1)} %slice.187), channel_id=1, source_target_pairs={{0,2},{1,3},{2,0},{3,1},{4,6},{5,7},{6,4},{7,5},{8,10},{9,11},{10,... | collective-permute-start | bytes 1769480 | tf_op jit(solution)/shard_map/ppermute | solution.py:478
  450.9 11.0 %collective-permute-start.29 = (bf16[192,1024]{1,0:T(8,128)(2,1)}, bf16[192,1024]{1,0:T(8,128)(2,1)S(1)}, u32[]{:S(2)}, u32[]{:S(2)}) collective-permute-start(bf16[192,1024]{1,0:T(8,128)(2,1)} %get-tuple-element.176), channel_id=1, source_target_pairs={{0,2},{1,3},{2,0},{3,1},{4,6},{5,7},{6,4},{7,5},{8,10},{9,11},{10,... | collective-permute-start | bytes 1179656 | tf_op jit(solution)/shard_map/ppermute | solution.py:478
  458.3 1.3 collective-permute-start.23
  459.7 5.2 %collective-permute-start.24 = (f32[8,1024]{1,0:T(8,128)S(1)}, f32[8,1024]{1,0:T(8,128)S(1)}, u32[]{:S(2)}, u32[]{:S(2)}) collective-permute-start(f32[8,1024]{1,0:T(8,128)S(1)} %slice.151), channel_id=1, source_target_pairs={{0,2},{1,3},{2,0},{3,1},{4,6},{5,7},{6,4},{7,5},{8,10},{9,11},{10,... | collective-permute-start | bytes 98312 | tf_op jit(solution)/shard_map/ppermute | solution.py:478
  462.2 40.4 %copy-start.33 = (bf16[192,768]{1,0:T(8,128)(2,1)S(1)}, bf16[192,768]{1,0:T(8,128)(2,1)}, u32[]{:S(2)}) copy-start(bf16[192,768]{1,0:T(8,128)(2,1)} %get-tuple-element.173) | copy-start | bytes 884740
  462.2 45.9 %collective-permute-start.30 = (bf16[384,1024]{1,0:T(8,128)(2,1)S(1)}, bf16[384,1024]{1,0:T(8,128)(2,1)S(1)}, u32[]{:S(2)}, u32[]{:S(2)}) collective-permute-start(bf16[384,1024]{1,0:T(8,128)(2,1)S(1)} %maximum_select_fusion.1), channel_id=1, source_target_pairs={{0,1},{1,0},{2,3},{3,2},{4,5},{5,4},{6,7},{7,6},{8,9},{9,8},{10,11... | collective-permute-start | bytes 2359304 | tf_op jit(solution)/shard_map/ppermute | solution.py:478
  462.3 41.2 %copy-start.28 = (bf16[3,768,192]{1,2,0:T(8,128)(2,1)S(1)}, bf16[3,768,192]{1,2,0:T(8,128)(2,1)}, u32[]{:S(2)}) copy-start(bf16[3,768,192]{1,2,0:T(8,128)(2,1)} %get-tuple-element.172) | copy-start | bytes 2654212
  (43 other events, 243.1 us)
Sparse Core Ops, SparseCore 0:
  282.9 167.9 all-reduce.10

commit v2 on v1

--- a/solution.py
+++ b/solution.py
@@ -44,6 +44,10 @@
     return (u * gain_ref[...].astype(F32) + shift_ref[...].astype(F32)).astype(BF)
 
 
+def log2(size):
+    return size.bit_length() - 1
+
+
 def whole(shape):
     return pl.BlockSpec(shape, lambda *_: (0,) * len(shape))
 
@@ -96,16 +100,14 @@
     pieces, nb, piece, width = xk_ref.shape
     rows = pieces * nb * piece
 
-    def slot_of(lanes):
-        row = lax.broadcasted_iota(jnp.int32, (rows, lanes), 0)
-        part = row // (nb * piece)
-        inner = row % (nb * piece)
-        order = jnp.zeros((rows, lanes), jnp.int32)
-        for p in range(pieces):
-            order = jnp.where(part == p, sc[ORD + p], order)
-        return (j * nb + inner // piece) * block + order * piece + inner % piece
-
-    slot = slot_of(step)
+    line = lax.broadcasted_iota(jnp.int32, (rows, 1), 0)
+    part = line >> log2(nb * piece)
+    inner = line & (nb * piece - 1)
+    order = jnp.zeros((rows, 1), jnp.int32)
+    for p in range(pieces):
+        order = jnp.where(part == p, sc[ORD + p], order)
+    slot = (j * nb + (inner >> log2(piece))) * block + order * piece + (inner & (piece - 1))
+    group = group_of(slot, sc, CUM)
     acc[...] = jnp.zeros_like(acc)
 
     def one(t, _):
@@ -119,9 +121,8 @@
     xk_ref[...] = kept.astype(BF).reshape(xk_ref.shape)
     a = norm_low(kept, g_ref, s_ref)
     q = (dot_nn(a, w_ref[0]) + b_ref[0:1, :].astype(F32)).astype(BF)
-    slot128 = slot_of(128)
     lane = lax.broadcasted_iota(jnp.int32, (rows, 128), 1)
-    other = (lane != group_of(slot128, sc, CUM)) & (lane <= CLIPS)
+    other = (lane != group) & (lane <= CLIPS)
     mask = jnp.where(other, BIG, 0.0).astype(BF)
     pairs = q.shape[1] // 128
     out = []
@@ -136,12 +137,12 @@
 
     @pl.when(pl.program_id(0) == 0)
     def _():
-        token = lax.broadcasted_iota(jnp.int32, (keys, 128), 0)
+        token = lax.broadcasted_iota(jnp.int32, (keys, 1), 0)
         lane = lax.broadcasted_iota(jnp.int32, (keys, 128), 1)
         hot = jnp.where(lane == group_of(token, sc, END), 1.0, 0.0).astype(BF)
         for h in range(heads):
             pair = h // 2
-            mine = (lane // HD) == (h % 2)
+            mine = (lane >> 6) == (h % 2)
             k = k_ref[:, 128 * pair : 128 * (pair + 1)].astype(F32)
             v = v_ref[:, 128 * pair : 128 * (pair + 1)].astype(F32)
             kaug[h, :, :128] = jnp.where(mine, k * (HD**-0.5), 0.0).astype(BF)
@@ -171,10 +172,10 @@
     a = norm_low(x.astype(F32), g_ref, s_ref)
     a_ref[...] = a
     wide = q_ref.shape[1]
-    row = lax.broadcasted_iota(jnp.int32, (rows, wide), 0)
+    line = lax.broadcasted_iota(jnp.int32, (rows, 1), 0)
     lane = lax.broadcasted_iota(jnp.int32, (rows, wide), 1)
-    slot = (row // piece) * block + sc[ORD + pl.program_id(0)] * piece + row % piece
-    same = (lane - used) == group_of(slot, sc, CUM)
+    slot = (line >> log2(piece)) * block + sc[ORD + pl.program_id(0)] * piece + (line & (piece - 1))
+    same = lane == group_of(slot, sc, CUM) + used
     other = jnp.logical_not(same) & (lane >= used) & (lane <= used + CLIPS)
     q = (dot_nn(a, w_ref[0]) + b_ref[0:1, :].astype(F32)).astype(BF)
     q_ref[...] = jnp.where(other, BIG, q.astype(F32)).astype(BF)
@@ -211,7 +212,7 @@
         k = k_ref[...].astype(F32)
         v = v_ref[...].astype(F32)
         for h in range(heads):
-            mine = (lane // HD) == h
+            mine = (lane >> 6) == h
             kaug[h] = jnp.where(mine | (lane >= used), k, 0.0).astype(BF)
             vaug[h] = jnp.where(mine, v, 0.0).astype(BF)
 
@@ -232,23 +233,23 @@
     qb_ref[...] = put_three(q.astype(F32), lane, used, logs).astype(BF)
 
 
-def student_back_kernel(used, ds_ref, w_ref, mixed_ref, qb_ref, k_ref, v_ref, kt_ref, out_ref, sums_ref, kaug, vaug, dk, dv, dqs):
+def student_back_kernel(used, picked, ds_ref, w_ref, mixed_ref, qb_ref, k_ref, v_ref, kt_ref, out_ref, sums_ref, kaug, vaug, dk, dv, dqs):
     keys, wide = k_ref.shape
-    heads = used // HD
     j = pl.program_id(0)
     steps = pl.num_programs(0)
+    lo, size = HD * picked[0], HD * len(picked)
 
     @pl.when(j == 0)
     def _():
         lane = lax.broadcasted_iota(jnp.int32, (keys, wide), 1)
         k = k_ref[...].astype(F32)
         v = v_ref[...].astype(F32)
-        for h in range(heads):
-            mine = (lane // HD) == h
+        for i, h in enumerate(picked):
+            mine = (lane >> 6) == h
             ones = one_lanes(lane, used, h)
             keep = mine | ((lane >= used) & (lane <= used + CLIPS))
-            kaug[h] = jnp.where(ones, 1.0, jnp.where(keep, k, 0.0)).astype(BF)
-            vaug[h] = jnp.where(ones, 1.0, jnp.where(mine, v, 0.0)).astype(BF)
+            kaug[i] = jnp.where(ones, 1.0, jnp.where(keep, k, 0.0)).astype(BF)
+            vaug[i] = jnp.where(ones, 1.0, jnp.where(mine, v, 0.0)).astype(BF)
         dk[...] = jnp.zeros_like(dk)
         dv[...] = jnp.zeros_like(dv)
         dqs[...] = jnp.zeros_like(dqs)
@@ -259,30 +260,31 @@
     da = dot_nt(ds_ref[...], w_ref[...]).astype(BF).astype(F32)
     product = da * mixed_ref[...]
     deltas = [
-        jnp.sum(jnp.where((lane // HD) == h, product, 0.0), axis=1, keepdims=True)
-        for h in range(heads)
+        jnp.sum(jnp.where((lane >> 6) == h, product, 0.0), axis=1, keepdims=True)
+        if h in picked
+        else jnp.zeros((rows, 1), F32)
+        for h in range(used // HD)
     ]
     daug = put_three(da, lane, used, deltas).astype(BF)
     qf = qb.astype(F32)
     grads_q = []
-    for h in range(heads):
-        mine = (lane // HD) == h
-        pt = jnp.exp(dot_nt(kaug[h], qb))
-        dpt = dot_nt(vaug[h], daug)
+    for i, h in enumerate(picked):
+        mine = (lane >> 6) == h
+        pt = jnp.exp(dot_nt(kaug[i], qb))
+        dpt = dot_nt(vaug[i], daug)
         dst = (pt * dpt).astype(BF)
         dv[...] += dot_nn(pt.astype(BF), jnp.where(mine, da, 0.0).astype(BF))
         dk[...] += dot_nn(dst, jnp.where(mine, qf, 0.0).astype(BF))
         grads_q.append(dot_nn(kt_ref[HD * h : HD * (h + 1), :], dst))
-    grads_q.append(jnp.zeros((wide - used, rows), F32))
     dq = jnp.concatenate(grads_q, axis=0).T.astype(BF)
-    out_ref[pl.ds(pl.multiple_of(j * rows, rows), rows), 0:wide] = dq
+    out_ref[pl.ds(pl.multiple_of(j * rows, rows), rows), 0:size] = dq
     dqs[...] += jnp.sum(dq.astype(F32), axis=0, keepdims=True)
 
     @pl.when(j == steps - 1)
     def _():
-        out_ref[:, wide : 2 * wide] = (dk[...] * (HD**-0.5)).astype(BF)
-        low = dv[...].astype(BF)
-        out_ref[:, 2 * wide : 3 * wide] = low
+        out_ref[:, size : 2 * size] = (dk[:, lo : lo + size] * (HD**-0.5)).astype(BF)
+        low = dv[:, lo : lo + size].astype(BF)
+        out_ref[:, 2 * size : 3 * size] = low
         sums_ref[...] = jnp.concatenate(
             [dqs[...], jnp.sum(low.astype(F32), axis=0, keepdims=True)], axis=0
         )
@@ -293,55 +295,60 @@
     return pre * phi, phi + pre * (0.3989422804014327 * jnp.exp(-0.5 * pre * pre))
 
 
-def flipped(ref, lo, hi):
+def flipped(ref):
     half = ref.shape[0] // 2
-    return jnp.concatenate([ref[half:, lo:hi], ref[:half, lo:hi]], axis=0)
+    return jnp.concatenate([ref[half:], ref[:half]], axis=0)
 
 
 def forward_kernel(
-    student, half_steps,
-    near_ref, far_ref, w0, w1, w2, w3, x_ref, ob_ref, g_ref, s_ref,
+    mode, half_steps,
+    c0, c1, c2, c3, w0, w1, w2, w3, x_ref, ob_ref, g_ref, s_ref,
     f1a, f1b, b1a, b1b, f2a, f2b, b2_ref, *rest,
 ):
-    if student:
+    both = mode == "both"
+    if both:
         send_ref, own_ref, sent_ref, a2_ref, act_ref, slope_ref, a2, acc, base = rest
+    elif mode == "own":
+        own_ref, a2, acc, base = rest
     else:
-        send_ref, own_ref, a2, acc, base = rest
+        send_ref, a2, acc = rest
     j = pl.program_id(0)
     rows = x_ref.shape[0]
 
     @pl.when(j == 0)
     def _():
-        c = w0.shape[0]
+        far = (flipped(c2), flipped(c3)) if both else (c2[...], c3[...])
         parts = [
-            dot_nn(near_ref[:, :c], w0[...]),
-            dot_nn(near_ref[:, c : 2 * c], w1[...]),
-            dot_nn(flipped(far_ref, 0, c), w2[...]),
-            dot_nn(flipped(far_ref, c, 2 * c), w3[...]),
+            dot_nn(c0[...], w0[...]),
+            dot_nn(c1[...], w1[...]),
+            dot_nn(far[0], w2[...]),
+            dot_nn(far[1], w3[...]),
         ]
-        if not student:
+        if not both:
             parts = [p.astype(BF).astype(F32) for p in parts]
         resid = x_ref[...].astype(F32) + (parts[0] + parts[1] + parts[2] + parts[3])
         resid = resid + ob_ref[...].astype(F32)
-        if student:
+        if both:
             low = resid.astype(BF)
             sent_ref[...] = low
             resid = low.astype(F32)
         a2[...] = norm_low(resid, g_ref, s_ref)
-        if student:
+        if both:
             a2_ref[...] = a2[...]
-        base[...] = resid[: rows // 2] + b2_ref[...].astype(F32)
+            base[...] = resid[: rows // 2] + b2_ref[...].astype(F32)
+        elif mode == "own":
+            base[...] = resid + b2_ref[...].astype(F32)
         acc[...] = jnp.zeros_like(acc)
 
     def half(f1, b1, f2):
         pre = dot_nn(a2[...], f1[...]) + b1[...].astype(F32)
-        if student:
+        if both:
             act, slope = gelu_both(pre)
             slope_ref[...] = slope
         else:
             act = pre * (0.5 * (1.0 + lax.erf(pre * 0.7071067811865476)))
         act = act.astype(BF)
-        if student:
+        if both:
             act_ref[...] = act
         acc[...] += dot_nn(act, f2[...])
 
@@ -355,47 +362,58 @@
 
     @pl.when(j == 2 * half_steps - 1)
     def _():
-        own_ref[...] = acc[: rows // 2] + base[...]
-        send_ref[...] = acc[rows // 2 :].astype(BF)
-
-
-def forward(student, near, far, w_out, x, out_b, gain, shift, f1, b1, f2, b2, chunk):
-    rows, width = near.shape[0], x.shape[1]
-    hidden = f1[0].shape[1]
+        if both:
+            own_ref[...] = acc[: rows // 2] + base[...]
+            send_ref[...] = acc[rows // 2 :].astype(BF)
+        elif mode == "own":
+            own_ref[...] = acc[...] + base[...]
+        else:
+            send_ref[...] = acc[...].astype(BF)
+
+
+def forward(mode, name, rows, ctx, w_out, x, out_b, gain, shift, f1, b1, f2, b2, chunk):
+    width = x.shape[1]
+    heads_wide, hidden = w_out[0].shape[0], f1[0].shape[1]
     n = hidden // chunk
+    both = mode == "both"
+    near_at = 1 if mode == "send" else 0
+    far_at = 1 if mode == "own" else 0
     first = lambda j: jnp.minimum(j, n - 1)
     second = lambda j: jnp.maximum(j - n, 0)
-    specs = [whole(near.shape), whole(far.shape)] + [whole(w.shape) for w in w_out]
-    specs += [pl.BlockSpec((rows, width), lambda j: (0, 0))] + [whole((1, width))] * 3
+    at = lambda i, w: pl.BlockSpec((rows, w), lambda j: (i, 0))
+    specs = [at(near_at, heads_wide)] * 2 + [at(far_at, heads_wide)] * 2
+    specs += [whole(w.shape) for w in w_out]
+    specs += [at(near_at, width)] + [whole((1, width))] * 3
     specs += [pl.BlockSpec((width, chunk), lambda j, f=f: (0, f(j))) for f in (first, second)]
     specs += [pl.BlockSpec((1, chunk), lambda j, f=f: (0, f(j))) for f in (first, second)]
     specs += [pl.BlockSpec((chunk, width), lambda j, f=f: (f(j), 0)) for f in (first, second)]
     specs += [whole((1, width))]
     half = rows // 2
-    outs = [sds((half, width), BF), sds((half, width), F32)]
-    out_specs = [whole((half, width))] * 2
-    if student:
-        outs += [sds((rows, width), BF)] * 2 + [sds((rows, 2 * hidden), BF), sds((rows, 2 * hidden), F32)]
-        out_specs += [whole((rows, width))] * 2 + [pl.BlockSpec((rows, chunk), lambda j: (0, j))] * 2
+    scratch = [pltpu.VMEM((rows, width), BF), pltpu.VMEM((rows, width), F32)]
+    if both:
+        outs = [sds((half, width), BF), sds((half, width), F32)] + [sds((rows, width), BF)] * 2
+        outs += [sds((rows, 2 * hidden), BF), sds((rows, 2 * hidden), F32)]
+        out_specs = [whole((half, width))] * 2 + [whole((rows, width))] * 2
+        out_specs += [pl.BlockSpec((rows, chunk), lambda j: (0, j))] * 2
+        scratch += [pltpu.VMEM((half, width), F32)]
+    elif mode == "own":
+        outs, out_specs = sds((rows, width), F32), whole((rows, width))
+        scratch += [pltpu.VMEM((rows, width), F32)]
+    else:
+        outs, out_specs = sds((rows, width), BF), whole((rows, width))
     return call(
-        functools.partial(forward_kernel, student, n),
-        "student_forward" if student else "teacher_forward",
-        (2 * n,),
-        specs,
-        out_specs,
-        outs,
-        (near, far, *w_out, x, out_b, gain, shift, *f1, *b1, *f2, b2),
-        scratch=[pltpu.VMEM((rows, width), BF), pltpu.VMEM((rows, width), F32), pltpu.VMEM((half, width), F32)],
-        flops=2 * rows * width * (4 * w_out[0].shape[0] + 4 * hidden),
-    )
-
-
-def head_kernel(block, sc, own_ref, recv_ref, out_ref, w_ref, b_ref, inv_ref, dg_ref, do_ref, loss_ref, hb_ref, ob_ref):
+        functools.partial(forward_kernel, mode, n), name, (2 * n,), specs, out_specs, outs,
+        (*ctx, *w_out, x, out_b, gain, shift, *f1, *b1, *f2, b2),
+        scratch=scratch,
+        flops=2 * rows * width * (4 * heads_wide + 4 * hidden),
+    )
+
+
+def head_kernel(block, piece, sc, own_ref, recv_ref, out_ref, w_ref, b_ref, inv_ref, dg_ref, do_ref, loss_ref, hb_ref, ob_ref):
     rows, width = own_ref.shape
     target = (own_ref[...] + recv_ref[...].astype(F32)).astype(BF).astype(F32)
-    row = lax.broadcasted_iota(jnp.int32, (rows, 1), 0)
-    piece = block // 4
-    slot = (row // piece) * block + sc[ORD] * piece + row % piece
+    line = lax.broadcasted_iota(jnp.int32, (rows, 1), 0)
+    slot = (line >> log2(piece)) * block + sc[ORD] * piece + (line & (piece - 1))
     live = slot < sc[CUM + CLIPS - 1]
     group = group_of(slot, sc, CUM)
     weight = jnp.zeros((rows, 1), F32)
@@ -413,34 +431,27 @@
     ob_ref[...] = jnp.sum(do.astype(F32), axis=0, keepdims=True)
 
 
-def feed_back_kernel(d0, d1, act_ref, slope_ref, a2_ref, f1a, f1b, f2a, f2b,
-                     g1_ref, g1s_ref, g2_ref, g2s_ref, own_ref, send_ref, gb_ref, d, acc):
-    j = pl.program_id(0)
+def feed_back_kernel(d0, d1, act_ref, slope_ref, a2_ref, f1, f2, *rest):
+    last = len(rest) == 7
+    if last:
+        before, g1_ref, g2_ref, gb_ref, own_ref, send_ref, d = rest
+    else:
+        g1_ref, g2_ref, gb_ref, acc_ref, d = rest
     half = d0.shape[0]
-
-    @pl.when(j == 0)
-    def _():
-        d[:half] = d0[...]
-        d[half:] = d1[...]
-        acc[...] = jnp.zeros_like(acc)
-
-    def part(f1, f2, g1, g2):
-        grad = d[...]
-        dpre = (dot_nt(grad, f2[...]) * slope_ref[...]).astype(BF)
-        gb_ref[...] = jnp.sum(dpre.astype(F32), axis=0, keepdims=True)
-        acc[...] += dot_nt(dpre, f1[...])
-        g2[...] = dot_tn(act_ref[...], grad).astype(g2.dtype)
-        g1[...] = dot_tn(a2_ref[...], dpre).astype(g1.dtype)
-
-    @pl.when(j == 0)
-    def _():
-        part(f1a, f2a, g1_ref, g2_ref)
-
-    @pl.when(j == 1)
-    def _():
-        part(f1b, f2b, g1s_ref, g2s_ref)
-        own_ref[...] = acc[:half]
-        send_ref[...] = acc[half:].astype(BF)
+    d[:half] = d0[...]
+    d[half:] = d1[...]
+    grad = d[...]
+    dpre = (dot_nt(grad, f2[...]) * slope_ref[...]).astype(BF)
+    gb_ref[...] = jnp.sum(dpre.astype(F32), axis=0, keepdims=True)
+    part = dot_nt(dpre, f1[...])
+    if last:
+        part += before[...]
+        own_ref[...] = part[:half]
+        send_ref[...] = part[half:].astype(BF)
+    else:
+        acc_ref[...] = part
+    g2_ref[...] = dot_tn(act_ref[...], grad).astype(g2_ref.dtype)
+    g1_ref[...] = dot_tn(a2_ref[...], dpre).astype(g1_ref.dtype)
 
 
 def norm_back_kernel(own_ref, recv_ref, base_ref, x_ref, g_ref, dx_ref, sums_ref):
@@ -545,10 +556,8 @@
     s_f1 = (s_fc1, core(s_fc1))
     s_f2 = (s_fc2, core(s_fc2))
     biases = core(jnp.concatenate([t_fc1_bias, s_fc1_bias]))
-    t_b1 = (row(t_fc1_bias), row(biases[: t_fc1_bias.shape[0]]))
-    s_b1 = (row(s_fc1_bias), row(biases[t_fc1_bias.shape[0] :]))
-    t_w = (t_out, core(t_out), t_w2, core(t_w2))
-    s_w = (s_out, core(s_out), s_w2, core(s_w2))
+    t_w1 = core(t_out)
+    s_w1 = core(s_out)
 
     w_pad = jnp.pad(s_qkv, ((0, 0), (0, 0), (0, wide - used)))
     b_pad = jnp.pad(s_qv_bias, ((0, 0), (0, wide - used)))
@@ -577,8 +586,17 @@
         scratch=[pltpu.VMEM((heads, rows, wide), BF)] * 2,
         flops=heads * rows * rows * wide * 4,
     )
-    s_near = jnp.concatenate([ctx[:near], core(ctx[near:])], axis=1)
-    s_far = across(s_near)
+
+    ctx, teacher_rows, t_w2, s_w2, t_f1, t_f2, s_f1, s_f2, t_w1, s_w1, biases = lax.optimization_barrier(
+        (ctx, teacher_in, t_w2, s_w2, t_f1, t_f2, s_f1, s_f2, t_w1, s_w1, biases)
+    )
+    t_b1 = (row(t_fc1_bias), row(biases[: t_fc1_bias.shape[0]]))
+    s_b1 = (row(s_fc1_bias), row(biases[t_fc1_bias.shape[0] :]))
+    s_c0 = ctx[:near]
+    s_c1 = core(ctx[near:])
+    s_c2 = across(s_c0)
+    t_w3 = core(t_w2)
+    s_w3 = core(s_w2)
 
     by_512 = lambda w: pl.BlockSpec((512, w), lambda j: (j, 0))
     cols = t_qkv.shape[2]
@@ -587,9 +605,11 @@
         [by_512(t_width), whole((1, t_width)), whole((1, t_width)), whole(t_qkv.shape), whole(t_qv_bias.shape)],
         [by_512(cols)] * 2,
         [sds((tokens, cols), BF)] * 2,
-        (teacher_in, row(t_norm1_gain), row(t_norm1_shift), t_qkv, t_qv_bias),
+        (teacher_rows, row(t_norm1_gain), row(t_norm1_shift), t_qkv, t_qv_bias),
         flops=2 * tokens * t_width * 2 * cols,
     )
+    tk, teacher_rows, s_c1, t_w3, s_w3 = lax.optimization_barrier((tk, teacher_rows, s_c1, t_w3, s_w3))
+    s_c3 = across(s_c1)
     by_slot = lambda w: pl.BlockSpec((mp, nb, piece, w), lambda j, sc: (0, j, 0, 0))
     x_kept, tq = call(
         functools.partial(teacher_q_kernel, slots, block, span), "teacher_q", (steps,),
@@ -599,7 +619,7 @@
         ],
         [by_slot(t_width), by_slot(2 * cols)],
         [sds((mp, slots, piece, t_width), BF), sds((mp, slots, piece, 2 * cols), BF)],
-        (teacher_in, rank, row(t_norm1_gain), row(t_norm1_shift), t_qkv, t_qv_bias),
+        (teacher_rows, rank, row(t_norm1_gain), row(t_norm1_shift), t_qkv, t_qv_bias),
         scratch=[pltpu.VMEM((span, t_width), F32)],
         flops=2 * rows * t_width * (cols + 512), scalars=scalars,
     )
@@ -612,20 +632,28 @@
         scratch=[pltpu.VMEM((cols // HD, tokens, 256), BF), pltpu.VMEM((cols // HD, tokens, 128), BF)],
         flops=(cols // HD) * rows * tokens * (512 + 256), scalars=scalars,
     ).reshape(rows, cols)
-    t_near = jnp.concatenate([t_ctx[:near], core(t_ctx[near:])], axis=1)
-    t_far = across(t_near)
-
+
+    t_ctx, s_c2, s_c3 = lax.optimization_barrier((t_ctx, s_c2, s_c3))
+    t_c0 = t_ctx[:near]
+    t_c2 = across(t_c0)
+    t_c1 = core(t_ctx[near:])
+    t_c3 = across(t_c1)
     s_send, s_own, sent, a2, act, slope = forward(
-        True, s_near, s_far, s_w, x_stud, row(s_out_bias), row(s_norm2_gain), row(s_norm2_shift),
-        s_f1, s_b1, s_f2, row(s_fc2_bias), s_fc1.shape[1],
-    )
-    out_rows = (s_own + across(s_send).astype(F32)).astype(BF)
-
-    t_send, t_own = forward(
-        False, t_near, t_far, t_w, x_kept.reshape(rows, t_width), row(t_out_bias), row(t_norm2_gain),
-        row(t_norm2_shift), t_f1, t_b1, t_f2, row(t_fc2_bias), 512,
-    )
+        "both", "student_forward", near, (s_c0, s_c1, s_c2, s_c3), (s_out, s_w1, s_w2, s_w3), x_stud,
+        row(s_out_bias), row(s_norm2_gain), row(s_norm2_shift), s_f1, s_b1, s_f2, row(s_fc2_bias), s_fc1.shape[1],
+    )
+    s_send, t_c2, t_c3 = lax.optimization_barrier((s_send, t_c2, t_c3))
+    s_recv = across(s_send)
+    t_args = (
+        (t_ctx, t_c1, t_c2, t_c3), (t_out, t_w1, t_w2, t_w3), x_kept.reshape(rows, t_width), row(t_out_bias),
+        row(t_norm2_gain), row(t_norm2_shift), t_f1, t_b1, t_f2, row(t_fc2_bias),
+    )
+    t_send = forward("send", "teacher_forward_far", mine, *t_args, 512)
+    s_recv, t_args, t_send = lax.optimization_barrier((s_recv, t_args, t_send))
     t_recv = across(t_send)
+    t_own = forward("own", "teacher_forward_own", mine, *t_args, 512)
+    t_own, t_recv = lax.optimization_barrier((t_own, t_recv))
+    out_rows = (s_own + s_recv.astype(F32)).astype(BF)
 
     owners = lax.dynamic_index_in_dim(block_owner, home, 0, keepdims=False)
     capacity = (slots + homes - 1) // homes
@@ -643,12 +671,9 @@
     lane = jnp.arange(capacity, dtype=jnp.int32)
     target_slot = jnp.where(lane[None, :] < per_source[:, None], before[:, None] + lane[None, :], OWN).reshape(-1)
     choose = (jnp.arange(OWN, dtype=jnp.int32)[:, None] == target_slot[None, :]).astype(BF)
-    student_out = jnp.dot(
-        choose, inbound.reshape(homes * capacity, piece * width), preferred_element_type=BF
-    ).reshape(OWN, piece, width)
 
     d_guess, d_out, loss_row, head_b_row, fc2_b_row = call(
-        functools.partial(head_kernel, block), "head", (1,),
+        functools.partial(head_kernel, block, piece), "head", (1,),
         [
             whole((mine, t_width)), whole((mine, t_width)), whole((mine, width)), whole((width, t_width)),
             whole((1, t_width)), pl.BlockSpec(memory_space=pltpu.SMEM),
@@ -660,78 +685,171 @@
     )
     d_out_far = across(d_out)
     g_head = dot_tn(out_rows, d_guess)
-
-    hidden = s_fc1.shape[1]
-    cut = pl.BlockSpec((near, hidden), lambda j: (0, j))
-    g1, g1_send, g2, g2_send, da2_own, da2_send, b1_row = call(
-        feed_back_kernel, "feed_back", (2,),
-        [whole((mine, width))] * 2 + [cut, cut, whole((near, width))]
-        + [whole((width, hidden))] * 2 + [whole((hidden, width))] * 2,
-        [whole((width, hidden))] * 2 + [whole((hidden, width))] * 2 + [whole((mine, width))] * 2
-        + [pl.BlockSpec((1, hidden), lambda j: (0, j))],
-        [
-            sds((width, hidden), F32), sds((width, hidden), BF), sds((hidden, width), F32), sds((hidden, width), BF),
-            sds((mine, width), F32), sds((mine, width), BF), sds((1, 2 * hidden), F32),
-        ],
-        (d_out, d_out_far, act, slope, a2, *s_f1, *s_f2),
-        scratch=[pltpu.VMEM((near, width), BF), pltpu.VMEM((near, width), F32)],
-        flops=2 * near * width * hidden * 8,
-    )
-    da2_far = across(da2_send)
-    d_sent, sums2 = norm_back("norm2_back", da2_own, da2_far, d_out, sent[:mine], row(s_norm2_gain), BF)
-
     side = me % 2
     level = me // 2
     half_rows = width // 2
     quarter = width // 4
-    low_head = g_head.astype(BF)
-    head_send = lax.dynamic_slice_in_dim(low_head, (1 - side) * half_rows, half_rows, 0)
-    head_half = lax.dynamic_slice_in_dim(g_head, side * half_rows, half_rows, 0) + core(head_send).astype(F32)
-    low_half = head_half.astype(BF)
-    head_send2 = lax.dynamic_slice_in_dim(low_half, (1 - level) * quarter, quarter, 0)
-    head_quarter = lax.dynamic_slice_in_dim(head_half, level * quarter, quarter, 0) + across(head_send2).astype(F32)
-
-    g2_sum = (g2 + core(g2_send).astype(F32)).astype(BF)
-    g1_sum = (g1 + core(g1_send).astype(F32)).astype(BF)
-    head_all = lax.psum(head_quarter.astype(BF), "dp")
-    g2_all = lax.psum(g2_sum, "dp")
-    g1_all = lax.psum(g1_sum, "dp")
-
+    head_send = lax.dynamic_slice_in_dim(g_head, (1 - side) * half_rows, half_rows, 0).astype(BF)
+    head_recv = core(head_send)
+    d_out_far, inbound, head_recv = lax.optimization_barrier((d_out_far, inbound, head_recv))
+    student_out = jnp.dot(
+        choose, inbound.reshape(homes * capacity, piece * width), preferred_element_type=BF
+    ).reshape(OWN, piece, width)
+
+    hidden = s_fc1.shape[1]
+    cut = lambda i: pl.BlockSpec((near, hidden), lambda j: (0, i))
+    square, line = whole((width, hidden)), whole((1, hidden))
+    feed_specs = lambda i: [whole((mine, width))] * 2 + [cut(i), cut(i), whole((near, width)), square, whole((hidden, width))]
+    feed_flops = 2 * near * width * hidden * 4
+    g1_send, g2_send, b1_send, da2_part = call(
+        feed_back_kernel, "feed_back_far", (1,), feed_specs(1),
+        [square, whole((hidden, width)), line, whole((near, width))],
+        [sds((width, hidden), BF), sds((hidden, width), BF), sds((1, hidden), F32), sds((near, width), F32)],
+        (d_out, d_out_far, act, slope, a2, s_f1[1], s_f2[1]),
+        scratch=[pltpu.VMEM((near, width), BF)], flops=feed_flops,
+    )
+    g1_recv, g2_recv = core(g1_send), core(g2_send)
+    g1, g2, b1_own, da2_own, da2_send = call(
+        feed_back_kernel, "feed_back_own", (1,), feed_specs(0) + [whole((near, width))],
+        [square, whole((hidden, width)), line, whole((mine, width)), whole((mine, width))],
+        [
+            sds((width, hidden), F32), sds((hidden, width), F32), sds((1, hidden), F32),
+            sds((mine, width), F32), sds((mine, width), BF),
+        ],
+        (d_out, d_out_far, act, slope, a2, s_f1[0], s_f2[0], da2_part),
+        scratch=[pltpu.VMEM((near, width), BF)], flops=feed_flops,
+    )
+
+    head_half = lax.dynamic_slice_in_dim(g_head, side * half_rows, half_rows, 0) + head_recv.astype(F32)
+    head_send2 = lax.dynamic_slice_in_dim(head_half, (1 - level) * quarter, quarter, 0).astype(BF)
+    head_own = lax.dynamic_slice_in_dim(head_half, level * quarter, quarter, 0)
+    head_recv2 = across(head_send2)
+    g1_recv, g2_recv, head_recv2, g1, g2, da2_own, da2_send = lax.optimization_barrier(
+        (g1_recv, g2_recv, head_recv2, g1, g2, da2_own, da2_send)
+    )
+    da2_far = across(da2_send)
+
+    bits = log2(homes)
+    x_first = list(range(bits))
+    z_first = x_first[1:] + x_first[:1]
+
+    def partner(value, bit):
+        return lax.ppermute(value, "dp", [(i, i ^ (1 << bit)) for i in range(homes)])
+
+    def cut_half(value, bit):
+        size = value.shape[0] // 2
+        mark = (home >> bit) & 1
+        send = lax.dynamic_slice_in_dim(value, (1 - mark) * size, size, 0).astype(BF)
+        keep = lax.dynamic_slice_in_dim(value, mark * size, size, 0)
+        return keep, partner(send, bit)
+
+    def join_half(value, other, bit):
+        mark = (home >> bit) & 1
+        return jnp.where(
+            mark == 0, jnp.concatenate([value, other], axis=0), jnp.concatenate([other, value], axis=0)
+        )
+
+    def add(pair):
+        return (pair[0].astype(F32) + pair[1].astype(F32)).astype(BF)
+
+    head_quarter = (head_own + head_recv2.astype(F32)).reshape(-1, width)
+    head_rows = head_quarter.shape[0]
+    one = (jnp.concatenate([g1 + g1_recv.astype(F32), head_quarter], axis=0)).astype(BF)
+    two = (g2 + g2_recv.astype(F32)).astype(BF)
+
+    def halve(values, orders, step):
+        return [cut_half(v, o[step]) for v, o in zip(values, orders)]
+
+    def double(values, orders, step):
+        return [partner(v, o[step]) for v, o in zip(values, orders)]
+
+    def join(values, others, orders, step):
+        return [join_half(v, w, o[step]) for v, w, o in zip(values, others, orders)]
+
+    orders = (x_first, z_first)
+    sums = [one, two]
+    flight = halve(sums, orders, 0)
+
+    d_sent, sums2 = norm_back("norm2_back", da2_own, da2_far, d_out, sent[:mine], row(s_norm2_gain), BF)
     ds_near = jnp.concatenate([d_sent, across(d_sent)], axis=0)
     ds = jnp.concatenate([ds_near, core(ds_near)], axis=0)
+    ds, flight = lax.optimization_barrier((ds, flight))
+    sums = [add(p) for p in flight]
+    flight = halve(sums, orders, 1)
     so_pad = jnp.pad(s_out, ((0, wide - used), (0, 0)))
     k_turned = sk[:, :used].T
-    d_qkv, qv_sums = call(
-        functools.partial(student_back_kernel, used), "student_back", (rows // qrows,),
-        [
-            by_rows(width), whole((wide, width)), by_rows(wide), by_rows(wide), whole((rows, wide)),
-            whole((rows, wide)), whole((used, rows)),
-        ],
-        [whole((rows, 3 * wide)), whole((2, wide))],
-        [sds((rows, 3 * wide), BF), sds((2, wide), F32)],
-        (ds, so_pad, mixed, qb, sk, sv, k_turned),
-        scratch=[pltpu.VMEM((heads, rows, wide), BF)] * 2 + [pltpu.VMEM((rows, wide), F32)] * 2
-        + [pltpu.VMEM((1, wide), F32)],
-        flops=heads * rows * rows * wide * 9,
-    )
+
+    def back(name, picked):
+        size = HD * len(picked)
+        return call(
+            functools.partial(student_back_kernel, used, picked), name, (rows // qrows,),
+            [
+                by_rows(width), whole((wide, width)), by_rows(wide), by_rows(wide), whole((rows, wide)),
+                whole((rows, wide)), whole((used, rows)),
+            ],
+            [whole((rows, 3 * size)), whole((2, size))],
+            [sds((rows, 3 * size), BF), sds((2, size), F32)],
+            (ds, so_pad, mixed, qb, sk, sv, k_turned),
+            scratch=[pltpu.VMEM((len(picked), rows, wide), BF)] * 2 + [pltpu.VMEM((rows, wide), F32)] * 2
+            + [pltpu.VMEM((1, size), F32)],
+            flops=len(picked) * rows * rows * wide * 9,
+        )
+
+    pair, odd = tuple(range(heads - 1)), (heads - 1,)
+    d_pair, pair_sums = back("student_back_pair", pair)
     g_out = dot_tn(ctx, ds)
-    w_line = jnp.transpose(w_pad, (0, 2, 1)).reshape(3 * wide, width)
-    da1 = dot_nn(d_qkv, w_line)
-    da1_near = da1[:near] + core(da1[near:].astype(BF)).astype(F32)
+    d_pair, ds, flight = lax.optimization_barrier((d_pair, ds, flight))
+    sums = [add(p) for p in flight]
+    for step in range(2, bits):
+        flight = halve(sums, orders, step)
+        if step < bits - 1:
+            sums = [add(p) for p in flight]
+    d_odd, odd_sums = back("student_back_odd", odd)
+    d_odd, flight = lax.optimization_barrier((d_odd, flight))
+    sums = [add(p) for p in flight]
+    flight = double(sums, orders, bits - 1)
+
+    mixed_size = HD * (heads - 1)
+    w_turn = jnp.transpose(s_qkv, (0, 2, 1))
+    w_pair = w_turn[:, :mixed_size].reshape(3 * mixed_size, width)
+    w_odd = w_turn[:, mixed_size:].reshape(3 * HD, width)
+    da1 = dot_nn(d_pair, w_pair) + dot_nn(d_odd, w_odd)
+    da1_recv = core(da1[near:].astype(BF))
+    g_pair = dot_tn(d_pair, a_stud).astype(BF)
+    g_odd = dot_tn(d_odd, a_stud).astype(BF)
+    last = [g_pair, jnp.concatenate([g_odd, g_out.astype(BF)], axis=0)]
+    last, da1_recv, flight = lax.optimization_barrier((last, da1_recv, flight))
+    last_flight = halve(last, orders, 0)
+    da1_near = da1[:near] + da1_recv.astype(F32)
     da1_far = across(da1_near[mine:].astype(BF))
-    g_qkv = dot_tn(a_stud, d_qkv).reshape(width, 3, wide)[:, :, :used]
+    sums = join(sums, flight, orders, bits - 1)
+    for step in range(bits - 2, 0, -1):
+        flight = double(sums, orders, step)
+        sums = join(sums, flight, orders, step)
     grad_in, sums1 = norm_back("norm1_back", da1_near[:mine], da1_far, d_sent, x_stud[:mine], row(s_norm1_gain), F32)
-
-    fit = lambda v: jnp.pad(v, ((0, 0), (0, t_width - v.shape[1])))
+    last = [add(p) for p in last_flight]
+
+    fit = lambda v: jnp.pad(v, ((0, 0), (0, width - v.shape[1])))
+    loss_fit = jnp.sum(loss_row.reshape(-1, t_width // 4), axis=0, keepdims=True)
     short = jnp.concatenate(
-        [fit(sums1[:2]), fit(sums2), fit(fc2_b_row), head_b_row, loss_row, fit(b1_row[:, hidden:])], axis=0
-    )
-    short_in = core(short)
-    short_own = jnp.concatenate([short[:8], fit(b1_row[:, :hidden])], axis=0) + short_in
-    short_sum = short_own[:8] + across(short_own[:8])
-    short_dp = jnp.concatenate([short_sum, short_own[8:], fit(qv_sums)], axis=0)
-    qkv_all, out_all, short_all = lax.psum((g_qkv.astype(BF), g_out.astype(BF), short_dp.astype(BF)), "dp")
-
+        [sums1[:2], sums2, fc2_b_row, head_b_row[:, :width], fit(head_b_row[:, width:]), fit(loss_fit), b1_send],
+        axis=0,
+    )
+    short_own = jnp.concatenate([short[:9], b1_own], axis=0) + core(short)
+    short_sum = short_own[:9] + across(short_own[:9])
+    qv = jnp.concatenate([pair_sums, odd_sums], axis=1)
+    short_all = jnp.concatenate([short_sum, short_own[9:], fit(qv), jnp.zeros((4, width), F32)], axis=0)
+
+    flight = double(sums, orders, 0)
+    for step in range(1, bits):
+        last = [add(p) for p in halve(last, orders, step)]
+        short_all = short_all + partner(short_all, step - 1)
+    short_all = short_all + partner(short_all, bits - 1)
+    for step in range(bits - 1, -1, -1):
+        last = join(last, double(last, orders, step), orders, step)
+    sums = join(sums, flight, orders, 0)
+
+    g1_all, head_all = sums[0][:width], sums[0][width:].reshape(quarter, t_width)
     head_other = across(head_all)
     head_pair = jnp.where(
         level == 0,
@@ -744,25 +862,28 @@
         jnp.concatenate([head_pair, head_peer], axis=0),
         jnp.concatenate([head_peer, head_pair], axis=0),
     ).astype(F32)
-    vec = short_all.astype(F32)
+    vec = short_all
+    qkv_turned = jnp.concatenate(
+        [last[0].reshape(3, mixed_size, width), last[1][: 3 * HD].reshape(3, HD, width)], axis=1
+    )
     return (
-        jnp.sum(vec[7]),
+        jnp.sum(vec[8]),
         student_out,
         grad_in.reshape(slots, piece, width),
-        vec[0, :width],
-        vec[1, :width],
-        jnp.transpose(qkv_all.astype(F32), (1, 0, 2)),
-        vec[9:11, :used],
-        out_all.astype(F32),
-        vec[4, :width],
-        vec[2, :width],
-        vec[3, :width],
+        vec[0],
+        vec[1],
+        jnp.transpose(qkv_turned, (0, 2, 1)).astype(F32),
+        vec[10:12, :used],
+        last[1][3 * HD :].astype(F32),
+        vec[4],
+        vec[2],
+        vec[3],
         g1_all.astype(F32),
-        vec[8, :hidden],
-        g2_all.astype(F32),
-        vec[5, :width],
+        vec[9],
+        sums[1].astype(F32),
+        vec[5],
         grad_head,
-        vec[6, :t_width],
+        jnp.concatenate([vec[6], vec[7, : t_width - width]]),
     )
 
 

time: 528 us -> 426 us (0.81)
  waiting for transfers between devices: 215 us -> 104 us
  starting transfers between devices: 27 us -> 63.7 us
  blocking collectives: 35.3 us -> 0 us
  Pallas kernels: 149 us -> 170 us
  other arithmetic: 24.4 us -> 38.3 us
  between operations: 15.5 us -> 2.45 us
  local copies, waits for them, and re-layouts: 38.6 us -> 32.7 us
    psum x1 -> x0, waiting for transfers between devices: 144 us -> none  [body(): lax.psum((g_qkv.astype(BF), g_out.astype(BF), short_dp.astype(BF)), 'dp')]
    ppermute x0 -> x27, waiting for transfers between devices: none -> 60.7 us  [partner(): return lax.ppermute(value, 'dp', [(i, i ^ 1 << bit) for i in range(homes)])]
    psum x1 -> x0, blocking collectives: 35.3 us -> none  [body(): lax.psum((g_qkv.astype(BF), g_out.astype(BF), short_dp.astype(BF)), 'dp')]
    ppermute x0 -> x27, starting transfers between devices: none -> 34.1 us  [partner(): return lax.ppermute(value, 'dp', [(i, i ^ 1 << bit) for i in range(homes)])]
    ppermute x31 -> x33, waiting for transfers between devices: 71.6 us -> 43 us  [swap(): return lax.ppermute(x, 'mp', [(i, i ^ bit) for i in range(count)])]
    pallas_call x12 -> x15, Pallas kernels: 149 us -> 170 us  [call(): return run(*([scalars] if lead else []), *args)]
    select_n x0 -> x11, other arithmetic: none -> 7.22 us  [join_half(): jnp.where(mark == 0, jnp.concatenate([value, other], axis=0), jnp.concate...]
    concatenate x3 -> x6, other arithmetic: 0.29 us -> 6.51 us  [the longest x1 2.9 us: body(): jnp.concatenate([g1 + g1_recv.astype(F32), head_quarter], axis=0)]
  transfers between devices with their start and end apart: 33 -> 61, of which waited for: 12 -> 19; matrix products, arithmetic and copies ran while one was open for 10% -> 15% of each run, Pallas kernels for 23% -> 38%
where the time goes in v2:
time: 426 us; the launch traced here: 419 us
  Pallas kernels  170 us (40%)
  waiting for transfers between devices  104 us (24%)
  starting transfers between devices  63.7 us (15%)
  other arithmetic  38.3 us (9%)
  local copies, waits for them, and re-layouts  32.7 us (8%)
  matrix products  8.05 us (2%)
    pallas_call x15, Pallas kernels, call(): return run(*([scalars] if lead else []), *args)  170 us
    ppermute x27, waiting for transfers between devices, partner(): return lax.ppermute(value, 'dp', [(i, i ^ 1 << bit) for i in range(homes)])  60.7 us
    ppermute x33, waiting for transfers between devices, swap(): return lax.ppermute(x, 'mp', [(i, i ^ bit) for i in range(count)])  43 us
    ppermute x27, starting transfers between devices, partner(): return lax.ppermute(value, 'dp', [(i, i ^ 1 << bit) for i in range(homes)])  34.1 us
    ppermute x33, starting transfers between devices, swap(): return lax.ppermute(x, 'mp', [(i, i ^ bit) for i in range(count)])  22.9 us
    unnamed x109, local copies, waits for them, and re-layouts  13.6 us
  transfers between devices with their start and end apart: 61, of which 19 were waited for; matrix products, arithmetic and copies ran while one was open for 15% of the time, Pallas kernels for 38%

profile of v2, /device:TPU:0, one launch (start us, length us, event | category | flops | bytes accessed | tf_op | source)
XLA Modules:
  0.0 419.0 jit_solution(5015000067724214970)
XLA Ops:
  0.7 3.0 collective-permute-start.1
  7.9 3.1 collective-permute-done.8
  13.1 2.3 copy.63
  15.5 2.5 pad.23.w_ref
  19.3 6.7 %student_qkv.1 = (bf16[1536,768]{1,0:T(8,128)(2,1)}, bf16[1536,768]{1,0:T(8,128)(2,1)}, bf16[1536,256]{1,0:T(8,128)(2,1)S(1)}, bf16[1536,256]{1,0:T(8,128)(2,1)S(1)}, bf16[1536,256]{1,0:T(8,128)(2,1)}) custom-call(s32[32]{0:T(128)S(1)} %concatenate.136.sc, bf16[12,4,32,768]{3,2,1,0:T(8,128)(2,1)} %bitcast.104, bf16[1,768]{1,0:T(2,128)(2,1)S(1)} %reshape.263.g_ref, ...), custom_call_target="tpu_custom_call" | custom-call | flops 1811939328 | bytes 10620928 | tf_op jit(solution)/shard_map/student_qkv/pallas_call | solution.py:78
  28.2 16.5 %student_attend.1 = (bf16[1536,192]{1,0:T(8,128)(2,1)S(1)}, f32[1536,256]{1,0:T(8,128)}, bf16[1536,256]{1,0:T(8,128)(2,1)S(1)}) custom-call(bf16[1536,256]{1,0:T(8,128)(2,1)} %copy-done.15, bf16[1536,256]{1,0:T(8,128)(2,1)} %copy-done.4, bf16[1536,256]{1,0:T(8,128)(2,1)} %get-tuple-element.139.v_ref), custom_call_target="tpu_custom_call" | custom-call | flops 7247757312 | bytes 5308416 | tf_op jit(solution)/shard_map/student_attend/pallas_call | solution.py:78
  48.1 7.3 %teacher_kv.1 = (bf16[2048,256]{1,0:T(8,128)(2,1)S(1)}, bf16[2048,256]{1,0:T(8,128)(2,1)}) custom-call(bf16[2048,1024]{1,0:T(8,128)(2,1)} %x_ref.1, bf16[1,1024]{1,0:T(2,128)(2,1)S(1)} %reshape.265.g_ref, bf16[1,1024]{1,0:T(2,128)(2,1)S(1)} %reshape.266.s_ref, bf16[3,1024,256]{2,1,0:T(8,128)(2,1)} %w_ref.4, bf16[2,256]{1,0:T(2,128)(2,1)S(1)} %copy-done.13), custom_call_target="tpu_custom_call" | custom-call | flops 2147483648 | bytes 7869440 | tf_op jit(solution)/shard_map/teacher_kv/pallas_call | solution.py:78
  55.8 11.8 %teacher_q.1 = (bf16[4,12,32,1024]{3,2,1,0:T(8,128)(2,1)}, bf16[4,12,32,512]{3,2,1,0:T(8,128)(2,1)S(1)}) custom-call(s32[32]{0:T(128)S(1)} %concatenate.136.sc, bf16[2048,1024]{1,0:T(8,128)(2,1)} %x_ref.1, s32[8,256]{1,0:T(8,128)S(1)} %broadcast_select_fusion.rank_ref, bf16[1,1024]{1,0:T(2,128)(2,1)S(1)} %reshape.265.g_ref, ...), custom_call_target="tpu_custom_call" | custom-call | flops 2415919104 | bytes 10499072 | tf_op jit(solution)/shard_map/teacher_q/pallas_call | solution.py:78
  68.8 24.2 %teacher_attend.1 = bf16[4,12,32,256]{3,2,1,0:T(8,128)(2,1)S(1)} custom-call(s32[32]{0:T(128)S(1)} %concatenate.136.sc, bf16[4,12,32,512]{3,2,1,0:T(8,128)(2,1)} %copy-done.14, bf16[2048,256]{1,0:T(8,128)(2,1)S(1)} %get-tuple-element.149.k_ref, bf16[2048,256]{1,0:T(8,128)(2,1)} %get-tuple-element.150.v_ref), custom_call_target="tpu_custom_call" | custom-call | flops 9663676416 | bytes 4456448 | tf_op jit(solution)/shard_map/teacher_attend/pallas_call | solution.py:78
  96.7 13.9 %student_forward.1 = (bf16[384,768]{1,0:T(8,128)(2,1)}, f32[384,768]{1,0:T(8,128)}, bf16[768,768]{1,0:T(8,128)(2,1)}, bf16[768,768]{1,0:T(8,128)(2,1)}, bf16[768,1536]{1,0:T(8,128)(2,1)}, /*index=5*/f32[768,1536]{1,0:T(8,128)}) custom-call(bf16[768,192]{1,0:T(8,128)(2,1)S(1)} %get-tuple-element.349.c0, bf16[768,192]{1,0:T(8,128)(2,1)S(1)} %collective-permute-done.9.c1, ...), custom_call_target="tpu_custom_call" | custom-call | flops 4529848320 | bytes 20653056 | tf_op jit(solution)/shard_map/student_forward/pallas_call | solution.py:78
  110.6 2.7 collective-permute-done.16.c3
  115.1 10.7 %teacher_forward_far.1 = bf16[384,1024]{1,0:T(8,128)(2,1)} custom-call(bf16[1536,256]{1,0:T(8,128)(2,1)} %bitcast.86, bf16[768,256]{1,0:T(8,128)(2,1)S(1)} %collective-permute-done.15.c1, bf16[768,256]{1,0:T(8,128)(2,1)S(1)} %collective-permute-done.14.c2, bf16[768,256]{1,0:T(8,128)(2,1)S(1)} %collective-permute-done.16.c3, bf16[256,1024]{1,0:T(8,128)(2,1)S(1)} %copy-done.3, ...), custom_call_target="tpu_custom_call" | custom-call | flops 4026531840 | bytes 16396288 | tf_op jit(solution)/shard_map/teacher_forward_far/pallas_call | solution.py:78
  125.8 2.1 collective-permute-done.17
  134.0 6.7 %all-to-all-start = ((bf16[16,32,768]{2,1,0:T(8,128)(2,1)}), bf16[16,32,768]{2,1,0:T(8,128)(2,1)}, u32[]{:S(2)}, u32[]{:S(2)}) async-start(bf16[16,32,768]{2,1,0:T(8,128)(2,1)} %copy.65), calls=%async_computation | async-start | bytes 1572864 | tf_op jit(solution)/shard_map/all_to_all | solution.py:666
  140.7 19.5 %teacher_forward_own.1.own_ref = f32[384,1024]{1,0:T(8,128)} custom-call(bf16[1536,256]{1,0:T(8,128)(2,1)} %bitcast.87, bf16[768,256]{1,0:T(8,128)(2,1)S(1)} %collective-permute-done.15.c1, bf16[768,256]{1,0:T(8,128)(2,1)S(1)} %collective-permute-done.14.c2, bf16[768,256]{1,0:T(8,128)(2,1)S(1)} %collective-permute-done.16.c3, ...), custom_call_target="tpu_custom_call" | custom-call | flops 4026531840 | bytes 17182720 | tf_op jit(solution)/shard_map/teacher_forward_own/pallas_call | solution.py:78
  160.2 4.6 %head.1 = (bf16[384,1024]{1,0:T(8,128)(2,1)S(1)}, bf16[384,768]{1,0:T(8,128)(2,1)S(1)}, f32[1,1024]{1,0:T(1,128)S(1)}, f32[1,1024]{1,0:T(1,128)S(1)}, f32[1,768]{1,0:T(1,128)S(1)}) custom-call(s32[32]{0:T(128)S(1)} %concatenate.136.sc, f32[384,1024]{1,0:T(8,128)} %teacher_forward_own.1.own_ref, bf16[384,1024]{1,0:T(8,128)(2,1)} %collective-permute-done.18.recv_ref, ...), custom_call_target="tpu_custom_call" | custom-call | flops 1207959552 | bytes 5911584 | tf_op jit(solution)/shard_map/head/pallas_call | solution.py:78
  168.0 13.8 %collective-permute-done.19.d1 = bf16[384,768]{1,0:T(8,128)(2,1)S(1)} collective-permute-done((bf16[384,768]{1,0:T(8,128)(2,1)S(1)}, bf16[384,768]{1,0:T(8,128)(2,1)S(1)}, u32[]{:S(2)}, u32[]{:S(2)}) %collective-permute-start.19) | collective-permute-done | bytes 589856 | tf_op jit(solution)/shard_map/ppermute | solution.py:489
  181.8 8.5 %feed_back_far.1 = (bf16[768,768]{1,0:T(8,128)(2,1)}, bf16[768,768]{1,0:T(8,128)(2,1)}, f32[1,768]{1,0:T(1,128)S(1)}, f32[768,768]{1,0:T(8,128)}) custom-call(bf16[384,768]{1,0:T(8,128)(2,1)S(1)} %get-tuple-element.197.d0.base_ref, bf16[384,768]{1,0:T(8,128)(2,1)S(1)} %collective-permute-done.19.d1, bf16[768,1536]{1,0:T(8,128)(2,1)} %get-tuple-element.200.act_ref, ...), custom_call_target="tpu_custom_call" | custom-call | flops 3623878656 | bytes 16518144 | tf_op jit(solution)/shard_map/feed_back_far/pallas_call | solution.py:78
  195.7 9.6 %feed_back_own.1 = (f32[768,768]{1,0:T(8,128)}, f32[768,768]{1,0:T(8,128)}, f32[1,768]{1,0:T(1,128)S(1)}, f32[384,768]{1,0:T(8,128)}, bf16[384,768]{1,0:T(8,128)(2,1)S(1)}) custom-call(bf16[384,768]{1,0:T(8,128)(2,1)S(1)} %get-tuple-element.197.d0.base_ref, bf16[384,768]{1,0:T(8,128)(2,1)S(1)} %collective-permute-done.19.d1, ...), custom_call_target="tpu_custom_call" | custom-call | flops 3623878656 | bytes 20646912 | tf_op jit(solution)/shard_map/feed_back_own/pallas_call | solution.py:78
  209.6 10.8 %collective-permute-done.24.recv_ref = bf16[384,768]{1,0:T(8,128)(2,1)S(1)} collective-permute-done((bf16[384,768]{1,0:T(8,128)(2,1)S(1)}, bf16[384,768]{1,0:T(8,128)(2,1)S(1)}, u32[]{:S(2)}, u32[]{:S(2)}) %collective-permute-start.24) | collective-permute-done | bytes 589856 | tf_op jit(solution)/shard_map/ppermute | solution.py:489
  220.4 2.5 norm2_back.1
  224.5 2.2 add_convert_fusion
  227.8 2.0 collective-permute-start.28
  229.9 7.2 %collective-permute-done.25 = bf16[384,768]{1,0:T(8,128)(2,1)S(1)} collective-permute-done((bf16[384,768]{1,0:T(8,128)(2,1)S(1)}, bf16[384,768]{1,0:T(8,128)(2,1)S(1)}, u32[]{:S(2)}, u32[]{:S(2)}) %collective-permute-start.25) | collective-permute-done | bytes 589856 | tf_op jit(solution)/shard_map/ppermute | solution.py:489
  238.8 2.2 add_convert_fusion.1
  241.1 2.9 fusion.2
  244.0 2.0 collective-permute-start.27
  252.1 2.9 pad_maximum_fusion.ds_ref
  255.0 9.5 %collective-permute-done.27 = bf16[512,768]{1,0:T(8,128)(2,1)} collective-permute-done((bf16[512,768]{1,0:T(8,128)(2,1)}, bf16[512,768]{1,0:T(8,128)(2,1)}, u32[]{:S(2)}, u32[]{:S(2)}) %collective-permute-start.27) | collective-permute-done | bytes 786464 | tf_op jit(solution)/shard_map/ppermute | solution.py:737
  265.8 2.7 collective-permute-start.30
  271.4 19.4 %student_back_pair.1 = (bf16[1536,384]{1,0:T(8,128)(2,1)}, f32[2,128]{1,0:T(2,128)S(1)}) custom-call(bf16[1536,768]{1,0:T(8,128)(2,1)} %pad_maximum_fusion.ds_ref, bf16[256,768]{1,0:T(8,128)(2,1)S(1)} %pad.25.w_ref, f32[1536,256]{1,0:T(8,128)} %get-tuple-element.221.mixed_ref, bf16[1536,256]{1,0:T(8,128)(2,1)S(1)} %copy-done.17, ...), custom_call_target="tpu_custom_call" | custom-call | flops 10871635968 | bytes 8455168 | tf_op jit(solution)/shard_map/student_back_pair/pallas_call | solution.py:78
  293.9 11.6 %student_back_odd.1 = (bf16[1536,192]{1,0:T(8,128)(2,1)S(1)}, f32[2,64]{1,0:T(2,128)S(1)}) custom-call(bf16[1536,768]{1,0:T(8,128)(2,1)} %pad_maximum_fusion.ds_ref, bf16[256,768]{1,0:T(8,128)(2,1)S(1)} %pad.25.w_ref, f32[1536,256]{1,0:T(8,128)} %get-tuple-element.221.mixed_ref, bf16[1536,256]{1,0:T(8,128)(2,1)} %copy-done.16, bf16[1536,256]{1,0:T(8,128)(2,1)} %copy-done.4, ...), custom_call_target="tpu_custom_call" | custom-call | flops 5435817984 | bytes 7864832 | tf_op jit(solution)/shard_map/student_back_odd/pallas_call | solution.py:78
  312.0 2.4 collective-permute-start.34
  316.5 6.0 %collective-permute-done.34 = bf16[128,768]{1,0:T(8,128)(2,1)S(1)} collective-permute-done((bf16[128,768]{1,0:T(8,128)(2,1)S(1)}, bf16[128,768]{1,0:T(8,128)(2,1)S(1)}, u32[]{:S(2)}, u32[]{:S(2)}) %collective-permute-start.34) | collective-permute-done | bytes 196640 | tf_op jit(solution)/shard_map/ppermute | solution.py:737
  327.6 3.0 collective-permute-start.54
  330.7 10.0 %collective-permute-done.56 = bf16[192,768]{1,0:T(8,128)(2,1)S(1)} collective-permute-done((bf16[192,768]{1,0:T(8,128)(2,1)S(1)}, bf16[192,768]{1,0:T(8,128)(2,1)S(1)}, u32[]{:S(2)}, u32[]{:S(2)}) %collective-permute-start.56) | collective-permute-done | bytes 294944 | tf_op jit(solution)/shard_map/ppermute | solution.py:737
  341.1 2.1 collective-permute-start.43
  343.1 11.6 %collective-permute-done.48 = bf16[192,768]{1,0:T(8,128)(2,1)S(1)} collective-permute-done((bf16[192,768]{1,0:T(8,128)(2,1)S(1)}, bf16[192,768]{1,0:T(8,128)(2,1)S(1)}, u32[]{:S(2)}, u32[]{:S(2)}) %collective-permute-start.48) | collective-permute-done | bytes 294944 | tf_op jit(solution)/shard_map/ppermute | solution.py:737
  355.9 13.8 %collective-permute-done.43 = bf16[96,768]{1,0:T(8,128)(2,1)S(1)} collective-permute-done((bf16[96,768]{1,0:T(8,128)(2,1)S(1)}, bf16[96,768]{1,0:T(8,128)(2,1)S(1)}, u32[]{:S(2)}, u32[]{:S(2)}) %collective-permute-start.43) | collective-permute-done | bytes 147488 | tf_op jit(solution)/shard_map/ppermute | solution.py:737
  371.2 4.0 collective-permute-done.44
  375.5 3.3 norm1_back.1
  381.7 3.3 collective-permute-start.46
  386.2 2.0 collective-permute-start.52
  393.4 2.0 collective-permute-start.41
  399.7 2.0 maximum_select_fusion
  403.8 2.9 fusion.1
  408.0 2.7 collective-permute-done.58
  416.3 2.2 fusion
  (352 shorter events, 95.9 us)
Async XLA Ops:
  0.7 17.9 %collective-permute-start.1 = (bf16[192,768]{1,0:T(8,128)(2,1)}, bf16[192,768]{1,0:T(8,128)(2,1)S(1)}, u32[]{:S(2)}, u32[]{:S(2)}) collective-permute-start(bf16[192,768]{1,0:T(8,128)(2,1)} %w0.2), channel_id=1, source_target_pairs={{0,2},{1,3},{2,0},{3,1},{4,6},{5,7},{6,4},{7,5},{8,10},{9,11},{10,... | collective-permute-start | bytes 884744 | tf_op jit(solution)/shard_map/ppermute | solution.py:489
  3.7 15.2 %collective-permute-start.7 = (bf16[192,768]{1,0:T(8,128)(2,1)}, bf16[192,768]{1,0:T(8,128)(2,1)S(1)}, u32[]{:S(2)}, u32[]{:S(2)}) collective-permute-start(bf16[192,768]{1,0:T(8,128)(2,1)} %w0.2), channel_id=1, source_target_pairs={{0,1},{1,0},{2,3},{3,2},{4,5},{5,4},{6,7},{7,6},{8,9},{9,8},{10,11... | collective-permute-start | bytes 884744 | tf_op jit(solution)/shard_map/ppermute | solution.py:489
  3.7 41.1 %collective-permute-start.2 = (bf16[1024,1024]{1,0:T(8,128)(2,1)}, bf16[1024,1024]{1,0:T(8,128)(2,1)S(1)}, u32[]{:S(2)}, u32[]{:S(2)}) collective-permute-start(bf16[1024,1024]{1,0:T(8,128)(2,1)} %f1a.2), channel_id=1, source_target_pairs={{0,1},{1,0},{2,3},{3,2},{4,5},{5,4},{6,7},{7,6},{8,9},{9,8},{10,11... | collective-permute-start | bytes 6291464 | tf_op jit(solution)/shard_map/ppermute | solution.py:489
  4.2 40.6 %collective-permute-start.3 = (bf16[1024,1024]{1,0:T(8,128)(2,1)}, bf16[1024,1024]{1,0:T(8,128)(2,1)}, u32[]{:S(2)}, u32[]{:S(2)}) collective-permute-start(bf16[1024,1024]{1,0:T(8,128)(2,1)} %f2a.2), channel_id=1, source_target_pairs={{0,1},{1,0},{2,3},{3,2},{4,5},{5,4},{6,7},{7,6},{8,9},{9,8},{10,11... | collective-permute-start | bytes 6291464 | tf_op jit(solution)/shard_map/ppermute | solution.py:489
  11.0 16.8 %collective-permute-start = (bf16[256,1024]{1,0:T(8,128)(2,1)}, bf16[256,1024]{1,0:T(8,128)(2,1)}, u32[]{:S(2)}, u32[]{:S(2)}) collective-permute-start(bf16[256,1024]{1,0:T(8,128)(2,1)} %w0.4), channel_id=1, source_target_pairs={{0,2},{1,3},{2,0},{3,1},{4,6},{5,7},{6,4},{7,5},{8,10},{9,11},{10,... | collective-permute-start | bytes 1572872 | tf_op jit(solution)/shard_map/ppermute | solution.py:489
  18.5 26.3 %collective-permute-start.4 = (bf16[768,768]{1,0:T(8,128)(2,1)}, bf16[768,768]{1,0:T(8,128)(2,1)}, u32[]{:S(2)}, u32[]{:S(2)}) collective-permute-start(bf16[768,768]{1,0:T(8,128)(2,1)} %f1), channel_id=1, source_target_pairs={{0,1},{1,0},{2,3},{3,2},{4,5},{5,4},{6,7},{7,6},{8,9},{9,8},{10,11... | collective-permute-start | bytes 3538952 | tf_op jit(solution)/shard_map/ppermute | solution.py:489
  18.9 25.9 %collective-permute-start.5 = (bf16[768,768]{1,0:T(8,128)(2,1)}, bf16[768,768]{1,0:T(8,128)(2,1)}, u32[]{:S(2)}, u32[]{:S(2)}) collective-permute-start(bf16[768,768]{1,0:T(8,128)(2,1)} %f2), channel_id=1, source_target_pairs={{0,1},{1,0},{2,3},{3,2},{4,5},{5,4},{6,7},{7,6},{8,9},{9,8},{10,11... | collective-permute-start | bytes 3538952 | tf_op jit(solution)/shard_map/ppermute | solution.py:489
  27.8 17.0 %collective-permute-start.6 = (bf16[256,1024]{1,0:T(8,128)(2,1)S(1)}, bf16[256,1024]{1,0:T(8,128)(2,1)S(1)}, u32[]{:S(2)}, u32[]{:S(2)}) collective-permute-start(bf16[256,1024]{1,0:T(8,128)(2,1)S(1)} %copy-done.3), channel_id=1, source_target_pairs={{0,1},{1,0},{2,3},{3,2},{4,5},{5,4},{6,7},{7,6},{8,9},{9,8},{10,11... | collective-permute-start | bytes 1572872 | tf_op jit(solution)/shard_map/ppermute | solution.py:489
  44.8 10.7 %collective-permute-start.10 = (bf16[256,1024]{1,0:T(8,128)(2,1)}, bf16[256,1024]{1,0:T(8,128)(2,1)S(1)}, u32[]{:S(2)}, u32[]{:S(2)}) collective-permute-start(bf16[256,1024]{1,0:T(8,128)(2,1)} %collective-permute-done.w2), channel_id=1, source_target_pairs={{0,1},{1,0},{2,3},{3,2},{4,5},{5,4},{6,7},{7,6},{8,9},{9,8},{10,11... | collective-permute-start | bytes 1572872 | tf_op jit(solution)/shard_map/ppermute | solution.py:489
  45.7 9.8 %collective-permute-start.9 = (bf16[768,192]{1,0:T(8,128)(2,1)S(1)}, bf16[768,192]{1,0:T(8,128)(2,1)S(1)}, u32[]{:S(2)}, u32[]{:S(2)}) collective-permute-start(bf16[768,192]{1,0:T(8,128)(2,1)S(1)} %get-tuple-element.348), channel_id=1, source_target_pairs={{0,1},{1,0},{2,3},{3,2},{4,5},{5,4},{6,7},{7,6},{8,9},{9,8},{10,11... | collective-permute-start | bytes 884744 | tf_op jit(solution)/shard_map/ppermute | solution.py:489
  45.9 9.6 %collective-permute-start.11 = (bf16[192,768]{1,0:T(8,128)(2,1)S(1)}, bf16[192,768]{1,0:T(8,128)(2,1)S(1)}, u32[]{:S(2)}, u32[]{:S(2)}) collective-permute-start(bf16[192,768]{1,0:T(8,128)(2,1)S(1)} %collective-permute-done.1.w2), channel_id=1, source_target_pairs={{0,1},{1,0},{2,3},{3,2},{4,5},{5,4},{6,7},{7,6},{8,9},{9,8},{10,11... | collective-permute-start | bytes 884744 | tf_op jit(solution)/shard_map/ppermute | solution.py:489
  46.3 46.7 %collective-permute-start.12 = (bf16[768,192]{1,0:T(8,128)(2,1)S(1)}, bf16[768,192]{1,0:T(8,128)(2,1)S(1)}, u32[]{:S(2)}, u32[]{:S(2)}) collective-permute-start(bf16[768,192]{1,0:T(8,128)(2,1)S(1)} %get-tuple-element.349.c0), channel_id=1, source_target_pairs={{0,2},{1,3},{2,0},{3,1},{4,6},{5,7},{6,4},{7,5},{8,10},{9,11},{10,... | collective-permute-start | bytes 884744 | tf_op jit(solution)/shard_map/ppermute | solution.py:489
  55.5 37.5 %collective-permute-start.13 = (bf16[768,192]{1,0:T(8,128)(2,1)S(1)}, bf16[768,192]{1,0:T(8,128)(2,1)S(1)}, u32[]{:S(2)}, u32[]{:S(2)}) collective-permute-start(bf16[768,192]{1,0:T(8,128)(2,1)S(1)} %collective-permute-done.9.c1), channel_id=1, source_target_pairs={{0,2},{1,3},{2,0},{3,1},{4,6},{5,7},{6,4},{7,5},{8,10},{9,11},{10,... | collective-permute-start | bytes 884744 | tf_op jit(solution)/shard_map/ppermute | solution.py:489
  93.7 16.9 %collective-permute-start.14 = (bf16[768,256]{1,0:T(8,128)(2,1)S(1)}, bf16[768,256]{1,0:T(8,128)(2,1)S(1)}, u32[]{:S(2)}, u32[]{:S(2)}) collective-permute-start(bf16[768,256]{1,0:T(8,128)(2,1)S(1)} %get-tuple-element.347), channel_id=1, source_target_pairs={{0,2},{1,3},{2,0},{3,1},{4,6},{5,7},{6,4},{7,5},{8,10},{9,11},{10,... | collective-permute-start | bytes 1179656 | tf_op jit(solution)/shard_map/ppermute | solution.py:489
  95.6 17.7 %collective-permute-start.16 = (bf16[768,256]{1,0:T(8,128)(2,1)S(1)}, bf16[768,256]{1,0:T(8,128)(2,1)S(1)}, u32[]{:S(2)}, u32[]{:S(2)}) collective-permute-start(bf16[768,256]{1,0:T(8,128)(2,1)S(1)} %collective-permute-done.15.c1), channel_id=1, source_target_pairs={{0,2},{1,3},{2,0},{3,1},{4,6},{5,7},{6,4},{7,5},{8,10},{9,11},{10,... | collective-permute-start | bytes 1179656 | tf_op jit(solution)/shard_map/ppermute | solution.py:489
  113.3 14.7 %collective-permute-start.17 = (bf16[384,768]{1,0:T(8,128)(2,1)}, bf16[384,768]{1,0:T(8,128)(2,1)S(1)}, u32[]{:S(2)}, u32[]{:S(2)}) collective-permute-start(bf16[384,768]{1,0:T(8,128)(2,1)} %get-tuple-element.163), channel_id=1, source_target_pairs={{0,2},{1,3},{2,0},{3,1},{4,6},{5,7},{6,4},{7,5},{8,10},{9,11},{10,... | collective-permute-start | bytes 1769480 | tf_op jit(solution)/shard_map/ppermute | solution.py:489
  128.0 32.3 %collective-permute-start.18 = (bf16[384,1024]{1,0:T(8,128)(2,1)}, bf16[384,1024]{1,0:T(8,128)(2,1)}, u32[]{:S(2)}, u32[]{:S(2)}) collective-permute-start(bf16[384,1024]{1,0:T(8,128)(2,1)} %teacher_forward_far.1), channel_id=1, source_target_pairs={{0,2},{1,3},{2,0},{3,1},{4,6},{5,7},{6,4},{7,5},{8,10},{9,11},{10,... | collective-permute-start | bytes 2359304 | tf_op jit(solution)/shard_map/ppermute | solution.py:489
  134.0 34.0 %all-to-all-start = ((bf16[16,32,768]{2,1,0:T(8,128)(2,1)}), bf16[16,32,768]{2,1,0:T(8,128)(2,1)}, u32[]{:S(2)}, u32[]{:S(2)}) async-start(bf16[16,32,768]{2,1,0:T(8,128)(2,1)} %copy.65), calls=%async_computation | async-start | bytes 1572864 | tf_op jit(solution)/shard_map/all_to_all | solution.py:666
  166.0 15.8 %collective-permute-start.20 = (bf16[384,1024]{1,0:T(8,128)(2,1)S(1)}, bf16[384,1024]{1,0:T(8,128)(2,1)}, u32[]{:S(2)}, u32[]{:S(2)}) collective-permute-start(bf16[384,1024]{1,0:T(8,128)(2,1)S(1)} %dynamic-slice_convert_fusion), channel_id=1, source_target_pairs={{0,1},{1,0},{2,3},{3,2},{4,5},{5,4},{6,7},{7,6},{8,9},{9,8},{10,11... | collective-permute-start | bytes 2359304 | tf_op jit(solution)/shard_map/ppermute | solution.py:489
  167.5 14.3 %collective-permute-start.19 = (bf16[384,768]{1,0:T(8,128)(2,1)S(1)}, bf16[384,768]{1,0:T(8,128)(2,1)S(1)}, u32[]{:S(2)}, u32[]{:S(2)}) collective-permute-start(bf16[384,768]{1,0:T(8,128)(2,1)S(1)} %get-tuple-element.197.d0.base_ref), channel_id=1, source_target_pairs={{0,2},{1,3},{2,0},{3,1},{4,6},{5,7},{6,4},{7,5},{8,10},{9,11},{10,... | collective-permute-start | bytes 1769480 | tf_op jit(solution)/shard_map/ppermute | solution.py:489
  190.3 15.1 %collective-permute-start.21 = (bf16[768,768]{1,0:T(8,128)(2,1)}, bf16[768,768]{1,0:T(8,128)(2,1)}, u32[]{:S(2)}, u32[]{:S(2)}) collective-permute-start(bf16[768,768]{1,0:T(8,128)(2,1)} %get-tuple-element.203), channel_id=1, source_target_pairs={{0,1},{1,0},{2,3},{3,2},{4,5},{5,4},{6,7},{7,6},{8,9},{9,8},{10,11... | collective-permute-start | bytes 3538952 | tf_op jit(solution)/shard_map/ppermute | solution.py:489
  190.3 15.1 %collective-permute-start.22 = (bf16[768,768]{1,0:T(8,128)(2,1)}, bf16[768,768]{1,0:T(8,128)(2,1)}, u32[]{:S(2)}, u32[]{:S(2)}) collective-permute-start(bf16[768,768]{1,0:T(8,128)(2,1)} %get-tuple-element.204), channel_id=1, source_target_pairs={{0,1},{1,0},{2,3},{3,2},{4,5},{5,4},{6,7},{7,6},{8,9},{9,8},{10,11... | collective-permute-start | bytes 3538952 | tf_op jit(solution)/shard_map/ppermute | solution.py:489
  193.9 11.4 %collective-permute-start.23 = (bf16[192,1024]{1,0:T(8,128)(2,1)S(1)}, bf16[192,1024]{1,0:T(8,128)(2,1)S(1)}, u32[]{:S(2)}, u32[]{:S(2)}) collective-permute-start(bf16[192,1024]{1,0:T(8,128)(2,1)S(1)} %dynamic-slice_convert_fusion.1), channel_id=1, source_target_pairs={{0,2},{1,3},{2,0},{3,1},{4,6},{5,7},{6,4},{7,5},{8,10},{9,11},{10,... | collective-permute-start | bytes 1179656 | tf_op jit(solution)/shard_map/ppermute | solution.py:489
  205.4 15.0 %collective-permute-start.24 = (bf16[384,768]{1,0:T(8,128)(2,1)S(1)}, bf16[384,768]{1,0:T(8,128)(2,1)S(1)}, u32[]{:S(2)}, u32[]{:S(2)}) collective-permute-start(bf16[384,768]{1,0:T(8,128)(2,1)S(1)} %get-tuple-element.212), channel_id=1, source_target_pairs={{0,2},{1,3},{2,0},{3,1},{4,6},{5,7},{6,4},{7,5},{8,10},{9,11},{10,... | collective-permute-start | bytes 1769480 | tf_op jit(solution)/shard_map/ppermute | solution.py:489
  222.9 14.1 %collective-permute-start.25 = (bf16[384,768]{1,0:T(8,128)(2,1)S(1)}, bf16[384,768]{1,0:T(8,128)(2,1)S(1)}, u32[]{:S(2)}, u32[]{:S(2)}) collective-permute-start(bf16[384,768]{1,0:T(8,128)(2,1)S(1)} %get-tuple-element.214.base_ref), channel_id=1, source_target_pairs={{0,2},{1,3},{2,0},{3,1},{4,6},{5,7},{6,4},{7,5},{8,10},{9,11},{10,... | collective-permute-start | bytes 1769480 | tf_op jit(solution)/shard_map/ppermute | solution.py:489
  227.8 27.2 %collective-permute-start.28 = (bf16[384,768]{1,0:T(8,128)(2,1)}, bf16[384,768]{1,0:T(8,128)(2,1)}, u32[]{:S(2)}, u32[]{:S(2)}) collective-permute-start(bf16[384,768]{1,0:T(8,128)(2,1)} %get-tuple-element.342), channel_id=1, source_target_pairs={{0,8},{4,12},{8,0},{12,4},{16,24},{20,28},{24,16},{28,20},{1,9},{5... | collective-permute-start | bytes 1769480 | tf_op jit(solution)/shard_map/ppermute | solution.py:737
  238.2 13.9 %collective-permute-start.26 = (bf16[768,768]{1,0:T(8,128)(2,1)}, bf16[768,768]{1,0:T(8,128)(2,1)}, u32[]{:S(2)}, u32[]{:S(2)}) collective-permute-start(bf16[768,768]{1,0:T(8,128)(2,1)} %pad_maximum_fusion.1), channel_id=1, source_target_pairs={{0,1},{1,0},{2,3},{3,2},{4,5},{5,4},{6,7},{7,6},{8,9},{9,8},{10,11... | collective-permute-start | bytes 3538952 | tf_op jit(solution)/shard_map/ppermute | solution.py:489
  244.0 20.5 %collective-permute-start.27 = (bf16[512,768]{1,0:T(8,128)(2,1)}, bf16[512,768]{1,0:T(8,128)(2,1)}, u32[]{:S(2)}, u32[]{:S(2)}) collective-permute-start(bf16[512,768]{1,0:T(8,128)(2,1)} %get-tuple-element.340), channel_id=1, source_target_pairs={{0,4},{4,0},{8,12},{12,8},{16,20},{20,16},{24,28},{28,24},{1,5},{5... | collective-permute-start | bytes 2359304 | tf_op jit(solution)/shard_map/ppermute | solution.py:737
  265.8 25.7 %collective-permute-start.30 = (bf16[192,768]{1,0:T(8,128)(2,1)S(1)}, bf16[192,768]{1,0:T(8,128)(2,1)S(1)}, u32[]{:S(2)}, u32[]{:S(2)}) collective-permute-start(bf16[192,768]{1,0:T(8,128)(2,1)S(1)} %get-tuple-element.352), channel_id=1, source_target_pairs={{0,16},{4,20},{8,24},{12,28},{16,0},{20,4},{24,8},{28,12},{1,17},{... | collective-permute-start | bytes 884744 | tf_op jit(solution)/shard_map/ppermute | solution.py:737
  269.9 21.6 %collective-permute-start.29 = (bf16[256,768]{1,0:T(8,128)(2,1)S(1)}, bf16[256,768]{1,0:T(8,128)(2,1)S(1)}, u32[]{:S(2)}, u32[]{:S(2)}) collective-permute-start(bf16[256,768]{1,0:T(8,128)(2,1)S(1)} %get-tuple-element.344), channel_id=1, source_target_pairs={{0,8},{4,12},{8,0},{12,4},{16,24},{20,28},{24,16},{28,20},{1,9},{5... | collective-permute-start | bytes 1179656 | tf_op jit(solution)/shard_map/ppermute | solution.py:737
  291.6 14.0 %collective-permute-start.32 = (bf16[96,768]{1,0:T(8,128)(2,1)S(1)}, bf16[96,768]{1,0:T(8,128)(2,1)S(1)}, u32[]{:S(2)}, u32[]{:S(2)}) collective-permute-start(bf16[96,768]{1,0:T(8,128)(2,1)S(1)} %get-tuple-element.356), channel_id=1, source_target_pairs={{0,4},{4,0},{8,12},{12,8},{16,20},{20,16},{24,28},{28,24},{1,5},{5... | collective-permute-start | bytes 442376 | tf_op jit(solution)/shard_map/ppermute | solution.py:737
  293.2 12.3 %collective-permute-start.31 = (bf16[128,768]{1,0:T(8,128)(2,1)S(1)}, bf16[128,768]{1,0:T(8,128)(2,1)S(1)}, u32[]{:S(2)}, u32[]{:S(2)}) collective-permute-start(bf16[128,768]{1,0:T(8,128)(2,1)S(1)} %get-tuple-element.354), channel_id=1, source_target_pairs={{0,16},{4,20},{8,24},{12,28},{16,0},{20,4},{24,8},{28,12},{1,17},{... | collective-permute-start | bytes 589832 | tf_op jit(solution)/shard_map/ppermute | solution.py:737
  308.6 13.9 %collective-permute-start.33 = (bf16[768,768]{1,0:T(8,128)(2,1)S(1)}, bf16[768,768]{1,0:T(8,128)(2,1)S(1)}, u32[]{:S(2)}, u32[]{:S(2)}) collective-permute-start(bf16[768,768]{1,0:T(8,128)(2,1)S(1)} %slice.201), channel_id=1, source_target_pairs={{0,1},{1,0},{2,3},{3,2},{4,5},{5,4},{6,7},{7,6},{8,9},{9,8},{10,11... | collective-permute-start | bytes 3538952 | tf_op jit(solution)/shard_map/ppermute | solution.py:489
  312.0 10.5 %collective-permute-start.34 = (bf16[128,768]{1,0:T(8,128)(2,1)S(1)}, bf16[128,768]{1,0:T(8,128)(2,1)S(1)}, u32[]{:S(2)}, u32[]{:S(2)}) collective-permute-start(bf16[128,768]{1,0:T(8,128)(2,1)S(1)} %add_convert_fusion.10), channel_id=1, source_target_pairs={{0,16},{4,20},{8,24},{12,28},{16,0},{20,4},{24,8},{28,12},{1,17},{... | collective-permute-start | bytes 589832 | tf_op jit(solution)/shard_map/ppermute | solution.py:737
  324.0 51.5 %collective-permute-start.36 = (bf16[384,768]{1,0:T(8,128)(2,1)S(1)}, bf16[384,768]{1,0:T(8,128)(2,1)S(1)}, u32[]{:S(2)}, u32[]{:S(2)}) collective-permute-start(bf16[384,768]{1,0:T(8,128)(2,1)S(1)} %slice.202), channel_id=1, source_target_pairs={{0,2},{1,3},{2,0},{3,1},{4,6},{5,7},{6,4},{7,5},{8,10},{9,11},{10,... | collective-permute-start | bytes 1769480 | tf_op jit(solution)/shard_map/ppermute | solution.py:489
  325.6 15.1 %collective-permute-start.56 = (bf16[192,768]{1,0:T(8,128)(2,1)S(1)}, bf16[192,768]{1,0:T(8,128)(2,1)S(1)}, u32[]{:S(2)}, u32[]{:S(2)}) collective-permute-start(bf16[192,768]{1,0:T(8,128)(2,1)S(1)} %maximum_select_fusion.11), channel_id=1, source_target_pairs={{0,16},{4,20},{8,24},{12,28},{16,0},{20,4},{24,8},{28,12},{1,17},{... | collective-permute-start | bytes 884744 | tf_op jit(solution)/shard_map/ppermute | solution.py:737
  325.7 15.2 %collective-permute-start.42 = (bf16[192,768]{1,0:T(8,128)(2,1)S(1)}, bf16[192,768]{1,0:T(8,128)(2,1)S(1)}, u32[]{:S(2)}, u32[]{:S(2)}) collective-permute-start(bf16[192,768]{1,0:T(8,128)(2,1)S(1)} %constant_dynamic-slice_fusion.5), channel_id=1, source_target_pairs={{0,4},{4,0},{8,12},{12,8},{16,20},{20,16},{24,28},{28,24},{1,5},{5... | collective-permute-start | bytes 884744 | tf_op jit(solution)/shard_map/ppermute | solution.py:737
  327.6 27.3 %collective-permute-start.54 = (bf16[256,768]{1,0:T(8,128)(2,1)S(1)}, bf16[256,768]{1,0:T(8,128)(2,1)S(1)}, u32[]{:S(2)}, u32[]{:S(2)}) collective-permute-start(bf16[256,768]{1,0:T(8,128)(2,1)S(1)} %maximum_select_fusion.8), channel_id=1, source_target_pairs={{0,8},{4,12},{8,0},{12,4},{16,24},{20,28},{24,16},{28,20},{1,9},{5... | collective-permute-start | bytes 1179656 | tf_op jit(solution)/shard_map/ppermute | solution.py:737
  330.6 24.1 %collective-permute-start.48 = (bf16[192,768]{1,0:T(8,128)(2,1)S(1)}, bf16[192,768]{1,0:T(8,128)(2,1)S(1)}, u32[]{:S(2)}, u32[]{:S(2)}) collective-permute-start(bf16[192,768]{1,0:T(8,128)(2,1)S(1)} %constant_dynamic-slice_fusion.2), channel_id=1, source_target_pairs={{0,8},{4,12},{8,0},{12,4},{16,24},{20,28},{24,16},{28,20},{1,9},{5... | collective-permute-start | bytes 884744 | tf_op jit(solution)/shard_map/ppermute | solution.py:737
  340.9 63.0 %collective-permute-start.57 = (bf16[384,768]{1,0:T(8,128)(2,1)S(1)}, bf16[384,768]{1,0:T(8,128)(2,1)}, u32[]{:S(2)}, u32[]{:S(2)}) collective-permute-start(bf16[384,768]{1,0:T(8,128)(2,1)S(1)} %maximum_select_fusion.7), channel_id=1, source_target_pairs={{0,8},{4,12},{8,0},{12,4},{16,24},{20,28},{24,16},{28,20},{1,9},{5... | collective-permute-start | bytes 1769480 | tf_op jit(solution)/shard_map/ppermute | solution.py:737
  341.1 28.6 %collective-permute-start.43 = (bf16[96,768]{1,0:T(8,128)(2,1)S(1)}, bf16[96,768]{1,0:T(8,128)(2,1)S(1)}, u32[]{:S(2)}, u32[]{:S(2)}) collective-permute-start(bf16[96,768]{1,0:T(8,128)(2,1)S(1)} %constant_dynamic-slice_fusion.4), channel_id=1, source_target_pairs={{0,8},{4,12},{8,0},{12,4},{16,24},{20,28},{24,16},{28,20},{1,9},{5... | collective-permute-start | bytes 442376 | tf_op jit(solution)/shard_map/ppermute | solution.py:737
  354.8 15.4 %collective-permute-start.49 = (bf16[96,768]{1,0:T(8,128)(2,1)S(1)}, bf16[96,768]{1,0:T(8,128)(2,1)S(1)}, u32[]{:S(2)}, u32[]{:S(2)}) collective-permute-start(bf16[96,768]{1,0:T(8,128)(2,1)S(1)} %constant_dynamic-slice_fusion.1), channel_id=1, source_target_pairs={{0,16},{4,20},{8,24},{12,28},{16,0},{20,4},{24,8},{28,12},{1,17},{... | collective-permute-start | bytes 442376 | tf_op jit(solution)/shard_map/ppermute | solution.py:737
  355.2 44.5 %collective-permute-start.55 = (bf16[512,768]{1,0:T(8,128)(2,1)S(1)}, bf16[512,768]{1,0:T(8,128)(2,1)}, u32[]{:S(2)}, u32[]{:S(2)}) collective-permute-start(bf16[512,768]{1,0:T(8,128)(2,1)S(1)} %maximum_select_fusion.3), channel_id=1, source_target_pairs={{0,4},{4,0},{8,12},{12,8},{16,20},{20,16},{24,28},{28,24},{1,5},{5... | collective-permute-start | bytes 2359304 | tf_op jit(solution)/shard_map/ppermute | solution.py:737
  381.7 9.4 %collective-permute-start.46 = (bf16[96,768]{1,0:T(8,128)(2,1)S(1)}, bf16[96,768]{1,0:T(8,128)(2,1)S(1)}, u32[]{:S(2)}, u32[]{:S(2)}) collective-permute-start(bf16[96,768]{1,0:T(8,128)(2,1)S(1)} %maximum_select_fusion.12), channel_id=1, source_target_pairs={{0,8},{4,12},{8,0},{12,4},{16,24},{20,28},{24,16},{28,20},{1,9},{5... | collective-permute-start | bytes 442376 | tf_op jit(solution)/shard_map/ppermute | solution.py:737
  386.2 9.8 %collective-permute-start.52 = (bf16[96,768]{1,0:T(8,128)(2,1)S(1)}, bf16[96,768]{1,0:T(8,128)(2,1)S(1)}, u32[]{:S(2)}, u32[]{:S(2)}) collective-permute-start(bf16[96,768]{1,0:T(8,128)(2,1)S(1)} %maximum_select_fusion.13), channel_id=1, source_target_pairs={{0,16},{4,20},{8,24},{12,28},{16,0},{20,4},{24,8},{28,12},{1,17},{... | collective-permute-start | bytes 442376 | tf_op jit(solution)/shard_map/ppermute | solution.py:737
  391.1 15.6 %collective-permute-start.47 = (bf16[192,768]{1,0:T(8,128)(2,1)S(1)}, bf16[192,768]{1,0:T(8,128)(2,1)}, u32[]{:S(2)}, u32[]{:S(2)}) collective-permute-start(bf16[192,768]{1,0:T(8,128)(2,1)S(1)} %maximum_select_fusion.9), channel_id=1, source_target_pairs={{0,4},{4,0},{8,12},{12,8},{16,20},{20,16},{24,28},{28,24},{1,5},{5... | collective-permute-start | bytes 884744 | tf_op jit(solution)/shard_map/ppermute | solution.py:737
  396.7 14.3 %collective-permute-start.53 = (bf16[192,768]{1,0:T(8,128)(2,1)}, bf16[192,768]{1,0:T(8,128)(2,1)}, u32[]{:S(2)}, u32[]{:S(2)}) collective-permute-start(bf16[192,768]{1,0:T(8,128)(2,1)} %maximum_select_fusion.10), channel_id=1, source_target_pairs={{0,8},{4,12},{8,0},{12,4},{16,24},{20,28},{24,16},{28,20},{1,9},{5... | collective-permute-start | bytes 884744 | tf_op jit(solution)/shard_map/ppermute | solution.py:737
  402.1 8.5 %collective-permute-start.58 = (bf16[192,1024]{1,0:T(8,128)(2,1)S(1)}, bf16[192,1024]{1,0:T(8,128)(2,1)S(1)}, u32[]{:S(2)}, u32[]{:S(2)}) collective-permute-start(bf16[192,1024]{1,0:T(8,128)(2,1)S(1)} %reshape.292), channel_id=1, source_target_pairs={{0,2},{1,3},{2,0},{3,1},{4,6},{5,7},{6,4},{7,5},{8,10},{9,11},{10,... | collective-permute-start | bytes 1179656 | tf_op jit(solution)/shard_map/ppermute | solution.py:489
  (66 other events, 384.8 us)
